TPU v7x, 32 devices: a whole 2x2x4 slice. The times are simulated.
32 devices in a mesh: group: 2 (over x), ctx: 16 (over z, y, core).
Axes of the slice: x: 2, y: 2, z: 4, core: 2. Of those that a mesh axis runs over, the one named last changes fastest.
Arguments:
- signal: bfloat16 [32768, 256], P(('group', 'ctx')), parts along dimension 0, may hold values from -6 to 6
- gate_one: bfloat16 [32768, 256], P(('group', 'ctx')), parts along dimension 0, may hold values from -6 to 6
- mix_two: bfloat16 [32768, 256], P(('group', 'ctx')), parts along dimension 0, may hold values from -6 to 6
- gate_two: bfloat16 [32768, 256], P(('group', 'ctx')), parts along dimension 0, may hold values from -6 to 6
- skip_one: float32 [256], replicated, may hold values from 0.5 to 1.5
- skip_two: float32 [256], replicated, may hold values from 0.5 to 1.5
- spectrum_one: bfloat16 [2, 32, 1024, 256], P(None, 'ctx'), may hold values from -6 to 6, as said below
- spectrum_two: bfloat16 [2, 32, 1024, 256], P(None, 'ctx'), may hold values from -6 to 6, as said below
Outputs:
- response: bfloat16 [32768, 256], P(('group', 'ctx')), parts along dimension 0
There are 2 independent parts, one for each index of `group`. A program takes and returns all parts, laid end to end along the dimension named above; an argument that names none is the same for every part. Nothing has to cross between parts.
Inputs may be any that keep to these rules, and one draw needn't show every extreme that they name: `spectrum_one`: the spectrum is Hermitian, as that of a real filter: H[32768 - k] is the complex conjugate of H[k]; H[0] and H[16384] are real. `spectrum_two`: the spectrum is Hermitian, as that of a real filter: H[32768 - k] is the complex conjugate of H[k]; H[0] and H[16384] are real.
All inputs are finite; a program needn't handle non-finite values.
Results may differ from a plain program's by a relative error of at most 0.0049.
Values may be sent and summed in bfloat16 or wider, within the bound.
No kernel may reach another device: no remote copies, remote signals or barrier semaphores. Data moves between devices by JAX's collectives and lax.ppermute only.
A program may use at most 128 MiB of HBM per device.

v0:
```python
import math

import jax
import jax.numpy as jnp
from jax import lax
from jax.sharding import PartitionSpec as P

highest = lax.Precision.HIGHEST


def phase_table(row_count, col_count, period, sign_value):
    products = (
        jnp.arange(row_count, dtype=jnp.int32)[:, None]
        * jnp.arange(col_count, dtype=jnp.int32)[None, :]
        % period
    )
    angles = sign_value * 2.0 * math.pi / period * products.astype(jnp.float32)
    return (jnp.cos(angles), jnp.sin(angles))


def twiddle(freq_index, time_index, period, sign_value):
    products = freq_index * time_index % period
    angles = sign_value * 2.0 * math.pi / period * products.astype(jnp.float32)
    return (jnp.cos(angles), jnp.sin(angles))


def rotate(real_part, imag_part, cosine_part, sine_part):
    return (
        real_part * cosine_part - imag_part * sine_part,
        real_part * sine_part + imag_part * cosine_part,
    )


def complex_einsum(pattern, table_pair, value_pair):
    cosine_part, sine_part = table_pair
    real_part, imag_part = value_pair
    real_out = jnp.einsum(pattern, cosine_part, real_part, precision=highest) - jnp.einsum(
        pattern, sine_part, imag_part, precision=highest
    )
    imag_out = jnp.einsum(pattern, cosine_part, imag_part, precision=highest) + jnp.einsum(
        pattern, sine_part, real_part, precision=highest
    )
    return (real_out, imag_out)


def rows_forward(values, doubled):
    cosine_part, sine_part = phase_table(doubled, values.shape[0], doubled, -1.0)
    real_out = jnp.einsum("kp,p...->k...", cosine_part, values, precision=highest)
    imag_out = jnp.einsum("kp,p...->k...", sine_part, values, precision=highest)
    return (real_out, imag_out)


def rows_inverse(value_pair, row_count, doubled, period):
    cosine_part, sine_part = phase_table(row_count, doubled, doubled, 1.0)
    real_part, imag_part = value_pair
    summed = jnp.einsum("pk,k...->p...", cosine_part, real_part, precision=highest) - jnp.einsum(
        "pk,k...->p...", sine_part, imag_part, precision=highest
    )
    return summed / period


def time_transform(value_pair, sign_value):
    real_part, imag_part = value_pair
    length = real_part.shape[1]
    low_len = 32
    high_len = length // low_len
    first_table = phase_table(high_len, high_len, high_len, sign_value)
    turn_cos, turn_sin = twiddle(
        jnp.arange(high_len, dtype=jnp.int32)[:, None],
        jnp.arange(low_len, dtype=jnp.int32)[None, :],
        length,
        sign_value,
    )
    second_table = phase_table(low_len, low_len, low_len, sign_value)
    shape_in = (real_part.shape[0], high_len, low_len, real_part.shape[2])
    sectioned = complex_einsum(
        "qn,knac->kqac", first_table, (real_part.reshape(shape_in), imag_part.reshape(shape_in))
    )
    sectioned = rotate(
        sectioned[0], sectioned[1], turn_cos[None, :, :, None], turn_sin[None, :, :, None]
    )
    result = complex_einsum("pa,kqac->kpqc", second_table, sectioned)
    return (result[0].reshape(real_part.shape), result[1].reshape(real_part.shape))


def apply_filter(value_pair, spec_real, spec_imag):
    return rotate(value_pair[0], value_pair[1], spec_real, spec_imag)


def pencil_core(source, spectrum):
    ctx_count = lax.axis_size("ctx")
    ctx_index = lax.axis_index("ctx")
    length = source.shape[0]
    channels = source.shape[1]
    doubled = 2 * ctx_count
    total_len = doubled * length
    group_len = length // ctx_count
    columns = lax.all_to_all(
        source.reshape(1, length, channels), "ctx", split_axis=1, concat_axis=0, tiled=True
    )
    real_part, imag_part = rows_forward(columns.astype(jnp.float32), doubled)
    time_index = ctx_index * group_len + jnp.arange(group_len, dtype=jnp.int32)
    turn_cos, turn_sin = twiddle(
        jnp.arange(doubled, dtype=jnp.int32)[:, None], time_index[None, :], total_len, -1.0
    )
    real_part, imag_part = rotate(real_part, imag_part, turn_cos[:, :, None], turn_sin[:, :, None])
    real_part, imag_part = (
        lax.all_to_all(real_part, "ctx", split_axis=0, concat_axis=1, tiled=True),
        lax.all_to_all(imag_part, "ctx", split_axis=0, concat_axis=1, tiled=True),
    )
    spectral = time_transform((real_part, imag_part), -1.0)
    spectral = apply_filter(
        spectral, spectrum[0].astype(jnp.float32), spectrum[1].astype(jnp.float32)
    )
    real_part, imag_part = time_transform(spectral, 1.0)
    freq_index = 2 * ctx_index + jnp.arange(2, dtype=jnp.int32)
    turn_cos, turn_sin = twiddle(
        freq_index[:, None], jnp.arange(length, dtype=jnp.int32)[None, :], total_len, 1.0
    )
    real_part, imag_part = rotate(real_part, imag_part, turn_cos[:, :, None], turn_sin[:, :, None])
    real_part, imag_part = (
        lax.all_to_all(real_part, "ctx", split_axis=1, concat_axis=0, tiled=True),
        lax.all_to_all(imag_part, "ctx", split_axis=1, concat_axis=0, tiled=True),
    )
    convolved = rows_inverse((real_part, imag_part), ctx_count, doubled, total_len)
    returned = lax.all_to_all(convolved, "ctx", split_axis=0, concat_axis=1, tiled=True)
    return returned.reshape(length, channels)


def long_conv(source, spectrum):
    return pencil_core(source, spectrum)


def on_device(signal, gate_one, mix_two, gate_two, skip_one, skip_two, spectrum_one, spectrum_two):
    first = long_conv(signal, spectrum_one)
    middle = (
        gate_one.astype(jnp.float32)
        * (first + skip_one * signal.astype(jnp.float32))
        * mix_two.astype(jnp.float32)
    ).astype(jnp.bfloat16)
    second = long_conv(middle, spectrum_two)
    return (gate_two.astype(jnp.float32) * (second + skip_two * middle.astype(jnp.float32))).astype(
        jnp.bfloat16
    )


def solution(mesh):
    return jax.shard_map(
        on_device,
        mesh=mesh,
        in_specs=(
            P(("group", "ctx"), None),
            P(("group", "ctx"), None),
            P(("group", "ctx"), None),
            P(("group", "ctx"), None),
            P(),
            P(),
            P(None, "ctx", None, None),
            P(None, "ctx", None, None),
        ),
        out_specs=P(("group", "ctx"), None),
        check_vma=False,
    )
```

profile of v0, /device:TPU:0, one launch (start us, length us, event | category | flops | bytes accessed | tf_op | source)
XLA Modules:
  0.0 686.4 jit_solution(13161832707850061949)
XLA Ops:
  7.1 7.4 %all-to-all-start = ((bf16[16,2,8192]{2,1,0:T(2,128)(2,1)}), bf16[16,2,8192]{2,1,0:T(2,128)(2,1)S(1)}, u32[]{:S(2)}, u32[]{:S(2)}) async-start(bf16[16,2,8192]{2,1,0:T(2,128)(2,1)} %reshape.277), calls=%async_computation | async-start | bytes 1048576 | tf_op jit(solution)/shard_map/all_to_all | solution.py:98
  14.8 14.2 %all-to-all-done = bf16[16,2,8192]{2,1,0:T(2,128)(2,1)S(1)} async-done(((bf16[16,2,8192]{2,1,0:T(2,128)(2,1)}), bf16[16,2,8192]{2,1,0:T(2,128)(2,1)S(1)}, u32[]{:S(2)}, u32[]{:S(2)}) %all-to-all-start) | async-done | bytes 524320 | tf_op jit(solution)/shard_map/all_to_all | solution.py:98
  44.8 36.9 %all-to-all-done.2 = f32[32,64,256]{2,1,0:T(8,128)S(1)} async-done(((f32[32,64,256]{2,1,0:T(8,128)}), f32[32,64,256]{2,1,0:T(8,128)S(1)}, u32[]{:S(2)}, u32[]{:S(2)}) %all-to-all-start.2) | async-done | bytes 2097184 | tf_op jit(solution)/shard_map/all_to_all | solution.py:109
  83.2 11.7 %all-to-all-start.1 = ((f32[32,64,256]{2,1,0:T(8,128)}), f32[32,64,256]{2,1,0:T(8,128)}, u32[]{:S(2)}, u32[]{:S(2)}) async-start(f32[32,64,256]{2,1,0:T(8,128)} %copy.149), calls=%async_computation.1 | async-start | bytes 4194304 | tf_op jit(solution)/shard_map/all_to_all | solution.py:108
  100.1 4.7 fusion.56
  109.3 26.2 %all-to-all-done.1 = f32[32,64,256]{2,1,0:T(8,128)} async-done(((f32[32,64,256]{2,1,0:T(8,128)}), f32[32,64,256]{2,1,0:T(8,128)}, u32[]{:S(2)}, u32[]{:S(2)}) %all-to-all-start.1) | async-done | bytes 2097184 | tf_op jit(solution)/shard_map/all_to_all | solution.py:108
  155.1 5.7 fusion.12
  190.8 11.2 %all-to-all-start.4 = ((f32[2,1024,256]{2,0,1:T(2,128)}), f32[2,1024,256]{2,0,1:T(2,128)S(1)}, u32[]{:S(2)}, u32[]{:S(2)}) async-start(f32[2,1024,256]{2,0,1:T(2,128)} %copy.178), calls=%async_computation.4 | async-start | bytes 4194304 | tf_op jit(solution)/shard_map/all_to_all | solution.py:123
  206.6 36.5 %all-to-all-done.4 = f32[2,1024,256]{2,0,1:T(2,128)S(1)} async-done(((f32[2,1024,256]{2,0,1:T(2,128)}), f32[2,1024,256]{2,0,1:T(2,128)S(1)}, u32[]{:S(2)}, u32[]{:S(2)}) %all-to-all-start.4) | async-done | bytes 2097184 | tf_op jit(solution)/shard_map/all_to_all | solution.py:123
  243.1 11.5 %all-to-all-start.3 = ((f32[2,1024,256]{2,0,1:T(2,128)}), f32[2,1024,256]{2,0,1:T(2,128)}, u32[]{:S(2)}, u32[]{:S(2)}) async-start(f32[2,1024,256]{2,0,1:T(2,128)} %copy.175), calls=%async_computation.3 | async-start | bytes 4194304 | tf_op jit(solution)/shard_map/all_to_all | solution.py:122
  260.5 35.3 %all-to-all-done.3 = f32[2,1024,256]{2,0,1:T(2,128)} async-done(((f32[2,1024,256]{2,0,1:T(2,128)}), f32[2,1024,256]{2,0,1:T(2,128)}, u32[]{:S(2)}, u32[]{:S(2)}) %all-to-all-start.3) | async-done | bytes 2097184 | tf_op jit(solution)/shard_map/all_to_all | solution.py:122
  308.8 36.3 %all_to_all.174 = f32[16,64,256]{2,1,0:T(8,128)S(1)} all-to-all(f32[16,64,256]{2,1,0:T(8,128)S(1)} %copy.181), channel_id=1, replica_groups=mesh['group'=2,'ctx'=16] {'ctx'}, dimensions={0} | all-to-all | bytes 2097152 | tf_op jit(solution)/shard_map/all_to_all | solution.py:126
  350.1 19.2 %all_to_all.175 = bf16[16,2,8192]{2,1,0:T(2,128)(2,1)S(1)} all-to-all(bf16[16,2,8192]{2,1,0:T(2,128)(2,1)S(1)} %reshape.279), channel_id=1, replica_groups=mesh['group'=2,'ctx'=16] {'ctx'}, dimensions={0} | all-to-all | bytes 1048576 | tf_op jit(solution)/shard_map/all_to_all | solution.py:98
  385.2 36.9 %all-to-all-done.8 = f32[32,64,256]{2,1,0:T(8,128)S(1)} async-done(((f32[32,64,256]{2,1,0:T(8,128)}), f32[32,64,256]{2,1,0:T(8,128)S(1)}, u32[]{:S(2)}, u32[]{:S(2)}) %all-to-all-start.8) | async-done | bytes 2097184 | tf_op jit(solution)/shard_map/all_to_all | solution.py:109
  423.5 11.4 %all-to-all-start.7 = ((f32[32,64,256]{2,1,0:T(8,128)}), f32[32,64,256]{2,1,0:T(8,128)}, u32[]{:S(2)}, u32[]{:S(2)}) async-start(f32[32,64,256]{2,1,0:T(8,128)} %copy.185), calls=%async_computation.7 | async-start | bytes 4194304 | tf_op jit(solution)/shard_map/all_to_all | solution.py:108
  439.5 4.7 fusion.32
  444.1 4.6 fusion.34
  448.8 27.2 %all-to-all-done.7 = f32[32,64,256]{2,1,0:T(8,128)} async-done(((f32[32,64,256]{2,1,0:T(8,128)}), f32[32,64,256]{2,1,0:T(8,128)}, u32[]{:S(2)}, u32[]{:S(2)}) %all-to-all-start.7) | async-done | bytes 2097184 | tf_op jit(solution)/shard_map/all_to_all | solution.py:108
  495.7 5.7 fusion.4
  531.2 11.2 %all-to-all-start.10 = ((f32[2,1024,256]{2,0,1:T(2,128)}), f32[2,1024,256]{2,0,1:T(2,128)S(1)}, u32[]{:S(2)}, u32[]{:S(2)}) async-start(f32[2,1024,256]{2,0,1:T(2,128)} %copy.210), calls=%async_computation.10 | async-start | bytes 4194304 | tf_op jit(solution)/shard_map/all_to_all | solution.py:123
  547.0 36.5 %all-to-all-done.10 = f32[2,1024,256]{2,0,1:T(2,128)S(1)} async-done(((f32[2,1024,256]{2,0,1:T(2,128)}), f32[2,1024,256]{2,0,1:T(2,128)S(1)}, u32[]{:S(2)}, u32[]{:S(2)}) %all-to-all-start.10) | async-done | bytes 2097184 | tf_op jit(solution)/shard_map/all_to_all | solution.py:123
  583.5 11.5 %all-to-all-start.9 = ((f32[2,1024,256]{2,0,1:T(2,128)}), f32[2,1024,256]{2,0,1:T(2,128)}, u32[]{:S(2)}, u32[]{:S(2)}) async-start(f32[2,1024,256]{2,0,1:T(2,128)} %copy.207), calls=%async_computation.9 | async-start | bytes 4194304 | tf_op jit(solution)/shard_map/all_to_all | solution.py:122
  600.9 35.3 %all-to-all-done.9 = f32[2,1024,256]{2,0,1:T(2,128)} async-done(((f32[2,1024,256]{2,0,1:T(2,128)}), f32[2,1024,256]{2,0,1:T(2,128)}, u32[]{:S(2)}, u32[]{:S(2)}) %all-to-all-start.9) | async-done | bytes 2097184 | tf_op jit(solution)/shard_map/all_to_all | solution.py:122
  649.1 35.9 %all_to_all.176 = f32[16,64,256]{2,1,0:T(8,128)S(1)} all-to-all(f32[16,64,256]{2,1,0:T(8,128)S(1)} %copy.213), channel_id=1, replica_groups=mesh['group'=2,'ctx'=16] {'ctx'}, dimensions={0} | all-to-all | bytes 2097152 | tf_op jit(solution)/shard_map/all_to_all | solution.py:126
  (132 shorter events, 207.4 us)
Async XLA Ops:
  7.1 21.9 %all-to-all-start = ((bf16[16,2,8192]{2,1,0:T(2,128)(2,1)}), bf16[16,2,8192]{2,1,0:T(2,128)(2,1)S(1)}, u32[]{:S(2)}, u32[]{:S(2)}) async-start(bf16[16,2,8192]{2,1,0:T(2,128)(2,1)} %reshape.277), calls=%async_computation | async-start | bytes 1048576 | tf_op jit(solution)/shard_map/all_to_all | solution.py:98
  36.5 45.2 %all-to-all-start.2 = ((f32[32,64,256]{2,1,0:T(8,128)}), f32[32,64,256]{2,1,0:T(8,128)S(1)}, u32[]{:S(2)}, u32[]{:S(2)}) async-start(f32[32,64,256]{2,1,0:T(8,128)} %copy.152), calls=%async_computation.2 | async-start | bytes 4194304 | tf_op jit(solution)/shard_map/all_to_all | solution.py:109
  81.8 1.4 copy-start.6
  83.2 52.4 %all-to-all-start.1 = ((f32[32,64,256]{2,1,0:T(8,128)}), f32[32,64,256]{2,1,0:T(8,128)}, u32[]{:S(2)}, u32[]{:S(2)}) async-start(f32[32,64,256]{2,1,0:T(8,128)} %copy.149), calls=%async_computation.1 | async-start | bytes 4194304 | tf_op jit(solution)/shard_map/all_to_all | solution.py:108
  97.5 2.4 copy-start.7
  135.6 2.2 copy-start.4
  137.8 3.3 copy-start.3
  151.6 3.5 copy-start
  190.8 52.3 %all-to-all-start.4 = ((f32[2,1024,256]{2,0,1:T(2,128)}), f32[2,1024,256]{2,0,1:T(2,128)S(1)}, u32[]{:S(2)}, u32[]{:S(2)}) async-start(f32[2,1024,256]{2,0,1:T(2,128)} %copy.178), calls=%async_computation.4 | async-start | bytes 4194304 | tf_op jit(solution)/shard_map/all_to_all | solution.py:123
  243.1 52.6 %all-to-all-start.3 = ((f32[2,1024,256]{2,0,1:T(2,128)}), f32[2,1024,256]{2,0,1:T(2,128)}, u32[]{:S(2)}, u32[]{:S(2)}) async-start(f32[2,1024,256]{2,0,1:T(2,128)} %copy.175), calls=%async_computation.3 | async-start | bytes 4194304 | tf_op jit(solution)/shard_map/all_to_all | solution.py:122
  308.1 36.9 %copy-start.10 = (bf16[1024,256]{1,0:T(8,128)(2,1)S(1)}, bf16[1024,256]{1,0:T(8,128)(2,1)}, u32[]{:S(2)}) copy-start(bf16[1024,256]{1,0:T(8,128)(2,1)} %param.8) | copy-start | bytes 1572868
  308.1 36.9 %copy-start.12 = (bf16[1024,256]{1,0:T(8,128)(2,1)S(1)}, bf16[1024,256]{1,0:T(8,128)(2,1)}, u32[]{:S(2)}) copy-start(bf16[1024,256]{1,0:T(8,128)(2,1)} %param.10) | copy-start | bytes 1572868
  308.1 36.9 %copy-start.13 = (bf16[1024,256]{1,0:T(8,128)(2,1)S(1)}, bf16[1024,256]{1,0:T(8,128)(2,1)}, u32[]{:S(2)}) copy-start(bf16[1024,256]{1,0:T(8,128)(2,1)} %param.9) | copy-start | bytes 1572868
  308.1 36.9 %copy-start.14 = (f32[256]{0:T(256)S(1)}, f32[256]{0:T(256)}, u32[]{:S(2)}) copy-start(f32[256]{0:T(256)} %param.12) | copy-start | bytes 3076
  376.9 45.2 %all-to-all-start.8 = ((f32[32,64,256]{2,1,0:T(8,128)}), f32[32,64,256]{2,1,0:T(8,128)S(1)}, u32[]{:S(2)}, u32[]{:S(2)}) async-start(f32[32,64,256]{2,1,0:T(8,128)} %copy.188), calls=%async_computation.8 | async-start | bytes 4194304 | tf_op jit(solution)/shard_map/all_to_all | solution.py:109
  423.5 52.4 %all-to-all-start.7 = ((f32[32,64,256]{2,1,0:T(8,128)}), f32[32,64,256]{2,1,0:T(8,128)}, u32[]{:S(2)}, u32[]{:S(2)}) async-start(f32[32,64,256]{2,1,0:T(8,128)} %copy.185), calls=%async_computation.7 | async-start | bytes 4194304 | tf_op jit(solution)/shard_map/all_to_all | solution.py:108
  436.9 2.4 copy-start.9
  476.0 2.2 copy-start.5
  478.2 3.3 copy-start.2
  492.0 3.7 copy-start.1
  531.2 52.3 %all-to-all-start.10 = ((f32[2,1024,256]{2,0,1:T(2,128)}), f32[2,1024,256]{2,0,1:T(2,128)S(1)}, u32[]{:S(2)}, u32[]{:S(2)}) async-start(f32[2,1024,256]{2,0,1:T(2,128)} %copy.210), calls=%async_computation.10 | async-start | bytes 4194304 | tf_op jit(solution)/shard_map/all_to_all | solution.py:123
  583.5 52.7 %all-to-all-start.9 = ((f32[2,1024,256]{2,0,1:T(2,128)}), f32[2,1024,256]{2,0,1:T(2,128)}, u32[]{:S(2)}, u32[]{:S(2)}) async-start(f32[2,1024,256]{2,0,1:T(2,128)} %copy.207), calls=%async_computation.9 | async-start | bytes 4194304 | tf_op jit(solution)/shard_map/all_to_all | solution.py:122
  648.5 36.5 %copy-start.11 = (bf16[1024,256]{1,0:T(8,128)(2,1)S(1)}, bf16[1024,256]{1,0:T(8,128)(2,1)}, u32[]{:S(2)}) copy-start(bf16[1024,256]{1,0:T(8,128)(2,1)} %param.11) | copy-start | bytes 1572868
  648.5 36.5 %copy-start.15 = (f32[256]{0:T(256)S(1)}, f32[256]{0:T(256)}, u32[]{:S(2)}) copy-start(f32[256]{0:T(256)} %param.13) | copy-start | bytes 3076
  (1 other events, 1.4 us)
where the time goes:
time: 695 us; the launch traced here: 686 us
  waiting for transfers between devices  285 us (41%)
  matrix products  126 us (18%)
  blocking collectives  91.4 us (13%)
  starting transfers between devices  84.2 us (12%)
  local copies, waits for them, and re-layouts  81.4 us (12%)
  other arithmetic  17.3 us (2%)
    all_to_all x2, waiting for transfers between devices, pencil_core(): lax.all_to_all(imag_part, 'ctx', split_axis=0, concat_axis=1, tiled=True)  73.9 us
    all_to_all x2, waiting for transfers between devices, pencil_core(): lax.all_to_all(imag_part, 'ctx', split_axis=1, concat_axis=0, tiled=True)  73.1 us
    all_to_all x2, blocking collectives, pencil_core(): lax.all_to_all(convolved, 'ctx', split_axis=0, concat_axis=1, tiled=True)  72.1 us
    all_to_all x2, waiting for transfers between devices, pencil_core(): lax.all_to_all(real_part, 'ctx', split_axis=1, concat_axis=0, tiled=True)  70.6 us
    all_to_all x2, waiting for transfers between devices, pencil_core(): lax.all_to_all(real_part, 'ctx', split_axis=0, concat_axis=1, tiled=True)  53.4 us
    dot_general x8, matrix products, complex_einsum(): jnp.einsum(pattern, sine_part, real_part, precision=highest)  31.4 us
    dot_general x8, matrix products, complex_einsum(): jnp.einsum(pattern, sine_part, imag_part, precision=highest)  26.9 us
    dot_general x8, matrix products, complex_einsum(): jnp.einsum(pattern, cosine_part, imag_part, precision=highest)  26.2 us
  transfers between devices with their start and end apart: 9, of which 9 were waited for; matrix products, arithmetic and copies ran while one was open for 7% of the time, Pallas kernels for 0%

commit v1 on v0

v1 whole, which is shorter than its diff:
```python
import functools

import jax
import jax.numpy as jnp
import numpy as np
from jax import lax
from jax.experimental import pallas as pl
from jax.experimental.pallas import tpu as pltpu
from jax.sharding import PartitionSpec as P

F32 = jnp.float32
BF16 = jnp.bfloat16
LANES = 128
GROUP = 4
PARAMS = pltpu.CompilerParams(vmem_limit_bytes=48 * 1024 * 1024)


def split_table(table):
    high = table.astype(jnp.bfloat16)
    low = (table - high.astype(np.float64)).astype(jnp.bfloat16)
    return high, low


def make_tables(n, step):
    rows = n * step
    first_len = 2 * rows
    total = first_len * LANES
    turn = 2.0 * np.pi
    n1 = np.arange(rows)
    n2 = np.arange(LANES)
    forward_one, inverse_one, cosines, sines = [], [], [], []
    for half in range(2):
        k1 = np.array(
            [
                2 * (half * (n // 2) + source) + a + 2 * n * low
                for source in range(n // 2)
                for a in range(2)
                for low in range(step)
            ]
        )
        k1[:step] = [2 * n * j for j in range(step // 2)] + [n + 2 * n * j for j in range(step // 2)]
        angle = turn * ((k1[:, None] * n1[None, :]) % first_len) / first_len
        real_rows, imag_rows = np.cos(angle), -np.sin(angle)
        imag_rows[0] = np.cos(np.pi * n1)
        table = np.concatenate([real_rows, imag_rows], axis=0)
        forward_one.append(table)
        weight = np.full((2 * rows, 1), 2.0 / total)
        weight[0] = weight[rows] = 1.0 / total
        inverse_one.append((table * weight).T)
        angle = turn * ((k1[:, None] * n2[None, :]) % total) / total
        angle[0] = 0.0
        cosines.append(np.cos(angle))
        sines.append(-np.sin(angle))
    angle = turn * ((n2[:, None] * n2[None, :]) % LANES) / LANES
    cosine, sine = np.cos(angle), np.sin(angle)
    forward_two = np.block([[cosine, -sine], [sine, cosine]])
    inverse_two = np.block([[cosine, sine], [-sine, cosine]])
    half_lanes = LANES // 2
    even = turn * ((n2[:, None] * np.arange(half_lanes)[None, :]) % LANES) / LANES
    odd = turn * ((n2[:, None] * (1 + 2 * np.arange(half_lanes))[None, :]) % (2 * LANES)) / (2 * LANES)
    zero = np.zeros((LANES, half_lanes))
    even_imag = -np.sin(even)
    even_imag[:, 0] = np.cos(np.pi * n2)
    forward_row = np.block(
        [[np.cos(even), zero, even_imag, zero], [zero, np.cos(odd), zero, -np.sin(odd)]]
    )
    weight = np.full((2 * LANES, 1), 2.0)
    weight[0] = weight[LANES] = 1.0
    inverse_row = (forward_row * weight[:, 0][None, :]).T

    def along_rows(table):
        high, low = split_table(table)
        return np.concatenate([high, low, high], axis=0)

    def along_columns(table):
        high, low = split_table(table)
        return np.concatenate([high, low, high], axis=1)

    def two_columns(table):
        return np.concatenate(split_table(table), axis=1)

    return {
        "forward_one": np.stack([two_columns(t) for t in forward_one]),
        "inverse_one": np.stack([along_columns(t) for t in inverse_one]),
        "cosine": np.stack(cosines).astype(np.float32),
        "sine": np.stack(sines).astype(np.float32),
        "forward_two": along_rows(forward_two),
        "inverse_two": along_rows(inverse_two),
        "forward_row": along_rows(forward_row),
        "inverse_row": along_rows(inverse_row),
    }


def prep_kernel(scalars, signal, gate, mix, spec_one, spec_two, data, special, turned, strided):
    step = signal.shape[0] // LANES
    channels = signal.shape[1]
    devices = data.shape[0]
    rows = data.shape[1] // 2
    for part in range(2):
        for t in range(step):
            piece = pl.ds(t * LANES, LANES)
            if part == 0:
                value = signal[piece, :].astype(F32)
            else:
                value = gate[piece, :].astype(F32) * mix[piece, :].astype(F32)
            turned[pl.ds(t, channels, stride=step), :] = value.T
        data[:, part * rows : (part + 1) * rows, :] = (
            turned[...].reshape(devices, rows, LANES).astype(BF16)
        )
    is_first = scalars[3] == 1
    for index, spec in enumerate((spec_one, spec_two)):
        for ri in range(2):
            strided[ri] = spec[ri, 0].astype(F32)
        for j in range(step // 2):
            real_part, imag_part = (
                strided[ri, pl.ds(j, LANES, stride=step), :] for ri in range(2)
            )
            if j == 0:
                packed = pack_row(strided, real_part, imag_part, step)
                real_part = jnp.where(is_first, packed[0], real_part)
                imag_part = jnp.where(is_first, packed[1], imag_part)
            special[index, 0, j] = real_part.astype(BF16)
            special[index, 1, j] = imag_part.astype(BF16)


def pack_row(strided, real_part, imag_part, step):
    half = LANES // 2
    odd = [strided[ri, pl.ds(step // 2, LANES, stride=step), :] for ri in range(2)]
    packed_real = jnp.concatenate([real_part[:half], odd[0][:half]], axis=0)
    packed_imag = jnp.concatenate([imag_part[:half], odd[1][:half]], axis=0)
    top = lax.broadcasted_iota(jnp.int32, packed_imag.shape, 0) == 0
    middle = jnp.broadcast_to(real_part[half : half + 1], packed_imag.shape)
    return packed_real, jnp.where(top, middle, packed_imag)


def pack_kernel(scalars, spec_one, spec_two, special, *refs):
    *outs, strided, turned = refs
    peers = len(outs)
    step = spec_one.shape[2] // LANES
    channels = spec_one.shape[3]
    low_index = scalars[2]
    is_first = scalars[3] == 1
    is_middle = scalars[4] == 1
    row_count = 2 * step
    for index, spec in enumerate((spec_one, spec_two)):
        for a in range(2):
            for ri in range(2):
                strided[ri] = spec[ri, a].astype(F32)
            for low in range(step):
                pair = [strided[ri, pl.ds(low, LANES, stride=step), :] for ri in range(2)]
                if a == 0 and low == 0:
                    packed = pack_row(strided, pair[0], pair[1], step)
                    pair = [jnp.where(is_first, p, v) for p, v in zip(packed, pair)]
                for ri in range(2):
                    value = pair[ri]
                    if a == 0 and low < step // 2:
                        other = special[index, ri, low].astype(F32)
                        value = jnp.where(is_middle, other, value)
                    elif a == 0:
                        j = low - step // 2
                        own = strided[ri, pl.ds(j, LANES, stride=step), :]
                        other = special[index, ri, j].astype(F32)
                        value = jnp.where(is_first, other, jnp.where(is_middle, own, value))
                    row = ri * row_count + a * step + low
                    turned[pl.ds(row, channels, stride=2 * row_count), :] = value.T
        block = channels // peers * 2 * row_count
        for s, out in enumerate(outs):
            start = pl.multiple_of((low_index ^ s) * block, block)
            out[index] = turned[pl.ds(start, block), :].astype(BF16)


def split_value(value):
    high = value.astype(BF16)
    return high, (value - high.astype(F32)).astype(BF16)


def split_columns(value):
    high, low = split_value(value)
    return jnp.concatenate([high, high, low], axis=1)


def split_rows(value):
    high, low = split_value(value)
    return jnp.concatenate([high, high, low], axis=0)


def dot(left, right):
    return jnp.dot(left, right, preferred_element_type=F32)


def conv_kernel(peers, scalars, skip_one, skip_two, data, *refs):
    blocks = refs[:peers]
    (
        forward_one,
        inverse_one,
        cosine_ref,
        sine_ref,
        forward_two,
        inverse_two,
        forward_row,
        inverse_row,
        out,
        filters,
    ) = refs[peers:]
    devices = data.shape[0]
    per_device = data.shape[1] // 2
    rows = cosine_ref.shape[1]
    step = rows // devices
    count = per_device // step
    row_count = 2 * step
    low_index = scalars[2]
    for s in range(peers):
        filters[low_index ^ s] = blocks[s][...].reshape(2, count, 2 * row_count, LANES)
    cosine, sine = cosine_ref[0], sine_ref[0]
    top_row = lax.broadcasted_iota(jnp.int32, (step, 2 * LANES), 0) == 0
    corner = top_row[:, :LANES] & (lax.broadcasted_iota(jnp.int32, (step, LANES), 1) == 0)

    def with_top(values, tops):
        return [
            jnp.concatenate(
                [jnp.where(top_row, tops[c * step : (c + 1) * step], v[:step]), v[step:]], axis=0
            )
            for c, v in enumerate(values)
        ]

    def second_stage(values, table, row_table):
        main = dot(split_columns(jnp.concatenate(values, axis=0)), table[...])
        tops = dot(split_columns(jnp.concatenate([v[:step] for v in values], axis=0)), row_table[...])
        return with_top([main[c * rows : (c + 1) * rows] for c in range(GROUP)], tops)

    def convolve(fields, index, first):
        joined = jnp.concatenate(fields, axis=1)
        staged = dot(forward_one[0], jnp.concatenate([joined, joined], axis=0))
        turned = []
        for c in range(GROUP):
            lanes = slice(c * LANES, (c + 1) * LANES)
            real_part, imag_part = staged[:rows, lanes], staged[rows:, lanes]
            turned.append(
                jnp.concatenate(
                    [
                        real_part * cosine - imag_part * sine,
                        real_part * sine + imag_part * cosine,
                    ],
                    axis=1,
                )
            )
        spectral = second_stage(turned, forward_two, forward_row)
        products = []
        for c in range(GROUP):
            stored = filters[:, index, first + c]
            h_real = stored[:, :row_count].reshape(rows, LANES).astype(F32)
            h_imag = stored[:, row_count:].reshape(rows, LANES).astype(F32)
            x_real, x_imag = spectral[c][:, :LANES], spectral[c][:, LANES:]
            real_real, imag_imag = x_real * h_real, x_imag * h_imag
            y_real = real_real - imag_imag
            y_imag = x_real * h_imag + x_imag * h_real
            y_real = jnp.concatenate(
                [jnp.where(corner, real_real[:step], y_real[:step]), y_real[step:]], axis=0
            )
            y_imag = jnp.concatenate(
                [jnp.where(corner, imag_imag[:step], y_imag[:step]), y_imag[step:]], axis=0
            )
            products.append(jnp.concatenate([y_real, y_imag], axis=1))
        inverted = second_stage(products, inverse_two, inverse_row)
        columns = []
        for c in range(GROUP):
            real_part, imag_part = inverted[c][:, :LANES], inverted[c][:, LANES:]
            columns.append(
                jnp.concatenate(
                    [
                        real_part * cosine + imag_part * sine,
                        imag_part * cosine - real_part * sine,
                    ],
                    axis=0,
                )
            )
        result = dot(inverse_one[0], split_rows(jnp.concatenate(columns, axis=1)))
        return [result[:, c * LANES : (c + 1) * LANES] for c in range(GROUP)]

    def body(trip, carry):
        first = trip * GROUP
        size = GROUP * step
        base = pl.multiple_of(first * step, size)
        signal_rows = data[:, pl.ds(base, size), :].astype(F32)
        gate_rows = data[:, pl.ds(pl.multiple_of(per_device + base, size), size), :].astype(F32)

        def channel(values, c):
            return values[:, c * step : (c + 1) * step, :].reshape(rows, LANES)

        fields = [channel(signal_rows, c) for c in range(GROUP)]
        results = convolve([f.astype(BF16) for f in fields], 0, first)
        skip_base = scalars[0] * count + first
        middles = [
            (channel(gate_rows, c) * (results[c] + skip_one[skip_base + c] * fields[c])).astype(BF16)
            for c in range(GROUP)
        ]
        results = convolve(middles, 1, first)
        finals = [
            (results[c] + skip_two[skip_base + c] * middles[c].astype(F32)).reshape(
                devices, step, LANES
            )
            for c in range(GROUP)
        ]
        out[:, pl.ds(base, size), :] = jnp.concatenate(finals, axis=1).astype(BF16)
        return carry

    lax.fori_loop(0, count // GROUP, body, 0)


def final_kernel(back, gate, out, turned):
    step = gate.shape[0] // LANES
    channels = gate.shape[1]
    turned[...] = back[...].astype(F32).reshape(channels * step, LANES)
    for t in range(step):
        piece = pl.ds(t * LANES, LANES)
        value = turned[pl.ds(t, channels, stride=step), :].T
        out[piece, :] = (gate[piece, :].astype(F32) * value).astype(BF16)


def whole(shape):
    zeros = (0,) * len(shape)
    return pl.BlockSpec(shape, lambda i, scalars: zeros)


def by_half(shape):
    zeros = (0,) * (len(shape) - 1)
    return pl.BlockSpec((1,) + tuple(shape[1:]), lambda i, scalars: (scalars[1],) + zeros)


def on_device(signal, gate_one, mix_two, gate_two, skip_one, skip_two, spectrum_one, spectrum_two):
    n = lax.axis_size("ctx")
    me = lax.axis_index("ctx")
    peers = n // 2
    length, channels = signal.shape
    step = length // LANES
    count = channels // n
    per_device = count * step
    half_channels = channels // 2
    scalars = jnp.stack(
        [me, me // peers, me % peers, (me == 0).astype(jnp.int32), (me == peers).astype(jnp.int32)]
    ).astype(jnp.int32)

    other_half = pl.BlockSpec((2, 1, length, half_channels), lambda i, s: (0, 0, 0, 1 - s[1]))
    data, special = pl.pallas_call(
        prep_kernel,
        grid_spec=pltpu.PrefetchScalarGridSpec(
            num_scalar_prefetch=1,
            grid=(1,),
            in_specs=[whole(signal.shape)] * 3 + [other_half] * 2,
            out_specs=[
                whole((n, 2 * per_device, LANES)),
                whole((2, 2, step // 2, LANES, half_channels)),
            ],
            scratch_shapes=[
                pltpu.VMEM((channels * step, LANES), F32),
                pltpu.VMEM((2, length, half_channels), F32),
            ],
        ),
        out_shape=[
            jax.ShapeDtypeStruct((n, 2 * per_device, LANES), BF16),
            jax.ShapeDtypeStruct((2, 2, step // 2, LANES, half_channels), BF16),
        ],
        compiler_params=PARAMS,
        name="prep",
    )(scalars, signal, gate_one, mix_two, spectrum_one, spectrum_two)
    special = lax.ppermute(special, "ctx", [(0, peers), (peers, 0)])
    data = lax.all_to_all(data, "ctx", split_axis=0, concat_axis=0, tiled=True)

    block_shape = (2, count * 4 * step, LANES)
    own_half = pl.BlockSpec((2, 2, length, half_channels), lambda i, s: (0, 0, 0, s[1]))
    blocks = pl.pallas_call(
        pack_kernel,
        grid_spec=pltpu.PrefetchScalarGridSpec(
            num_scalar_prefetch=1,
            grid=(1,),
            in_specs=[own_half] * 2 + [whole(special.shape)],
            out_specs=[whole(block_shape)] * peers,
            scratch_shapes=[
                pltpu.VMEM((2, length, half_channels), F32),
                pltpu.VMEM((half_channels * 4 * step, LANES), F32),
            ],
        ),
        out_shape=[jax.ShapeDtypeStruct(block_shape, BF16)] * peers,
        compiler_params=PARAMS,
        name="pack",
    )(scalars, spectrum_one, spectrum_two, special)
    blocks = [
        block if s == 0 else lax.ppermute(block, "ctx", [(i, i ^ s) for i in range(n)])
        for s, block in enumerate(blocks)
    ]

    tables = {name: jnp.asarray(table) for name, table in make_tables(n, step).items()}
    out = pl.pallas_call(
        functools.partial(conv_kernel, peers),
        grid_spec=pltpu.PrefetchScalarGridSpec(
            num_scalar_prefetch=1,
            grid=(1,),
            in_specs=[pl.BlockSpec(memory_space=pltpu.SMEM)] * 2
            + [whole(data.shape)]
            + [whole(block_shape)] * peers
            + [by_half(tables[name].shape) for name in ("forward_one", "inverse_one", "cosine", "sine")]
            + [whole((3 * 2 * LANES, 2 * LANES))] * 4,
            out_specs=whole((n, per_device, LANES)),
            scratch_shapes=[pltpu.VMEM((peers, 2, count, 4 * step, LANES), BF16)],
        ),
        out_shape=jax.ShapeDtypeStruct((n, per_device, LANES), BF16),
        compiler_params=PARAMS,
        name="convolve",
    )(scalars, skip_one, skip_two, data, *blocks, *tables.values())

    back = lax.all_to_all(out, "ctx", split_axis=0, concat_axis=0, tiled=True)
    return pl.pallas_call(
        final_kernel,
        out_shape=jax.ShapeDtypeStruct((length, channels), BF16),
        scratch_shapes=[pltpu.VMEM((channels * step, LANES), F32)],
        compiler_params=PARAMS,
        name="final",
    )(back, gate_two)


def solution(mesh):
    return jax.shard_map(
        on_device,
        mesh=mesh,
        in_specs=(
            P(("group", "ctx"), None),
            P(("group", "ctx"), None),
            P(("group", "ctx"), None),
            P(("group", "ctx"), None),
            P(),
            P(),
            P(None, "ctx", None, None),
            P(None, "ctx", None, None),
        ),
        out_specs=P(("group", "ctx"), None),
        check_vma=False,
    )
```

time: 695 us -> 121 us (0.17); the launches traced: 686 us -> 120 us
  waiting for transfers between devices: 285 us -> 49.5 us
  matrix products: 126 us -> 0 us
  blocking collectives: 91.4 us -> 17.9 us
  starting transfers between devices: 84.2 us -> 16 us
  local copies, waits for them, and re-layouts: 81.4 us -> 15 us
  Pallas kernels: 0 us -> 21.6 us
  other arithmetic: 17.3 us -> 0 us
    all_to_all x9 -> x1, waiting for transfers between devices: 285 us -> 0.01 us  [on_device(): data = lax.all_to_all(data, 'ctx', split_axis=0, concat_axis=0, tiled=True)]
    dot_general x40 -> x0, matrix products: 126 us -> none  [the longest x8 31.4 us: complex_einsum(): jnp.einsum(pattern, sine_part, real_part, precision=highest)]
    all_to_all x9 -> x1, starting transfers between devices: 84.2 us -> 7.52 us  [on_device(): data = lax.all_to_all(data, 'ctx', split_axis=0, concat_axis=0, tiled=True)]
    all_to_all x3 -> x1, blocking collectives: 91.4 us -> 17.9 us  [on_device(): back = lax.all_to_all(out, 'ctx', split_axis=0, concat_axis=0, tiled=True)]
    ppermute x0 -> x8, waiting for transfers between devices: none -> 49.5 us  [the longest x1 27.3 us: on_device(): special = lax.ppermute(special, 'ctx', [(0, peers), (peers, 0)])]
    all_to_all x16 -> x0, local copies, waits for them, and re-layouts: 32.7 us -> none  [the longest x6 16.8 us: pencil_core(): lax.all_to_all(real_part, 'ctx', split_axis=1, concat_axis=0, tiled=True)]
    pallas_call x0 -> x4, Pallas kernels: none -> 21.6 us  [the longest x1 12 us: on_device(): pl.pallas_call(functools.partial(conv_kernel, peers), grid_spec=pltpu.Pre...]
    sub x6 -> x0, local copies, waits for them, and re-layouts: 19.9 us -> none  [the longest x4 17.5 us: rotate(): real_part * cosine_part - imag_part * sine_part]
  transfers between devices with their start and end apart: 9 -> 9, of which waited for: 9 -> 6; matrix products, arithmetic and copies ran while one was open for 7% -> 0% of each run, Pallas kernels for 0% -> 5%
where the time goes in v1:
time: 121 us; the launch traced here: 120 us
  waiting for transfers between devices  49.5 us (41%)
  Pallas kernels  21.6 us (18%)
  blocking collectives  17.9 us (15%)
  starting transfers between devices  16 us (13%)
  local copies, waits for them, and re-layouts  15 us (12%)
    ppermute x1, waiting for transfers between devices, on_device(): special = lax.ppermute(special, 'ctx', [(0, peers), (peers, 0)])  27.3 us
    ppermute x7, waiting for transfers between devices, on_device(): lax.ppermute(block, 'ctx', [(i, i ^ s) for i in range(n)])  22.2 us
    all_to_all x1, blocking collectives, on_device(): back = lax.all_to_all(out, 'ctx', split_axis=0, concat_axis=0, tiled=True)  17.9 us
    unnamed x40, local copies, waits for them, and re-layouts  14.9 us
    pallas_call x1, Pallas kernels, on_device(): pl.pallas_call(functools.partial(conv_kernel, peers), grid_spec=pltpu.Pre...  12 us
    all_to_all x1, starting transfers between devices, on_device(): data = lax.all_to_all(data, 'ctx', split_axis=0, concat_axis=0, tiled=True)  7.52 us
    pallas_call x1, Pallas kernels, on_device(): pl.pallas_call(pack_kernel, grid_spec=pltpu.PrefetchScalarGridSpec(num_sc...  5.79 us
    ppermute x1, starting transfers between devices, on_device(): special = lax.ppermute(special, 'ctx', [(0, peers), (peers, 0)])  4.86 us
  transfers between devices with their start and end apart: 9, of which 6 were waited for; matrix products, arithmetic and copies ran while one was open for 0% of the time, Pallas kernels for 5%

profile of v1, /device:TPU:0, one launch (start us, length us, event | category | flops | bytes accessed | tf_op | source)
XLA Modules:
  0.0 120.1 jit_solution(11093052325094466136)
XLA Ops:
  0.1 1.6 %copy-done = bf16[2,2,1024,256]{3,2,1,0:T(8,128)(2,1)S(1)} copy-done((bf16[2,2,1024,256]{3,2,1,0:T(8,128)(2,1)S(1)}, bf16[2,2,1024,256]{3,2,1,0:T(8,128)(2,1)}, u32[]{:S(2)}) %copy-start) | copy-done | bytes 2097176
  1.7 1.0 copy-done.3
  2.7 1.0 copy-done.4
  3.8 1.0 copy-done.5
  4.8 2.6 %prep.1 = (bf16[16,256,128]{2,1,0:T(8,128)(2,1)S(1)}, bf16[2,2,4,128,128]{4,3,2,1,0:T(8,128)(2,1)S(1)}) custom-call(s32[5]{0:T(128)S(1)} %stack.31.scalars, bf16[1024,256]{1,0:T(8,128)(2,1)S(1)} %copy-done.3, bf16[1024,256]{1,0:T(8,128)(2,1)S(1)} %copy-done.4, bf16[1024,256]{1,0:T(8,128)(2,1)S(1)} %copy-done.5, bf16[2,2,1024,256]{3,2,1,0:T(8,128)(2,1)S(1)} %copy-done, ...), custom_call_target="tpu_custom_call" | custom-call | tf_op jit(solution)/shard_map/prep/pallas_call | solution.py:344
  7.5 1.0 copy-done.2
  9.2 7.5 %all-to-all-start = ((bf16[16,256,128]{2,1,0:T(8,128)(2,1)}), bf16[16,256,128]{2,1,0:T(8,128)(2,1)S(1)}, u32[]{:S(2)}, u32[]{:S(2)}) async-start(bf16[16,256,128]{2,1,0:T(8,128)(2,1)} %copy-done.2), calls=%async_computation | async-start | bytes 2097152 | tf_op jit(solution)/shard_map/all_to_all | solution.py:367
  16.8 4.9 %collective-permute-start = (bf16[2,2,4,128,128]{4,3,2,1,0:T(8,128)(2,1)}, bf16[2,2,4,128,128]{4,3,2,1,0:T(8,128)(2,1)S(1)}, u32[]{:S(2)}, u32[]{:S(2)}) collective-permute-start(bf16[2,2,4,128,128]{4,3,2,1,0:T(8,128)(2,1)} %copy-done.19), channel_id=1, source_target_pairs={{0,8},{8,0},{16,24},{24,16}} | collective-permute-start | bytes 1572872 | tf_op jit(solution)/shard_map/ppermute | solution.py:366
  21.7 27.3 %collective-permute-done.special = bf16[2,2,4,128,128]{4,3,2,1,0:T(8,128)(2,1)S(1)} collective-permute-done((bf16[2,2,4,128,128]{4,3,2,1,0:T(8,128)(2,1)}, bf16[2,2,4,128,128]{4,3,2,1,0:T(8,128)(2,1)S(1)}, u32[]{:S(2)}, u32[]{:S(2)}) %collective-permute-start) | collective-permute-done | bytes 524320 | tf_op jit(solution)/shard_map/ppermute | solution.py:366
  48.9 5.8 %pack.1 = (bf16[2,512,128]{2,1,0:T(8,128)(2,1)S(1)}, bf16[2,512,128]{2,1,0:T(8,128)(2,1)S(1)}, bf16[2,512,128]{2,1,0:T(8,128)(2,1)S(1)}, bf16[2,512,128]{2,1,0:T...) custom-call(s32[5]{0:T(128)S(1)} %stack.31.scalars, ...), custom_call_target="tpu_custom_call" | custom-call | tf_op jit(solution)/shard_map/pack/pallas_call | solution.py:371
  55.4 1.9 %collective-permute-start.3 = (bf16[2,512,128]{2,1,0:T(8,128)(2,1)S(1)}, bf16[2,512,128]{2,1,0:T(8,128)(2,1)S(1)}, u32[]{:S(2)}, u32[]{:S(2)}) collective-permute-start(bf16[2,512,128]{2,1,0:T(8,128)(2,1)S(1)} %get-tuple-element.20), channel_id=1, source_target_pairs={{0,3},{1,2},{2,1},{3,0},{4,7},{5,6},{6,5},{7,4},{8,11},{9,10},{10,... | collective-permute-start | bytes 786440 | tf_op jit(solution)/shard_map/ppermute | solution.py:388
  57.3 1.6 %collective-permute-start.5 = (bf16[2,512,128]{2,1,0:T(8,128)(2,1)S(1)}, bf16[2,512,128]{2,1,0:T(8,128)(2,1)S(1)}, u32[]{:S(2)}, u32[]{:S(2)}) collective-permute-start(bf16[2,512,128]{2,1,0:T(8,128)(2,1)S(1)} %get-tuple-element.22), channel_id=1, source_target_pairs={{0,5},{1,4},{2,7},{3,6},{4,1},{5,0},{6,3},{7,2},{8,13},{9,12},{10,... | collective-permute-start | bytes 786440 | tf_op jit(solution)/shard_map/ppermute | solution.py:388
  59.1 5.5 %collective-permute-done.2.refs_2_ = bf16[2,512,128]{2,1,0:T(8,128)(2,1)S(1)} collective-permute-done((bf16[2,512,128]{2,1,0:T(8,128)(2,1)S(1)}, bf16[2,512,128]{2,1,0:T(8,128)(2,1)S(1)}, u32[]{:S(2)}, u32[]{:S(2)}) %collective-permute-start.2) | collective-permute-done | bytes 262176 | tf_op jit(solution)/shard_map/ppermute | solution.py:388
  64.5 4.8 %collective-permute-done.3.refs_3_ = bf16[2,512,128]{2,1,0:T(8,128)(2,1)S(1)} collective-permute-done((bf16[2,512,128]{2,1,0:T(8,128)(2,1)S(1)}, bf16[2,512,128]{2,1,0:T(8,128)(2,1)S(1)}, u32[]{:S(2)}, u32[]{:S(2)}) %collective-permute-start.3) | collective-permute-done | bytes 262176 | tf_op jit(solution)/shard_map/ppermute | solution.py:388
  69.4 1.4 %collective-permute-done.5.refs_5_ = bf16[2,512,128]{2,1,0:T(8,128)(2,1)S(1)} collective-permute-done((bf16[2,512,128]{2,1,0:T(8,128)(2,1)S(1)}, bf16[2,512,128]{2,1,0:T(8,128)(2,1)S(1)}, u32[]{:S(2)}, u32[]{:S(2)}) %collective-permute-start.5) | collective-permute-done | bytes 262176 | tf_op jit(solution)/shard_map/ppermute | solution.py:388
  70.8 6.7 %collective-permute-done.6.refs_6_ = bf16[2,512,128]{2,1,0:T(8,128)(2,1)S(1)} collective-permute-done((bf16[2,512,128]{2,1,0:T(8,128)(2,1)S(1)}, bf16[2,512,128]{2,1,0:T(8,128)(2,1)S(1)}, u32[]{:S(2)}, u32[]{:S(2)}) %collective-permute-start.6) | collective-permute-done | bytes 262176 | tf_op jit(solution)/shard_map/ppermute | solution.py:388
  77.4 3.9 %collective-permute-done.7.refs_7_ = bf16[2,512,128]{2,1,0:T(8,128)(2,1)S(1)} collective-permute-done((bf16[2,512,128]{2,1,0:T(8,128)(2,1)S(1)}, bf16[2,512,128]{2,1,0:T(8,128)(2,1)S(1)}, u32[]{:S(2)}, u32[]{:S(2)}) %collective-permute-start.7) | collective-permute-done | bytes 262176 | tf_op jit(solution)/shard_map/ppermute | solution.py:388
  81.3 1.0 copy-done.8
  82.3 1.0 copy-done.9
  83.3 1.0 copy-done.10
  84.3 1.0 copy-done.11
  89.0 12.0 %convolve.1 = bf16[16,128,128]{2,1,0:T(8,128)(2,1)S(1)} custom-call(s32[5]{0:T(128)S(1)} %stack.31.scalars, f32[256]{0:T(256)S(1)} %copy-done.17, f32[256]{0:T(256)S(1)} %copy-done.18, bf16[16,256,128]{2,1,0:T(8,128)(2,1)S(1)} %all-to-all-done.data, bf16[2,512,128]{2,1,0:T(8,128)(2,1)S(1)} %copy-done.14, ...), custom_call_target="tpu_custom_call" | custom-call | tf_op jit(solution)/shard_map/convolve/pallas_call | solution.py:393
  101.0 17.9 %all_to_all.10.back = bf16[16,128,128]{2,1,0:T(8,128)(2,1)S(1)} all-to-all(bf16[16,128,128]{2,1,0:T(8,128)(2,1)S(1)} %convolve.1), channel_id=1, replica_groups=mesh['group'=2,'ctx'=16] {'ctx'}, dimensions={0} | all-to-all | bytes 1048576 | tf_op jit(solution)/shard_map/all_to_all | solution.py:411
  118.9 1.2 %final.1 = bf16[1024,256]{1,0:T(8,128)(2,1)} custom-call(bf16[16,128,128]{2,1,0:T(8,128)(2,1)S(1)} %all_to_all.10.back, bf16[1024,256]{1,0:T(8,128)(2,1)S(1)} %copy-done.6), custom_call_target="tpu_custom_call" | custom-call | tf_op jit(solution)/shard_map/final/pallas_call | solution.py:412
  (40 shorter events, 5.5 us)
Async XLA Ops:
  0.1 1.6 %copy-start = (bf16[2,2,1024,256]{3,2,1,0:T(8,128)(2,1)S(1)}, bf16[2,2,1024,256]{3,2,1,0:T(8,128)(2,1)}, u32[]{:S(2)}) copy-start(bf16[2,2,1024,256]{3,2,1,0:T(8,128)(2,1)} %spec_one.3) | copy-start | bytes 6291460
  1.7 1.0 copy-start.3
  2.7 1.0 copy-start.4
  3.8 1.0 copy-start.5
  7.4 1.0 copy-start.2
  9.2 39.7 %copy-start.1 = (bf16[2,2,1024,256]{3,2,1,0:T(8,128)(2,1)S(1)}, bf16[2,2,1024,256]{3,2,1,0:T(8,128)(2,1)}, u32[]{:S(2)}) copy-start(bf16[2,2,1024,256]{3,2,1,0:T(8,128)(2,1)} %spec_one.3) | copy-start | bytes 6291460
  9.2 72.1 %all-to-all-start = ((bf16[16,256,128]{2,1,0:T(8,128)(2,1)}), bf16[16,256,128]{2,1,0:T(8,128)(2,1)S(1)}, u32[]{:S(2)}, u32[]{:S(2)}) async-start(bf16[16,256,128]{2,1,0:T(8,128)(2,1)} %copy-done.2), calls=%async_computation | async-start | bytes 2097152 | tf_op jit(solution)/shard_map/all_to_all | solution.py:367
  16.8 64.6 %copy-start.7 = (bf16[768,256]{1,0:T(8,128)(2,1)S(1)}, bf16[768,256]{1,0:T(8,128)(2,1)}, u32[]{:S(2)}) copy-start(bf16[768,256]{1,0:T(8,128)(2,1)} %constant.54.clone.refs_15_) | copy-start | bytes 1179652
  16.8 64.6 %copy-start.17 = (f32[256]{0:T(256)S(1)}, f32[256]{0:T(256)}, u32[]{:S(2)}) copy-start(f32[256]{0:T(256)} %skip_one.1) | copy-start | bytes 3076
  16.8 64.5 %copy-start.18 = (f32[256]{0:T(256)S(1)}, f32[256]{0:T(256)}, u32[]{:S(2)}) copy-start(f32[256]{0:T(256)} %skip_two.1) | copy-start | bytes 3076
  16.8 32.1 %collective-permute-start = (bf16[2,2,4,128,128]{4,3,2,1,0:T(8,128)(2,1)}, bf16[2,2,4,128,128]{4,3,2,1,0:T(8,128)(2,1)S(1)}, u32[]{:S(2)}, u32[]{:S(2)}) collective-permute-start(bf16[2,2,4,128,128]{4,3,2,1,0:T(8,128)(2,1)} %copy-done.19), channel_id=1, source_target_pairs={{0,8},{8,0},{16,24},{24,16}} | collective-permute-start | bytes 1572872 | tf_op jit(solution)/shard_map/ppermute | solution.py:366
  55.4 3.5 %collective-permute-start.1 = (bf16[2,512,128]{2,1,0:T(8,128)(2,1)S(1)}, bf16[2,512,128]{2,1,0:T(8,128)(2,1)S(1)}, u32[]{:S(2)}, u32[]{:S(2)}) collective-permute-start(bf16[2,512,128]{2,1,0:T(8,128)(2,1)S(1)} %get-tuple-element.18), channel_id=1, source_target_pairs={{0,1},{1,0},{2,3},{3,2},{4,5},{5,4},{6,7},{7,6},{8,9},{9,8},{10,11... | collective-permute-start | bytes 786440 | tf_op jit(solution)/shard_map/ppermute | solution.py:388
  55.4 9.1 %collective-permute-start.2 = (bf16[2,512,128]{2,1,0:T(8,128)(2,1)S(1)}, bf16[2,512,128]{2,1,0:T(8,128)(2,1)S(1)}, u32[]{:S(2)}, u32[]{:S(2)}) collective-permute-start(bf16[2,512,128]{2,1,0:T(8,128)(2,1)S(1)} %get-tuple-element.19), channel_id=1, source_target_pairs={{0,2},{1,3},{2,0},{3,1},{4,6},{5,7},{6,4},{7,5},{8,10},{9,11},{10,... | collective-permute-start | bytes 786440 | tf_op jit(solution)/shard_map/ppermute | solution.py:388
  55.4 13.9 %collective-permute-start.3 = (bf16[2,512,128]{2,1,0:T(8,128)(2,1)S(1)}, bf16[2,512,128]{2,1,0:T(8,128)(2,1)S(1)}, u32[]{:S(2)}, u32[]{:S(2)}) collective-permute-start(bf16[2,512,128]{2,1,0:T(8,128)(2,1)S(1)} %get-tuple-element.20), channel_id=1, source_target_pairs={{0,3},{1,2},{2,1},{3,0},{4,7},{5,6},{6,5},{7,4},{8,11},{9,10},{10,... | collective-permute-start | bytes 786440 | tf_op jit(solution)/shard_map/ppermute | solution.py:388
  57.3 12.1 %collective-permute-start.4 = (bf16[2,512,128]{2,1,0:T(8,128)(2,1)S(1)}, bf16[2,512,128]{2,1,0:T(8,128)(2,1)S(1)}, u32[]{:S(2)}, u32[]{:S(2)}) collective-permute-start(bf16[2,512,128]{2,1,0:T(8,128)(2,1)S(1)} %get-tuple-element.21), channel_id=1, source_target_pairs={{0,4},{1,5},{2,6},{3,7},{4,0},{5,1},{6,2},{7,3},{8,12},{9,13},{10,... | collective-permute-start | bytes 786440 | tf_op jit(solution)/shard_map/ppermute | solution.py:388
  57.3 13.5 %collective-permute-start.5 = (bf16[2,512,128]{2,1,0:T(8,128)(2,1)S(1)}, bf16[2,512,128]{2,1,0:T(8,128)(2,1)S(1)}, u32[]{:S(2)}, u32[]{:S(2)}) collective-permute-start(bf16[2,512,128]{2,1,0:T(8,128)(2,1)S(1)} %get-tuple-element.22), channel_id=1, source_target_pairs={{0,5},{1,4},{2,7},{3,6},{4,1},{5,0},{6,3},{7,2},{8,13},{9,12},{10,... | collective-permute-start | bytes 786440 | tf_op jit(solution)/shard_map/ppermute | solution.py:388
  58.9 18.5 %collective-permute-start.6 = (bf16[2,512,128]{2,1,0:T(8,128)(2,1)S(1)}, bf16[2,512,128]{2,1,0:T(8,128)(2,1)S(1)}, u32[]{:S(2)}, u32[]{:S(2)}) collective-permute-start(bf16[2,512,128]{2,1,0:T(8,128)(2,1)S(1)} %get-tuple-element.23), channel_id=1, source_target_pairs={{0,6},{1,7},{2,4},{3,5},{4,2},{5,3},{6,0},{7,1},{8,14},{9,15},{10,... | collective-permute-start | bytes 786440 | tf_op jit(solution)/shard_map/ppermute | solution.py:388
  64.5 16.8 %collective-permute-start.7 = (bf16[2,512,128]{2,1,0:T(8,128)(2,1)S(1)}, bf16[2,512,128]{2,1,0:T(8,128)(2,1)S(1)}, u32[]{:S(2)}, u32[]{:S(2)}) collective-permute-start(bf16[2,512,128]{2,1,0:T(8,128)(2,1)S(1)} %get-tuple-element.24), channel_id=1, source_target_pairs={{0,7},{1,6},{2,5},{3,4},{4,3},{5,2},{6,1},{7,0},{8,15},{9,14},{10,... | collective-permute-start | bytes 786440 | tf_op jit(solution)/shard_map/ppermute | solution.py:388
  81.3 1.0 copy-start.8
  82.3 1.0 copy-start.9
  83.3 1.0 copy-start.10
  84.3 1.0 copy-start.11
  85.3 0.9 copy-start.12
  89.0 29.8 %copy-start.6 = (bf16[1024,256]{1,0:T(8,128)(2,1)S(1)}, bf16[1024,256]{1,0:T(8,128)(2,1)}, u32[]{:S(2)}) copy-start(bf16[1024,256]{1,0:T(8,128)(2,1)} %gate.3) | copy-start | bytes 1572868
  (5 other events, 4.3 us)

commit v2 on v1

--- a/solution.py
+++ b/solution.py
@@ -12,7 +12,7 @@
 BF16 = jnp.bfloat16
 LANES = 128
 GROUP = 4
-PARAMS = pltpu.CompilerParams(vmem_limit_bytes=48 * 1024 * 1024)
+PARAMS = pltpu.CompilerParams(vmem_limit_bytes=60 * 1024 * 1024)
 
 
 def split_table(table):
@@ -91,7 +91,7 @@
     }
 
 
-def prep_kernel(scalars, signal, gate, mix, spec_one, spec_two, data, special, turned, strided):
+def prep_kernel(signal, gate, mix, data, turned):
     step = signal.shape[0] // LANES
     channels = signal.shape[1]
     devices = data.shape[0]
@@ -107,6 +107,10 @@
         data[:, part * rows : (part + 1) * rows, :] = (
             turned[...].reshape(devices, rows, LANES).astype(BF16)
         )
+
+
+def special_kernel(scalars, spec_one, spec_two, special, strided):
+    step = spec_one.shape[2] // LANES
     is_first = scalars[3] == 1
     for index, spec in enumerate((spec_one, spec_two)):
         for ri in range(2):
@@ -201,6 +205,7 @@
         inverse_row,
         out,
         filters,
+        landed,
     ) = refs[peers:]
     devices = data.shape[0]
     per_device = data.shape[1] // 2
@@ -209,8 +214,14 @@
     count = per_device // step
     row_count = 2 * step
     low_index = scalars[2]
-    for s in range(peers):
-        filters[low_index ^ s] = blocks[s][...].reshape(2, count, 2 * row_count, LANES)
+    copies = [
+        pltpu.make_async_copy(blocks[s], filters.at[low_index ^ s], landed.at[s])
+        for s in range(peers)
+    ]
+    for copy in copies:
+        copy.start()
+    for copy in copies:
+        copy.wait()
     cosine, sine = cosine_ref[0], sine_ref[0]
     top_row = lax.broadcasted_iota(jnp.int32, (step, 2 * LANES), 0) == 0
     corner = top_row[:, :LANES] & (lax.broadcasted_iota(jnp.int32, (step, LANES), 1) == 0)
@@ -247,7 +258,7 @@
         spectral = second_stage(turned, forward_two, forward_row)
         products = []
         for c in range(GROUP):
-            stored = filters[:, index, first + c]
+            stored = filters[:, index, pl.ds(pl.multiple_of((first + c) * 2 * row_count, 2 * row_count), 2 * row_count), :]
             h_real = stored[:, :row_count].reshape(rows, LANES).astype(F32)
             h_imag = stored[:, row_count:].reshape(rows, LANES).astype(F32)
             x_real, x_imag = spectral[c][:, :LANES], spectral[c][:, LANES:]
@@ -341,29 +352,28 @@
     ).astype(jnp.int32)
 
     other_half = pl.BlockSpec((2, 1, length, half_channels), lambda i, s: (0, 0, 0, 1 - s[1]))
-    data, special = pl.pallas_call(
-        prep_kernel,
+    special = pl.pallas_call(
+        special_kernel,
         grid_spec=pltpu.PrefetchScalarGridSpec(
             num_scalar_prefetch=1,
             grid=(1,),
-            in_specs=[whole(signal.shape)] * 3 + [other_half] * 2,
-            out_specs=[
-                whole((n, 2 * per_device, LANES)),
-                whole((2, 2, step // 2, LANES, half_channels)),
-            ],
-            scratch_shapes=[
-                pltpu.VMEM((channels * step, LANES), F32),
-                pltpu.VMEM((2, length, half_channels), F32),
-            ],
+            in_specs=[other_half] * 2,
+            out_specs=whole((2, 2, step // 2, LANES, half_channels)),
+            scratch_shapes=[pltpu.VMEM((2, length, half_channels), F32)],
         ),
-        out_shape=[
-            jax.ShapeDtypeStruct((n, 2 * per_device, LANES), BF16),
-            jax.ShapeDtypeStruct((2, 2, step // 2, LANES, half_channels), BF16),
-        ],
+        out_shape=jax.ShapeDtypeStruct((2, 2, step // 2, LANES, half_channels), BF16),
+        compiler_params=PARAMS,
+        name="special",
+    )(scalars, spectrum_one, spectrum_two)
+    special = lax.ppermute(special, "ctx", [(0, peers), (peers, 0)])
+    data = pl.pallas_call(
+        prep_kernel,
+        out_shape=jax.ShapeDtypeStruct((n, 2 * per_device, LANES), BF16),
+        scratch_shapes=[pltpu.VMEM((channels * step, LANES), F32)],
         compiler_params=PARAMS,
         name="prep",
-    )(scalars, signal, gate_one, mix_two, spectrum_one, spectrum_two)
-    special = lax.ppermute(special, "ctx", [(0, peers), (peers, 0)])
+    )(signal, gate_one, mix_two)
+    data, special = lax.optimization_barrier((data, special))
     data = lax.all_to_all(data, "ctx", split_axis=0, concat_axis=0, tiled=True)
 
     block_shape = (2, count * 4 * step, LANES)
@@ -397,11 +407,14 @@
             grid=(1,),
             in_specs=[pl.BlockSpec(memory_space=pltpu.SMEM)] * 2
             + [whole(data.shape)]
-            + [whole(block_shape)] * peers
+            + [pl.BlockSpec(memory_space=pl.ANY)] * peers
             + [by_half(tables[name].shape) for name in ("forward_one", "inverse_one", "cosine", "sine")]
             + [whole((3 * 2 * LANES, 2 * LANES))] * 4,
             out_specs=whole((n, per_device, LANES)),
-            scratch_shapes=[pltpu.VMEM((peers, 2, count, 4 * step, LANES), BF16)],
+            scratch_shapes=[
+                pltpu.VMEM((peers,) + block_shape, BF16),
+                pltpu.SemaphoreType.DMA((peers,)),
+            ],
         ),
         out_shape=jax.ShapeDtypeStruct((n, per_device, LANES), BF16),
         compiler_params=PARAMS,

time: 121 us -> 102 us (0.84)
  waiting for transfers between devices: 49.5 us -> 29.6 us
  local copies, waits for them, and re-layouts: 15 us -> 1.64 us
  Pallas kernels: 21.6 us -> 31.9 us
  starting transfers between devices: 16 us -> 19.9 us
    ppermute x1, waiting for transfers between devices: 27.3 us -> 4.38 us  [on_device(): special = lax.ppermute(special, 'ctx', [(0, peers), (peers, 0)])]
    unnamed x40 -> x18, local copies, waits for them, and re-layouts: 14.9 us -> 1.04 us
    ppermute x7, starting transfers between devices: 3.64 us -> 9.7 us  [on_device(): lax.ppermute(block, 'ctx', [(i, i ^ s) for i in range(n)])]
    pallas_call x1, Pallas kernels: 12 us -> 15.6 us  [on_device(): pl.pallas_call(functools.partial(conv_kernel, peers), grid_spec=pltpu.Pre...]
    pallas_call x1 -> x2, Pallas kernels: 2.64 us -> 5.96 us  [the longest x1 2.99 us: on_device(): pl.pallas_call(special_kernel, grid_spec=pltpu.PrefetchScalarGridSpec(num...]
    all_to_all x1, starting transfers between devices: 7.52 us -> 4.29 us  [on_device(): data = lax.all_to_all(data, 'ctx', split_axis=0, concat_axis=0, tiled=True)]
    ppermute x7, waiting for transfers between devices: 22.2 us -> 25.2 us  [on_device(): lax.ppermute(block, 'ctx', [(i, i ^ s) for i in range(n)])]
    pallas_call x1, Pallas kernels: 5.79 us -> 7.97 us  [on_device(): pl.pallas_call(pack_kernel, grid_spec=pltpu.PrefetchScalarGridSpec(num_sc...]
  transfers between devices with their start and end apart: 9 -> 9, of which waited for: 6 -> 6; matrix products, arithmetic and copies ran while one was open for 0% -> 0% of each run, Pallas kernels for 5% -> 11%
where the time goes in v2:
time: 102 us
  Pallas kernels  31.9 us (31%)
  waiting for transfers between devices  29.6 us (29%)
  starting transfers between devices  19.9 us (20%)
  blocking collectives  18.8 us (18%)
  local copies, waits for them, and re-layouts  1.64 us (2%)
    ppermute x7, waiting for transfers between devices, on_device(): lax.ppermute(block, 'ctx', [(i, i ^ s) for i in range(n)])  25.2 us
    all_to_all x1, blocking collectives, on_device(): back = lax.all_to_all(out, 'ctx', split_axis=0, concat_axis=0, tiled=True)  18.8 us
    pallas_call x1, Pallas kernels, on_device(): pl.pallas_call(functools.partial(conv_kernel, peers), grid_spec=pltpu.Pre...  15.6 us
    ppermute x7, starting transfers between devices, on_device(): lax.ppermute(block, 'ctx', [(i, i ^ s) for i in range(n)])  9.7 us
    pallas_call x1, Pallas kernels, on_device(): pl.pallas_call(pack_kernel, grid_spec=pltpu.PrefetchScalarGridSpec(num_sc...  7.97 us
    ppermute x1, starting transfers between devices, on_device(): special = lax.ppermute(special, 'ctx', [(0, peers), (peers, 0)])  5.93 us
    ppermute x1, waiting for transfers between devices, on_device(): special = lax.ppermute(special, 'ctx', [(0, peers), (peers, 0)])  4.38 us
    all_to_all x1, starting transfers between devices, on_device(): data = lax.all_to_all(data, 'ctx', split_axis=0, concat_axis=0, tiled=True)  4.29 us
  transfers between devices with their start and end apart: 9, of which 6 were waited for; matrix products, arithmetic and copies ran while one was open for 0% of the time, Pallas kernels for 11%

profile of v2, /device:TPU:0, one launch (start us, length us, event | category | flops | bytes accessed | tf_op | source)
XLA Modules:
  0.0 101.9 jit_solution(9518659230369344868)
XLA Ops:
  0.0 0.6 stack.31.scalars
  0.6 3.0 %special.1 = bf16[2,2,4,128,128]{4,3,2,1,0:T(8,128)(2,1)} custom-call(s32[5]{0:T(128)} %stack.31.scalars, bf16[2,2,1024,256]{3,2,1,0:T(8,128)(2,1)} %spec_one.3, bf16[2,2,1024,256]{3,2,1,0:T(8,128)(2,1)} %spec_two.3), custom_call_target="tpu_custom_call" | custom-call | tf_op jit(solution)/shard_map/special/pallas_call | solution.py:355
  3.6 5.9 %collective-permute-start = (bf16[2,2,4,128,128]{4,3,2,1,0:T(8,128)(2,1)}, bf16[2,2,4,128,128]{4,3,2,1,0:T(8,128)(2,1)S(1)}, u32[]{:S(2)}, u32[]{:S(2)}) collective-permute-start(bf16[2,2,4,128,128]{4,3,2,1,0:T(8,128)(2,1)} %special.1), channel_id=1, source_target_pairs={{0,8},{8,0},{16,24},{24,16}} | collective-permute-start | bytes 1572872 | tf_op jit(solution)/shard_map/ppermute | solution.py:368
  9.5 3.0 %prep.1 = bf16[16,256,128]{2,1,0:T(8,128)(2,1)} custom-call(bf16[1024,256]{1,0:T(8,128)(2,1)} %signal.1, bf16[1024,256]{1,0:T(8,128)(2,1)} %gate.2, bf16[1024,256]{1,0:T(8,128)(2,1)} %mix.1), custom_call_target="tpu_custom_call" | custom-call | tf_op jit(solution)/shard_map/prep/pallas_call | solution.py:369
  12.5 4.4 %collective-permute-done.special = bf16[2,2,4,128,128]{4,3,2,1,0:T(8,128)(2,1)S(1)} collective-permute-done((bf16[2,2,4,128,128]{4,3,2,1,0:T(8,128)(2,1)}, bf16[2,2,4,128,128]{4,3,2,1,0:T(8,128)(2,1)S(1)}, u32[]{:S(2)}, u32[]{:S(2)}) %collective-permute-start) | collective-permute-done | bytes 524320 | tf_op jit(solution)/shard_map/ppermute | solution.py:368
  16.9 4.3 %all-to-all-start = ((bf16[16,256,128]{2,1,0:T(8,128)(2,1)}), bf16[16,256,128]{2,1,0:T(8,128)(2,1)S(1)}, u32[]{:S(2)}, u32[]{:S(2)}) async-start(bf16[16,256,128]{2,1,0:T(8,128)(2,1)} %prep.1), calls=%async_computation | async-start | bytes 2097152 | tf_op jit(solution)/shard_map/all_to_all | solution.py:377
  21.2 8.0 %pack.1 = (bf16[2,512,128]{2,1,0:T(8,128)(2,1)}, bf16[2,512,128]{2,1,0:T(8,128)(2,1)}, bf16[2,512,128]{2,1,0:T(8,128)(2,1)}, bf16[2,512,128]{2,1,0:T(8,128)(2,1)...) custom-call(s32[5]{0:T(128)} %stack.31.scalars, ...), custom_call_target="tpu_custom_call" | custom-call | tf_op jit(solution)/shard_map/pack/pallas_call | solution.py:381
  29.2 0.4 collective-permute-start.1
  29.6 1.7 %collective-permute-start.2 = (bf16[2,512,128]{2,1,0:T(8,128)(2,1)}, bf16[2,512,128]{2,1,0:T(8,128)(2,1)S(1)}, u32[]{:S(2)}, u32[]{:S(2)}) collective-permute-start(bf16[2,512,128]{2,1,0:T(8,128)(2,1)} %get-tuple-element.19), channel_id=1, source_target_pairs={{0,2},{1,3},{2,0},{3,1},{4,6},{5,7},{6,4},{7,5},{8,10},{9,11},{10,... | collective-permute-start | bytes 786440 | tf_op jit(solution)/shard_map/ppermute | solution.py:398
  31.3 0.0 collective-permute-start.3
  31.3 1.7 %collective-permute-start.4 = (bf16[2,512,128]{2,1,0:T(8,128)(2,1)}, bf16[2,512,128]{2,1,0:T(8,128)(2,1)S(1)}, u32[]{:S(2)}, u32[]{:S(2)}) collective-permute-start(bf16[2,512,128]{2,1,0:T(8,128)(2,1)} %get-tuple-element.21), channel_id=1, source_target_pairs={{0,4},{1,5},{2,6},{3,7},{4,0},{5,1},{6,2},{7,3},{8,12},{9,13},{10,... | collective-permute-start | bytes 786440 | tf_op jit(solution)/shard_map/ppermute | solution.py:398
  33.0 0.1 collective-permute-start.5
  33.1 2.6 %collective-permute-start.6 = (bf16[2,512,128]{2,1,0:T(8,128)(2,1)}, bf16[2,512,128]{2,1,0:T(8,128)(2,1)S(1)}, u32[]{:S(2)}, u32[]{:S(2)}) collective-permute-start(bf16[2,512,128]{2,1,0:T(8,128)(2,1)} %get-tuple-element.23), channel_id=1, source_target_pairs={{0,6},{1,7},{2,4},{3,5},{4,2},{5,3},{6,0},{7,1},{8,14},{9,15},{10,... | collective-permute-start | bytes 786440 | tf_op jit(solution)/shard_map/ppermute | solution.py:398
  35.7 5.6 %collective-permute-done.2.refs_2_ = bf16[2,512,128]{2,1,0:T(8,128)(2,1)S(1)} collective-permute-done((bf16[2,512,128]{2,1,0:T(8,128)(2,1)}, bf16[2,512,128]{2,1,0:T(8,128)(2,1)S(1)}, u32[]{:S(2)}, u32[]{:S(2)}) %collective-permute-start.2) | collective-permute-done | bytes 262176 | tf_op jit(solution)/shard_map/ppermute | solution.py:398
  41.3 3.2 %collective-permute-start.7 = (bf16[2,512,128]{2,1,0:T(8,128)(2,1)}, bf16[2,512,128]{2,1,0:T(8,128)(2,1)S(1)}, u32[]{:S(2)}, u32[]{:S(2)}) collective-permute-start(bf16[2,512,128]{2,1,0:T(8,128)(2,1)} %get-tuple-element.24), channel_id=1, source_target_pairs={{0,7},{1,6},{2,5},{3,4},{4,3},{5,2},{6,1},{7,0},{8,15},{9,14},{10,... | collective-permute-start | bytes 786440 | tf_op jit(solution)/shard_map/ppermute | solution.py:398
  44.5 3.7 %collective-permute-done.3.refs_3_ = bf16[2,512,128]{2,1,0:T(8,128)(2,1)S(1)} collective-permute-done((bf16[2,512,128]{2,1,0:T(8,128)(2,1)}, bf16[2,512,128]{2,1,0:T(8,128)(2,1)S(1)}, u32[]{:S(2)}, u32[]{:S(2)}) %collective-permute-start.3) | collective-permute-done | bytes 262176 | tf_op jit(solution)/shard_map/ppermute | solution.py:398
  48.3 3.7 %collective-permute-done.5.refs_5_ = bf16[2,512,128]{2,1,0:T(8,128)(2,1)S(1)} collective-permute-done((bf16[2,512,128]{2,1,0:T(8,128)(2,1)}, bf16[2,512,128]{2,1,0:T(8,128)(2,1)S(1)}, u32[]{:S(2)}, u32[]{:S(2)}) %collective-permute-start.5) | collective-permute-done | bytes 262176 | tf_op jit(solution)/shard_map/ppermute | solution.py:398
  52.0 7.4 %collective-permute-done.6.refs_6_ = bf16[2,512,128]{2,1,0:T(8,128)(2,1)S(1)} collective-permute-done((bf16[2,512,128]{2,1,0:T(8,128)(2,1)}, bf16[2,512,128]{2,1,0:T(8,128)(2,1)S(1)}, u32[]{:S(2)}, u32[]{:S(2)}) %collective-permute-start.6) | collective-permute-done | bytes 262176 | tf_op jit(solution)/shard_map/ppermute | solution.py:398
  59.4 4.7 %collective-permute-done.7.refs_7_ = bf16[2,512,128]{2,1,0:T(8,128)(2,1)S(1)} collective-permute-done((bf16[2,512,128]{2,1,0:T(8,128)(2,1)}, bf16[2,512,128]{2,1,0:T(8,128)(2,1)S(1)}, u32[]{:S(2)}, u32[]{:S(2)}) %collective-permute-start.7) | collective-permute-done | bytes 262176 | tf_op jit(solution)/shard_map/ppermute | solution.py:398
  64.1 0.6 copy-done.8
  64.8 0.4 copy-done
  65.2 15.6 %convolve.1 = bf16[16,128,128]{2,1,0:T(8,128)(2,1)} custom-call(s32[5]{0:T(128)} %stack.31.scalars, f32[256]{0:T(256)} %skip_one.1, f32[256]{0:T(256)} %skip_two.1, bf16[16,256,128]{2,1,0:T(8,128)(2,1)} %copy-done, bf16[2,512,128]{2,1,0:T(8,128)(2,1)} %get-tuple-element.17.refs_0_, bf16[2,512,128]{2,1,0:T(8,128)(2,1)} %copy-done.2, ...), custom_call_target="tpu_custom_call" | custom-call | tf_op jit(solution)/shard_map/convolve/pallas_call | solution.py:403
  80.8 18.8 %all_to_all.10.back = bf16[16,128,128]{2,1,0:T(8,128)(2,1)} all-to-all(bf16[16,128,128]{2,1,0:T(8,128)(2,1)} %convolve.1), channel_id=1, replica_groups=mesh['group'=2,'ctx'=16] {'ctx'}, dimensions={0} | all-to-all | bytes 1048576 | tf_op jit(solution)/shard_map/all_to_all | solution.py:424
  99.5 2.4 %final.1 = bf16[1024,256]{1,0:T(8,128)(2,1)} custom-call(bf16[16,128,128]{2,1,0:T(8,128)(2,1)} %all_to_all.10.back, bf16[1024,256]{1,0:T(8,128)(2,1)} %gate.3), custom_call_target="tpu_custom_call" | custom-call | tf_op jit(solution)/shard_map/final/pallas_call | solution.py:425
  (19 shorter events, 0.0 us)
Async XLA Ops:
  3.6 13.3 %collective-permute-start = (bf16[2,2,4,128,128]{4,3,2,1,0:T(8,128)(2,1)}, bf16[2,2,4,128,128]{4,3,2,1,0:T(8,128)(2,1)S(1)}, u32[]{:S(2)}, u32[]{:S(2)}) collective-permute-start(bf16[2,2,4,128,128]{4,3,2,1,0:T(8,128)(2,1)} %special.1), channel_id=1, source_target_pairs={{0,8},{8,0},{16,24},{24,16}} | collective-permute-start | bytes 1572872 | tf_op jit(solution)/shard_map/ppermute | solution.py:368
  16.9 4.3 %copy-start.1 = (bf16[2,2,4,128,128]{4,3,2,1,0:T(8,128)(2,1)}, bf16[2,2,4,128,128]{4,3,2,1,0:T(8,128)(2,1)S(1)}, u32[]{:S(2)}) copy-start(bf16[2,2,4,128,128]{4,3,2,1,0:T(8,128)(2,1)S(1)} %collective-permute-done.special) | copy-start | bytes 1572868
  16.9 47.2 %all-to-all-start = ((bf16[16,256,128]{2,1,0:T(8,128)(2,1)}), bf16[16,256,128]{2,1,0:T(8,128)(2,1)S(1)}, u32[]{:S(2)}, u32[]{:S(2)}) async-start(bf16[16,256,128]{2,1,0:T(8,128)(2,1)} %prep.1), calls=%async_computation | async-start | bytes 2097152 | tf_op jit(solution)/shard_map/all_to_all | solution.py:377
  29.2 3.9 %collective-permute-start.1 = (bf16[2,512,128]{2,1,0:T(8,128)(2,1)}, bf16[2,512,128]{2,1,0:T(8,128)(2,1)S(1)}, u32[]{:S(2)}, u32[]{:S(2)}) collective-permute-start(bf16[2,512,128]{2,1,0:T(8,128)(2,1)} %get-tuple-element.18), channel_id=1, source_target_pairs={{0,1},{1,0},{2,3},{3,2},{4,5},{5,4},{6,7},{7,6},{8,9},{9,8},{10,11... | collective-permute-start | bytes 786440 | tf_op jit(solution)/shard_map/ppermute | solution.py:398
  29.6 11.7 %collective-permute-start.2 = (bf16[2,512,128]{2,1,0:T(8,128)(2,1)}, bf16[2,512,128]{2,1,0:T(8,128)(2,1)S(1)}, u32[]{:S(2)}, u32[]{:S(2)}) collective-permute-start(bf16[2,512,128]{2,1,0:T(8,128)(2,1)} %get-tuple-element.19), channel_id=1, source_target_pairs={{0,2},{1,3},{2,0},{3,1},{4,6},{5,7},{6,4},{7,5},{8,10},{9,11},{10,... | collective-permute-start | bytes 786440 | tf_op jit(solution)/shard_map/ppermute | solution.py:398
  31.3 17.0 %collective-permute-start.3 = (bf16[2,512,128]{2,1,0:T(8,128)(2,1)}, bf16[2,512,128]{2,1,0:T(8,128)(2,1)S(1)}, u32[]{:S(2)}, u32[]{:S(2)}) collective-permute-start(bf16[2,512,128]{2,1,0:T(8,128)(2,1)} %get-tuple-element.20), channel_id=1, source_target_pairs={{0,3},{1,2},{2,1},{3,0},{4,7},{5,6},{6,5},{7,4},{8,11},{9,10},{10,... | collective-permute-start | bytes 786440 | tf_op jit(solution)/shard_map/ppermute | solution.py:398
  31.3 17.0 %collective-permute-start.4 = (bf16[2,512,128]{2,1,0:T(8,128)(2,1)}, bf16[2,512,128]{2,1,0:T(8,128)(2,1)S(1)}, u32[]{:S(2)}, u32[]{:S(2)}) collective-permute-start(bf16[2,512,128]{2,1,0:T(8,128)(2,1)} %get-tuple-element.21), channel_id=1, source_target_pairs={{0,4},{1,5},{2,6},{3,7},{4,0},{5,1},{6,2},{7,3},{8,12},{9,13},{10,... | collective-permute-start | bytes 786440 | tf_op jit(solution)/shard_map/ppermute | solution.py:398
  33.0 19.0 %collective-permute-start.5 = (bf16[2,512,128]{2,1,0:T(8,128)(2,1)}, bf16[2,512,128]{2,1,0:T(8,128)(2,1)S(1)}, u32[]{:S(2)}, u32[]{:S(2)}) collective-permute-start(bf16[2,512,128]{2,1,0:T(8,128)(2,1)} %get-tuple-element.22), channel_id=1, source_target_pairs={{0,5},{1,4},{2,7},{3,6},{4,1},{5,0},{6,3},{7,2},{8,13},{9,12},{10,... | collective-permute-start | bytes 786440 | tf_op jit(solution)/shard_map/ppermute | solution.py:398
  33.1 31.0 %copy-start.2 = (bf16[2,512,128]{2,1,0:T(8,128)(2,1)}, bf16[2,512,128]{2,1,0:T(8,128)(2,1)S(1)}, u32[]{:S(2)}) copy-start(bf16[2,512,128]{2,1,0:T(8,128)(2,1)S(1)} %collective-permute-done.1.refs_1_) | copy-start | bytes 786436
  33.1 26.3 %collective-permute-start.6 = (bf16[2,512,128]{2,1,0:T(8,128)(2,1)}, bf16[2,512,128]{2,1,0:T(8,128)(2,1)S(1)}, u32[]{:S(2)}, u32[]{:S(2)}) collective-permute-start(bf16[2,512,128]{2,1,0:T(8,128)(2,1)} %get-tuple-element.23), channel_id=1, source_target_pairs={{0,6},{1,7},{2,4},{3,5},{4,2},{5,3},{6,0},{7,1},{8,14},{9,15},{10,... | collective-permute-start | bytes 786440 | tf_op jit(solution)/shard_map/ppermute | solution.py:398
  41.3 22.8 %copy-start.3 = (bf16[2,512,128]{2,1,0:T(8,128)(2,1)}, bf16[2,512,128]{2,1,0:T(8,128)(2,1)S(1)}, u32[]{:S(2)}) copy-start(bf16[2,512,128]{2,1,0:T(8,128)(2,1)S(1)} %collective-permute-done.2.refs_2_) | copy-start | bytes 786436
  41.3 22.8 %collective-permute-start.7 = (bf16[2,512,128]{2,1,0:T(8,128)(2,1)}, bf16[2,512,128]{2,1,0:T(8,128)(2,1)S(1)}, u32[]{:S(2)}, u32[]{:S(2)}) collective-permute-start(bf16[2,512,128]{2,1,0:T(8,128)(2,1)} %get-tuple-element.24), channel_id=1, source_target_pairs={{0,7},{1,6},{2,5},{3,4},{4,3},{5,2},{6,1},{7,0},{8,15},{9,14},{10,... | collective-permute-start | bytes 786440 | tf_op jit(solution)/shard_map/ppermute | solution.py:398
  48.3 15.8 %copy-start.4 = (bf16[2,512,128]{2,1,0:T(8,128)(2,1)}, bf16[2,512,128]{2,1,0:T(8,128)(2,1)S(1)}, u32[]{:S(2)}) copy-start(bf16[2,512,128]{2,1,0:T(8,128)(2,1)S(1)} %collective-permute-done.3.refs_3_) | copy-start | bytes 786436
  48.3 15.8 %copy-start.5 = (bf16[2,512,128]{2,1,0:T(8,128)(2,1)}, bf16[2,512,128]{2,1,0:T(8,128)(2,1)S(1)}, u32[]{:S(2)}) copy-start(bf16[2,512,128]{2,1,0:T(8,128)(2,1)S(1)} %collective-permute-done.4.refs_4_) | copy-start | bytes 786436
  52.0 12.2 %copy-start.6 = (bf16[2,512,128]{2,1,0:T(8,128)(2,1)}, bf16[2,512,128]{2,1,0:T(8,128)(2,1)S(1)}, u32[]{:S(2)}) copy-start(bf16[2,512,128]{2,1,0:T(8,128)(2,1)S(1)} %collective-permute-done.5.refs_5_) | copy-start | bytes 786436
  59.4 4.7 %copy-start.7 = (bf16[2,512,128]{2,1,0:T(8,128)(2,1)}, bf16[2,512,128]{2,1,0:T(8,128)(2,1)S(1)}, u32[]{:S(2)}) copy-start(bf16[2,512,128]{2,1,0:T(8,128)(2,1)S(1)} %collective-permute-done.6.refs_6_) | copy-start | bytes 786436
  64.1 0.7 copy-start.8
  64.1 1.1 %copy-start = (bf16[16,256,128]{2,1,0:T(8,128)(2,1)}, bf16[16,256,128]{2,1,0:T(8,128)(2,1)S(1)}, u32[]{:S(2)}) copy-start(bf16[16,256,128]{2,1,0:T(8,128)(2,1)S(1)} %all-to-all-done.data) | copy-start | bytes 3145732

commit v3 on v2

v3 whole, which is shorter than its diff:
```python
import functools

import jax
import jax.numpy as jnp
import numpy as np
from jax import lax
from jax.experimental import pallas as pl
from jax.experimental.pallas import tpu as pltpu
from jax.sharding import PartitionSpec as P

F32 = jnp.float32
BF16 = jnp.bfloat16
LANES = 128
GROUP = 8
SMALL = pltpu.CompilerParams(vmem_limit_bytes=24 * 1024 * 1024)
PARAMS = pltpu.CompilerParams(vmem_limit_bytes=60 * 1024 * 1024)


def split_table(table):
    high = table.astype(jnp.bfloat16)
    low = (table - high.astype(np.float64)).astype(jnp.bfloat16)
    return high, low


def make_tables(n, step):
    rows = n * step
    first_len = 2 * rows
    total = first_len * LANES
    turn = 2.0 * np.pi
    n1 = np.arange(rows)
    n2 = np.arange(LANES)
    forward_one, inverse_one, cosines, sines = [], [], [], []
    for half in range(2):
        k1 = np.array(
            [
                2 * (half * (n // 2) + source) + a + 2 * n * low
                for source in range(n // 2)
                for a in range(2)
                for low in range(step)
            ]
        )
        k1[:step] = [2 * n * j for j in range(step // 2)] + [n + 2 * n * j for j in range(step // 2)]
        angle = turn * ((k1[:, None] * n1[None, :]) % first_len) / first_len
        real_rows, imag_rows = np.cos(angle), -np.sin(angle)
        imag_rows[0] = np.cos(np.pi * n1)
        table = np.concatenate([real_rows, imag_rows], axis=0)
        forward_one.append(table)
        weight = np.full((2 * rows, 1), 2.0 / total)
        weight[0] = weight[rows] = 1.0 / total
        inverse_one.append((table * weight).T)
        angle = turn * ((k1[:, None] * n2[None, :]) % total) / total
        angle[0] = 0.0
        cosines.append(np.cos(angle))
        sines.append(-np.sin(angle))
    angle = turn * ((n2[:, None] * n2[None, :]) % LANES) / LANES
    cosine, sine = np.cos(angle), np.sin(angle)
    forward_two = np.block([[cosine, -sine], [sine, cosine]])
    inverse_two = np.block([[cosine, sine], [-sine, cosine]])
    half_lanes = LANES // 2
    even = turn * ((n2[:, None] * np.arange(half_lanes)[None, :]) % LANES) / LANES
    odd = turn * ((n2[:, None] * (1 + 2 * np.arange(half_lanes))[None, :]) % (2 * LANES)) / (2 * LANES)
    zero = np.zeros((LANES, half_lanes))
    even_imag = -np.sin(even)
    even_imag[:, 0] = np.cos(np.pi * n2)
    forward_row = np.block(
        [[np.cos(even), zero, even_imag, zero], [zero, np.cos(odd), zero, -np.sin(odd)]]
    )
    weight = np.full((2 * LANES, 1), 2.0)
    weight[0] = weight[LANES] = 1.0
    inverse_row = (forward_row * weight[:, 0][None, :]).T

    def along_rows(table):
        high, low = split_table(table)
        return np.concatenate([high, low, high], axis=0)

    def along_columns(table):
        high, low = split_table(table)
        return np.concatenate([high, low, high], axis=1)

    def two_columns(table):
        return np.concatenate(split_table(table), axis=1)

    return {
        "forward_one": np.stack([two_columns(t) for t in forward_one]),
        "inverse_one": np.stack([along_columns(t) for t in inverse_one]),
        "turns": np.stack([cosines, sines], axis=1).astype(np.float32),
        "forward_two": along_rows(forward_two),
        "inverse_two": along_rows(inverse_two),
        "forward_row": along_rows(forward_row),
        "inverse_row": along_rows(inverse_row),
    }


def prep_kernel(signal, gate, mix, data, turned):
    step = signal.shape[0] // LANES
    channels = signal.shape[1]
    devices = data.shape[0]
    rows = data.shape[1] // 2
    for part in range(2):
        for t in range(step):
            piece = pl.ds(t * LANES, LANES)
            if part == 0:
                value = signal[piece, :].astype(F32)
            else:
                value = gate[piece, :].astype(F32) * mix[piece, :].astype(F32)
            turned[pl.ds(t, channels, stride=step), :] = value.T
        data[:, part * rows : (part + 1) * rows, :] = (
            turned[...].reshape(devices, rows, LANES).astype(BF16)
        )


def place():
    n = lax.axis_size("ctx")
    me = lax.axis_index("ctx")
    peers = n // 2
    return me, me // peers, lax.rem(me, peers), me == 0, me == peers


def special_kernel(spec_one, spec_two, special, raw, strided, landed):
    step = spec_one.shape[2] // LANES
    width = raw.shape[3]
    _, half, _, is_first, _ = place()
    columns = pl.ds(pl.multiple_of((1 - half) * width, width), width)
    copies = [
        pltpu.make_async_copy(spec.at[ri, 0, :, columns], raw.at[index, ri], landed.at[index, ri])
        for index, spec in enumerate((spec_one, spec_two))
        for ri in range(2)
    ]
    for copy in copies:
        copy.start()
    for index in range(2):
        for ri in range(2):
            copies[2 * index + ri].wait()
            strided[ri] = raw[index, ri].astype(F32)
        for j in range(step // 2):
            pair = [strided[ri, pl.ds(j, LANES, stride=step), :] for ri in range(2)]
            if j == 0:
                packed = pack_row(strided, pair[0], pair[1], step)
                pair = [jnp.where(is_first, p, v) for p, v in zip(packed, pair)]
            for ri in range(2):
                special[index, ri, j] = pair[ri].astype(BF16)


def pack_row(strided, real_part, imag_part, step):
    half = LANES // 2
    odd = [strided[ri, pl.ds(step // 2, LANES, stride=step), :] for ri in range(2)]
    packed_real = jnp.concatenate([real_part[:half], odd[0][:half]], axis=0)
    packed_imag = jnp.concatenate([imag_part[:half], odd[1][:half]], axis=0)
    top = lax.broadcasted_iota(jnp.int32, packed_imag.shape, 0) == 0
    middle = jnp.broadcast_to(real_part[half : half + 1], packed_imag.shape)
    return packed_real, jnp.where(top, middle, packed_imag)


def pack_kernel(index, spec, special, *refs):
    *outs, raw, strided, turned, landed = refs
    peers = len(outs)
    step = spec.shape[2] // LANES
    channels = raw.shape[3]
    _, half, low_index, is_first, is_middle = place()
    row_count = 2 * step
    columns = pl.ds(pl.multiple_of(half * channels, channels), channels)
    copies = {
        (a, ri): pltpu.make_async_copy(
            spec.at[ri, a, :, columns], raw.at[a, ri], landed.at[a, ri]
        )
        for a in (1, 0)
        for ri in range(2)
    }
    for copy in copies.values():
        copy.start()
    for a in (1, 0):
        for ri in range(2):
            copies[a, ri].wait()
            strided[ri] = raw[a, ri].astype(F32)
        for low in range(step):
            pair = [strided[ri, pl.ds(low, LANES, stride=step), :] for ri in range(2)]
            if a == 0 and low == 0:
                packed = pack_row(strided, pair[0], pair[1], step)
                pair = [jnp.where(is_first, p, v) for p, v in zip(packed, pair)]
            for ri in range(2):
                value = pair[ri]
                if a == 0 and low < step // 2:
                    other = special[index, ri, low].astype(F32)
                    value = jnp.where(is_middle, other, value)
                elif a == 0:
                    j = low - step // 2
                    own = strided[ri, pl.ds(j, LANES, stride=step), :]
                    other = special[index, ri, j].astype(F32)
                    value = jnp.where(is_first, other, jnp.where(is_middle, own, value))
                row = ri * row_count + a * step + low
                turned[pl.ds(row, channels, stride=2 * row_count), :] = value.T
    block = channels // peers * 2 * row_count
    for s, out in enumerate(outs):
        start = pl.multiple_of((low_index ^ s) * block, block)
        out[...] = turned[pl.ds(start, block), :].astype(BF16)


def split_value(value):
    high = value.astype(BF16)
    return high, (value - high.astype(F32)).astype(BF16)


def split_columns(value):
    high, low = split_value(value)
    return jnp.concatenate([high, high, low], axis=1)


def split_rows(value):
    high, low = split_value(value)
    return jnp.concatenate([high, high, low], axis=0)


def dot(left, right):
    return jnp.dot(left, right, preferred_element_type=F32)


HALVED = ("forward_one", "turns", "inverse_one")
PARTS = ("data", "forward_one", "turns", "forward_two", "forward_row")
LATER = ("inverse_two", "inverse_row", "inverse_one")


def conv_kernel(peers, gated, skip, *refs):
    names = PARTS + LATER
    sources = dict(zip(names, refs))
    blocks, refs = refs[len(names) : len(names) + peers], refs[len(names) + peers :]
    out, refs = refs[0], refs[1:]
    buffers = dict(zip(names, refs))
    filters, landed = refs[len(names) :]
    me, half, low_index, _, _ = place()
    copies = {}
    for i, name in enumerate(names):
        source = sources[name].at[half] if name in HALVED else sources[name]
        copies[name] = pltpu.make_async_copy(source, buffers[name], landed.at[i])
    for s in range(peers):
        copies[s] = pltpu.make_async_copy(
            blocks[s], filters.at[low_index ^ s], landed.at[len(names) + s]
        )
    for name in PARTS + tuple(range(peers)) + LATER:
        copies[name].start()
    awaited = set()

    def need(*wanted):
        for name in wanted:
            if name not in awaited:
                awaited.add(name)
                copies[name].wait()

    data, turns = buffers["data"], buffers["turns"]
    devices = data.shape[0]
    per_device = out.shape[1]
    rows = turns.shape[1]
    step = rows // devices
    count = per_device // step
    row_count = 2 * step
    top_row = lax.broadcasted_iota(jnp.int32, (step, 2 * LANES), 0) == 0
    corner = top_row[:, :LANES] & (lax.broadcasted_iota(jnp.int32, (step, LANES), 1) == 0)

    def with_top(values, tops):
        return [
            jnp.concatenate(
                [jnp.where(top_row, tops[c * step : (c + 1) * step], v[:step]), v[step:]], axis=0
            )
            for c, v in enumerate(values)
        ]

    def second_stage(values, table, row_table):
        need(table, row_table)
        main = dot(split_columns(jnp.concatenate(values, axis=0)), buffers[table][...])
        tops = dot(split_columns(jnp.concatenate([v[:step] for v in values], axis=0)), buffers[row_table][...])
        return with_top([main[c * rows : (c + 1) * rows] for c in range(GROUP)], tops)

    def convolve(fields, first):
        joined = jnp.concatenate(fields, axis=1)
        need("forward_one", "turns")
        cosine, sine = turns[0], turns[1]
        staged = dot(buffers["forward_one"][...], jnp.concatenate([joined, joined], axis=0))
        turned = []
        for c in range(GROUP):
            lanes = slice(c * LANES, (c + 1) * LANES)
            real_part, imag_part = staged[:rows, lanes], staged[rows:, lanes]
            turned.append(
                jnp.concatenate(
                    [
                        real_part * cosine - imag_part * sine,
                        real_part * sine + imag_part * cosine,
                    ],
                    axis=1,
                )
            )
        spectral = second_stage(turned, "forward_two", "forward_row")
        need(*range(peers))
        products = []
        for c in range(GROUP):
            stored = filters[:, pl.ds(pl.multiple_of((first + c) * 2 * row_count, 2 * row_count), 2 * row_count), :]
            h_real = stored[:, :row_count].reshape(rows, LANES).astype(F32)
            h_imag = stored[:, row_count:].reshape(rows, LANES).astype(F32)
            x_real, x_imag = spectral[c][:, :LANES], spectral[c][:, LANES:]
            real_real, imag_imag = x_real * h_real, x_imag * h_imag
            y_real = real_real - imag_imag
            y_imag = x_real * h_imag + x_imag * h_real
            y_real = jnp.concatenate(
                [jnp.where(corner, real_real[:step], y_real[:step]), y_real[step:]], axis=0
            )
            y_imag = jnp.concatenate(
                [jnp.where(corner, imag_imag[:step], y_imag[:step]), y_imag[step:]], axis=0
            )
            products.append(jnp.concatenate([y_real, y_imag], axis=1))
        inverted = second_stage(products, "inverse_two", "inverse_row")
        columns = []
        for c in range(GROUP):
            real_part, imag_part = inverted[c][:, :LANES], inverted[c][:, LANES:]
            columns.append(
                jnp.concatenate(
                    [
                        real_part * cosine + imag_part * sine,
                        imag_part * cosine - real_part * sine,
                    ],
                    axis=0,
                )
            )
        need("inverse_one")
        result = dot(buffers["inverse_one"][...], split_rows(jnp.concatenate(columns, axis=1)))
        return [result[:, c * LANES : (c + 1) * LANES] for c in range(GROUP)]

    need("data")
    size = GROUP * step
    for first in range(0, count, GROUP):

        def channels(start):
            values = data[:, start : start + size, :].astype(F32)
            return [
                values[:, c * step : (c + 1) * step, :].reshape(rows, LANES) for c in range(GROUP)
            ]

        base = first * step
        fields = channels(base)
        results = convolve([f.astype(BF16) for f in fields], first)
        results = [skip[me * count + first + c] * fields[c] + results[c] for c in range(GROUP)]
        if gated:
            results = [g * r for g, r in zip(channels(per_device + base), results)]
        results = [r.reshape(devices, step, LANES) for r in results]
        out[:, base : base + size, :] = jnp.concatenate(results, axis=1).astype(BF16)


def final_kernel(back, gate, out, turned):
    step = gate.shape[0] // LANES
    channels = gate.shape[1]
    turned[...] = back[...].astype(F32).reshape(channels * step, LANES)
    for t in range(step):
        piece = pl.ds(t * LANES, LANES)
        value = turned[pl.ds(t, channels, stride=step), :].T
        out[piece, :] = (gate[piece, :].astype(F32) * value).astype(BF16)


ANY = pl.BlockSpec(memory_space=pl.ANY)
VMEM = pl.BlockSpec(memory_space=pltpu.VMEM)


def run_convolve(skip, values, blocks, gated, tables, n, step, count):
    peers = n // 2
    per_device = count * step
    operands = dict(tables, data=values)
    operands = [operands[name] for name in PARTS + LATER]
    buffers = [
        pltpu.VMEM(o.shape[1:] if name in HALVED else o.shape, o.dtype)
        for name, o in zip(PARTS + LATER, operands)
    ]
    return pl.pallas_call(
        functools.partial(conv_kernel, peers, gated),
        in_specs=[pl.BlockSpec(memory_space=pltpu.SMEM)] + [ANY] * (len(operands) + peers),
        out_specs=VMEM,
        out_shape=jax.ShapeDtypeStruct((n, per_device, LANES), BF16),
        scratch_shapes=buffers
        + [
            pltpu.VMEM((peers,) + blocks[0].shape, BF16),
            pltpu.SemaphoreType.DMA((len(operands) + peers,)),
        ],
        compiler_params=PARAMS,
        cost_estimate=pl.CostEstimate(
            flops=1200 * 1000 * 1000, bytes_accessed=6 * 1024 * 1024, transcendentals=0
        ),
        name="convolve",
    )(skip, *operands, *blocks)


def on_device(signal, gate_one, mix_two, gate_two, skip_one, skip_two, spectrum_one, spectrum_two):
    n = lax.axis_size("ctx")
    peers = n // 2
    length, channels = signal.shape
    step = length // LANES
    count = channels // n
    per_device = count * step
    half_channels = channels // 2

    special_shape = (2, 2, step // 2, LANES, half_channels)
    special = pl.pallas_call(
        special_kernel,
        in_specs=[ANY] * 2,
        out_specs=VMEM,
        out_shape=jax.ShapeDtypeStruct(special_shape, BF16),
        scratch_shapes=[
            pltpu.VMEM((2, 2, length, half_channels), BF16),
            pltpu.VMEM((2, length, half_channels), F32),
            pltpu.SemaphoreType.DMA((2, 2)),
        ],
        compiler_params=PARAMS,
        name="special",
    )(spectrum_one, spectrum_two)
    special = lax.ppermute(special, "ctx", [(0, peers), (peers, 0)])

    data = pl.pallas_call(
        prep_kernel,
        out_shape=jax.ShapeDtypeStruct((n, 2 * per_device, LANES), BF16),
        scratch_shapes=[pltpu.VMEM((channels * step, LANES), F32)],
        compiler_params=PARAMS,
        name="prep",
    )(signal, gate_one, mix_two)
    data, special = lax.optimization_barrier((data, special))
    data = lax.all_to_all(data, "ctx", split_axis=0, concat_axis=0, tiled=True)

    block_shape = (count * 4 * step, LANES)

    def spread(index, spectrum):
        blocks = pl.pallas_call(
            functools.partial(pack_kernel, index),
            in_specs=[ANY, VMEM],
            out_specs=[VMEM] * peers,
            out_shape=[jax.ShapeDtypeStruct(block_shape, BF16)] * peers,
            scratch_shapes=[
                pltpu.VMEM((2, 2, length, half_channels), BF16),
                pltpu.VMEM((2, length, half_channels), F32),
                pltpu.VMEM((half_channels * 4 * step, LANES), F32),
                pltpu.SemaphoreType.DMA((2, 2)),
            ],
            compiler_params=PARAMS,
            name="pack",
        )(spectrum, special)
        return [
            block if s == 0 else lax.ppermute(block, "ctx", [(i, i ^ s) for i in range(n)])
            for s, block in enumerate(blocks)
        ]

    blocks_one = spread(0, spectrum_one)
    blocks_two = spread(1, spectrum_two)
    tables = {name: jnp.asarray(table) for name, table in make_tables(n, step).items()}
    sizes = (tables, n, step, count)
    middle = run_convolve(skip_one, data, blocks_one, True, *sizes)
    out = run_convolve(skip_two, middle, blocks_two, False, *sizes)
    back = lax.all_to_all(out, "ctx", split_axis=0, concat_axis=0, tiled=True)
    return pl.pallas_call(
        final_kernel,
        out_shape=jax.ShapeDtypeStruct((length, channels), BF16),
        scratch_shapes=[pltpu.VMEM((channels * step, LANES), F32)],
        compiler_params=SMALL,
        name="final",
    )(back, gate_two)


def solution(mesh):
    return jax.shard_map(
        on_device,
        mesh=mesh,
        in_specs=(
            P(("group", "ctx"), None),
            P(("group", "ctx"), None),
            P(("group", "ctx"), None),
            P(("group", "ctx"), None),
            P(),
            P(),
            P(None, "ctx", None, None),
            P(None, "ctx", None, None),
        ),
        out_specs=P(("group", "ctx"), None),
        check_vma=False,
    )
```

time: 102 us -> 94.2 us (0.924)
  waiting for transfers between devices: 29.6 us -> 15.1 us
  starting transfers between devices: 19.9 us -> 25.4 us
    ppermute x7 -> x14, waiting for transfers between devices: 25.2 us -> 10.7 us  [spread(): lax.ppermute(block, 'ctx', [(i, i ^ s) for i in range(n)])]
    ppermute x7 -> x14, starting transfers between devices: 9.7 us -> 15.2 us  [spread(): lax.ppermute(block, 'ctx', [(i, i ^ s) for i in range(n)])]
    pallas_call x1, Pallas kernels: 2.4 us -> 1.2 us  [on_device(): pl.pallas_call(final_kernel, out_shape=jax.ShapeDtypeStruct((length, chan...]
    pallas_call x3 -> x5, Pallas kernels: 26.5 us -> 27.3 us  [the longest x2 15.4 us: run_convolve(): pl.pallas_call(functools.partial(conv_kernel, peers, gated), in_specs=[pl...]
  transfers between devices with their start and end apart: 9 -> 16, of which waited for: 6 -> 6; matrix products, arithmetic and copies ran while one was open for 0% -> 0% of each run, Pallas kernels for 11% -> 22%
where the time goes in v3:
time: 94.2 us; the launch traced here: 93.6 us
  Pallas kernels  31.5 us (33%)
  starting transfers between devices  25.4 us (27%)
  blocking collectives  19.6 us (21%)
  waiting for transfers between devices  15.1 us (16%)
  local copies, waits for them, and re-layouts  1.69 us (2%)
    all_to_all x1, blocking collectives, on_device(): back = lax.all_to_all(out, 'ctx', split_axis=0, concat_axis=0, tiled=True)  19.6 us
    pallas_call x2, Pallas kernels, run_convolve(): pl.pallas_call(functools.partial(conv_kernel, peers, gated), in_specs=[pl...  15.4 us
    ppermute x14, starting transfers between devices, spread(): lax.ppermute(block, 'ctx', [(i, i ^ s) for i in range(n)])  15.2 us
    ppermute x14, waiting for transfers between devices, spread(): lax.ppermute(block, 'ctx', [(i, i ^ s) for i in range(n)])  10.7 us
    pallas_call x2, Pallas kernels, spread(): pl.pallas_call(functools.partial(pack_kernel, index), in_specs=[ANY, VMEM...  9.83 us
    ppermute x1, starting transfers between devices, on_device(): special = lax.ppermute(special, 'ctx', [(0, peers), (peers, 0)])  5.94 us
    ppermute x1, waiting for transfers between devices, on_device(): special = lax.ppermute(special, 'ctx', [(0, peers), (peers, 0)])  4.39 us
    all_to_all x1, starting transfers between devices, on_device(): data = lax.all_to_all(data, 'ctx', split_axis=0, concat_axis=0, tiled=True)  4.29 us
  transfers between devices with their start and end apart: 16, of which 6 were waited for; matrix products, arithmetic and copies ran while one was open for 0% of the time, Pallas kernels for 22%

profile of v3, /device:TPU:0, one launch (start us, length us, event | category | flops | bytes accessed | tf_op | source)
XLA Modules:
  0.0 93.6 jit_solution(11105436563113990390)
XLA Ops:
  0.0 2.2 %special.1 = bf16[2,2,4,128,128]{4,3,2,1,0:T(8,128)(2,1)} custom-call(bf16[2,2,1024,256]{3,2,1,0:T(8,128)(2,1)} %spec.2, bf16[2,2,1024,256]{3,2,1,0:T(8,128)(2,1)} %spec.3), custom_call_target="tpu_custom_call" | custom-call | tf_op jit(solution)/shard_map/special/pallas_call | solution.py:396
  2.2 5.9 %collective-permute-start = (bf16[2,2,4,128,128]{4,3,2,1,0:T(8,128)(2,1)}, bf16[2,2,4,128,128]{4,3,2,1,0:T(8,128)(2,1)S(1)}, u32[]{:S(2)}, u32[]{:S(2)}) collective-permute-start(bf16[2,2,4,128,128]{4,3,2,1,0:T(8,128)(2,1)} %special.1), channel_id=1, source_target_pairs={{0,8},{8,0},{16,24},{24,16}} | collective-permute-start | bytes 1572872 | tf_op jit(solution)/shard_map/ppermute | solution.py:409
  8.1 3.0 %prep.1 = bf16[16,256,128]{2,1,0:T(8,128)(2,1)} custom-call(bf16[1024,256]{1,0:T(8,128)(2,1)} %signal.1, bf16[1024,256]{1,0:T(8,128)(2,1)} %gate.2, bf16[1024,256]{1,0:T(8,128)(2,1)} %mix.1), custom_call_target="tpu_custom_call" | custom-call | tf_op jit(solution)/shard_map/prep/pallas_call | solution.py:411
  11.1 4.4 %collective-permute-done.special = bf16[2,2,4,128,128]{4,3,2,1,0:T(8,128)(2,1)S(1)} collective-permute-done((bf16[2,2,4,128,128]{4,3,2,1,0:T(8,128)(2,1)}, bf16[2,2,4,128,128]{4,3,2,1,0:T(8,128)(2,1)S(1)}, u32[]{:S(2)}, u32[]{:S(2)}) %collective-permute-start) | collective-permute-done | bytes 524320 | tf_op jit(solution)/shard_map/ppermute | solution.py:409
  15.5 4.3 %all-to-all-start = ((bf16[16,256,128]{2,1,0:T(8,128)(2,1)}), bf16[16,256,128]{2,1,0:T(8,128)(2,1)S(1)}, u32[]{:S(2)}, u32[]{:S(2)}) async-start(bf16[16,256,128]{2,1,0:T(8,128)(2,1)} %prep.1), calls=%async_computation | async-start | bytes 2097152 | tf_op jit(solution)/shard_map/all_to_all | solution.py:419
  19.8 4.9 %pack.2 = (bf16[512,128]{1,0:T(8,128)(2,1)}, bf16[512,128]{1,0:T(8,128)(2,1)}, bf16[512,128]{1,0:T(8,128)(2,1)}, bf16[512,128]{1,0:T(8,128)(2,1)}, bf16[512,128]...) custom-call(bf16[2,2,1024,256]{3,2,1,0:T(8,128)(2,1)} %spec.2, ...), custom_call_target="tpu_custom_call" | custom-call | tf_op jit(solution)/shard_map/pack/pallas_call | solution.py:424
  25.2 1.7 %collective-permute-start.2 = (bf16[512,128]{1,0:T(8,128)(2,1)}, bf16[512,128]{1,0:T(8,128)(2,1)S(1)}, u32[]{:S(2)}, u32[]{:S(2)}) collective-permute-start(bf16[512,128]{1,0:T(8,128)(2,1)} %get-tuple-element.27), channel_id=1, source_target_pairs={{0,2},{1,3},{2,0},{3,1},{4,6},{5,7},{6,4},{7,5},{8,10},{9,11},{10,... | collective-permute-start | bytes 393224 | tf_op jit(solution)/shard_map/ppermute | solution.py:439
  26.9 1.7 %collective-permute-start.4 = (bf16[512,128]{1,0:T(8,128)(2,1)}, bf16[512,128]{1,0:T(8,128)(2,1)S(1)}, u32[]{:S(2)}, u32[]{:S(2)}) collective-permute-start(bf16[512,128]{1,0:T(8,128)(2,1)} %get-tuple-element.29), channel_id=1, source_target_pairs={{0,4},{1,5},{2,6},{3,7},{4,0},{5,1},{6,2},{7,3},{8,12},{9,13},{10,... | collective-permute-start | bytes 393224 | tf_op jit(solution)/shard_map/ppermute | solution.py:439
  28.6 4.9 %pack.3 = (bf16[512,128]{1,0:T(8,128)(2,1)}, bf16[512,128]{1,0:T(8,128)(2,1)}, bf16[512,128]{1,0:T(8,128)(2,1)}, bf16[512,128]{1,0:T(8,128)(2,1)}, bf16[512,128]...) custom-call(bf16[2,2,1024,256]{3,2,1,0:T(8,128)(2,1)} %spec.3, ...), custom_call_target="tpu_custom_call" | custom-call | tf_op jit(solution)/shard_map/pack/pallas_call | solution.py:424
  33.7 2.6 %collective-permute-start.6 = (bf16[512,128]{1,0:T(8,128)(2,1)S(1)}, bf16[512,128]{1,0:T(8,128)(2,1)S(1)}, u32[]{:S(2)}, u32[]{:S(2)}) collective-permute-start(bf16[512,128]{1,0:T(8,128)(2,1)S(1)} %copy-done.18), channel_id=1, source_target_pairs={{0,6},{1,7},{2,4},{3,5},{4,2},{5,3},{6,0},{7,1},{8,14},{9,15},{10,... | collective-permute-start | bytes 393224 | tf_op jit(solution)/shard_map/ppermute | solution.py:439
  36.4 2.0 %collective-permute-done.3.refs_11_ = bf16[512,128]{1,0:T(8,128)(2,1)S(1)} collective-permute-done((bf16[512,128]{1,0:T(8,128)(2,1)}, bf16[512,128]{1,0:T(8,128)(2,1)S(1)}, u32[]{:S(2)}, u32[]{:S(2)}) %collective-permute-start.3) | collective-permute-done | bytes 131104 | tf_op jit(solution)/shard_map/ppermute | solution.py:439
  38.4 2.7 %collective-permute-done.4.refs_12_ = bf16[512,128]{1,0:T(8,128)(2,1)S(1)} collective-permute-done((bf16[512,128]{1,0:T(8,128)(2,1)}, bf16[512,128]{1,0:T(8,128)(2,1)S(1)}, u32[]{:S(2)}, u32[]{:S(2)}) %collective-permute-start.4) | collective-permute-done | bytes 131104 | tf_op jit(solution)/shard_map/ppermute | solution.py:439
  41.1 1.7 %collective-permute-start.9 = (bf16[512,128]{1,0:T(8,128)(2,1)}, bf16[512,128]{1,0:T(8,128)(2,1)S(1)}, u32[]{:S(2)}, u32[]{:S(2)}) collective-permute-start(bf16[512,128]{1,0:T(8,128)(2,1)} %get-tuple-element.35), channel_id=1, source_target_pairs={{0,2},{1,3},{2,0},{3,1},{4,6},{5,7},{6,4},{7,5},{8,10},{9,11},{10,... | collective-permute-start | bytes 393224 | tf_op jit(solution)/shard_map/ppermute | solution.py:439
  42.8 2.2 %collective-permute-done.5.refs_13_ = bf16[512,128]{1,0:T(8,128)(2,1)S(1)} collective-permute-done((bf16[512,128]{1,0:T(8,128)(2,1)S(1)}, bf16[512,128]{1,0:T(8,128)(2,1)S(1)}, u32[]{:S(2)}, u32[]{:S(2)}) %collective-permute-start.5) | collective-permute-done | bytes 131104 | tf_op jit(solution)/shard_map/ppermute | solution.py:439
  44.9 2.1 %collective-permute-start.10 = (bf16[512,128]{1,0:T(8,128)(2,1)}, bf16[512,128]{1,0:T(8,128)(2,1)S(1)}, u32[]{:S(2)}, u32[]{:S(2)}) collective-permute-start(bf16[512,128]{1,0:T(8,128)(2,1)} %get-tuple-element.36), channel_id=1, source_target_pairs={{0,3},{1,2},{2,1},{3,0},{4,7},{5,6},{6,5},{7,4},{8,11},{9,10},{10,... | collective-permute-start | bytes 393224 | tf_op jit(solution)/shard_map/ppermute | solution.py:439
  47.1 2.6 %collective-permute-done.6.refs_14_ = bf16[512,128]{1,0:T(8,128)(2,1)S(1)} collective-permute-done((bf16[512,128]{1,0:T(8,128)(2,1)S(1)}, bf16[512,128]{1,0:T(8,128)(2,1)S(1)}, u32[]{:S(2)}, u32[]{:S(2)}) %collective-permute-start.6) | collective-permute-done | bytes 131104 | tf_op jit(solution)/shard_map/ppermute | solution.py:439
  50.3 1.3 %collective-permute-done.7.refs_15_ = bf16[512,128]{1,0:T(8,128)(2,1)S(1)} collective-permute-done((bf16[512,128]{1,0:T(8,128)(2,1)S(1)}, bf16[512,128]{1,0:T(8,128)(2,1)S(1)}, u32[]{:S(2)}, u32[]{:S(2)}) %collective-permute-start.7) | collective-permute-done | bytes 131104 | tf_op jit(solution)/shard_map/ppermute | solution.py:439
  52.0 1.5 %collective-permute-start.13 = (bf16[512,128]{1,0:T(8,128)(2,1)}, bf16[512,128]{1,0:T(8,128)(2,1)S(1)}, u32[]{:S(2)}, u32[]{:S(2)}) collective-permute-start(bf16[512,128]{1,0:T(8,128)(2,1)} %get-tuple-element.39), channel_id=1, source_target_pairs={{0,6},{1,7},{2,4},{3,5},{4,2},{5,3},{6,0},{7,1},{8,14},{9,15},{10,... | collective-permute-start | bytes 393224 | tf_op jit(solution)/shard_map/ppermute | solution.py:439
  53.5 2.1 %collective-permute-start.14 = (bf16[512,128]{1,0:T(8,128)(2,1)}, bf16[512,128]{1,0:T(8,128)(2,1)S(1)}, u32[]{:S(2)}, u32[]{:S(2)}) collective-permute-start(bf16[512,128]{1,0:T(8,128)(2,1)} %get-tuple-element.40), channel_id=1, source_target_pairs={{0,7},{1,6},{2,5},{3,4},{4,3},{5,2},{6,1},{7,0},{8,15},{9,14},{10,... | collective-permute-start | bytes 393224 | tf_op jit(solution)/shard_map/ppermute | solution.py:439
  55.7 0.9 copy-done.1
  56.6 7.7 %convolve.2.refs_0_ = bf16[16,128,128]{2,1,0:T(8,128)(2,1)} custom-call(f32[256]{0:T(256)} %skip.2, bf16[16,256,128]{2,1,0:T(8,128)(2,1)} %copy-done.1, bf16[2,256,256]{2,1,0:T(8,128)(2,1)} %constant.14.clone.refs_1_, f32[2,2,128,128]{3,2,1,0:T(8,128)} %constant.16.clone.refs_2_, bf16[768,256]{1,0:T(8,128)(2,1)} %constant.17.clone.refs_3_, ...), custom_call_target="tpu_custom_call" | custom-call | flops 1200000000 | bytes 6291456 | tf_op jit(solution)/shard_map/convolve/pallas_call | solution.py:368
  65.1 7.7 %convolve.3 = bf16[16,128,128]{2,1,0:T(8,128)(2,1)} custom-call(f32[256]{0:T(256)} %skip.3, bf16[16,128,128]{2,1,0:T(8,128)(2,1)} %convolve.2.refs_0_, bf16[2,256,256]{2,1,0:T(8,128)(2,1)} %constant.14.clone.refs_1_, f32[2,2,128,128]{3,2,1,0:T(8,128)} %constant.16.clone.refs_2_, bf16[768,256]{1,0:T(8,128)(2,1)} %constant.17.clone.refs_3_, ...), custom_call_target="tpu_custom_call" | custom-call | flops 1200000000 | bytes 6291456 | tf_op jit(solution)/shard_map/convolve/pallas_call | solution.py:368
  72.8 19.6 %all_to_all.10.back = bf16[16,128,128]{2,1,0:T(8,128)(2,1)S(1)} all-to-all(bf16[16,128,128]{2,1,0:T(8,128)(2,1)} %convolve.3), channel_id=1, replica_groups=mesh['group'=2,'ctx'=16] {'ctx'}, dimensions={0} | all-to-all | bytes 1048576 | tf_op jit(solution)/shard_map/all_to_all | solution.py:449
  92.4 1.2 %final.1 = bf16[1024,256]{1,0:T(8,128)(2,1)} custom-call(bf16[16,128,128]{2,1,0:T(8,128)(2,1)S(1)} %all_to_all.10.back, bf16[1024,256]{1,0:T(8,128)(2,1)S(1)} %copy-done), custom_call_target="tpu_custom_call" | custom-call | tf_op jit(solution)/shard_map/final/pallas_call | solution.py:450
  (56 shorter events, 2.6 us)
Async XLA Ops:
  2.2 13.3 %collective-permute-start = (bf16[2,2,4,128,128]{4,3,2,1,0:T(8,128)(2,1)}, bf16[2,2,4,128,128]{4,3,2,1,0:T(8,128)(2,1)S(1)}, u32[]{:S(2)}, u32[]{:S(2)}) collective-permute-start(bf16[2,2,4,128,128]{4,3,2,1,0:T(8,128)(2,1)} %special.1), channel_id=1, source_target_pairs={{0,8},{8,0},{16,24},{24,16}} | collective-permute-start | bytes 1572872 | tf_op jit(solution)/shard_map/ppermute | solution.py:409
  15.5 40.1 %all-to-all-start = ((bf16[16,256,128]{2,1,0:T(8,128)(2,1)}), bf16[16,256,128]{2,1,0:T(8,128)(2,1)S(1)}, u32[]{:S(2)}, u32[]{:S(2)}) async-start(bf16[16,256,128]{2,1,0:T(8,128)(2,1)} %prep.1), calls=%async_computation | async-start | bytes 2097152 | tf_op jit(solution)/shard_map/all_to_all | solution.py:419
  24.7 11.6 %copy-start.17 = (bf16[512,128]{1,0:T(8,128)(2,1)S(1)}, bf16[512,128]{1,0:T(8,128)(2,1)}, u32[]{:S(2)}) copy-start(bf16[512,128]{1,0:T(8,128)(2,1)} %get-tuple-element.32) | copy-start | bytes 393220
  24.7 9.0 %collective-permute-start.1 = (bf16[512,128]{1,0:T(8,128)(2,1)}, bf16[512,128]{1,0:T(8,128)(2,1)S(1)}, u32[]{:S(2)}, u32[]{:S(2)}) collective-permute-start(bf16[512,128]{1,0:T(8,128)(2,1)} %get-tuple-element.26), channel_id=1, source_target_pairs={{0,1},{1,0},{2,3},{3,2},{4,5},{5,4},{6,7},{7,6},{8,9},{9,8},{10,11... | collective-permute-start | bytes 393224 | tf_op jit(solution)/shard_map/ppermute | solution.py:439
  25.2 11.1 %collective-permute-start.2 = (bf16[512,128]{1,0:T(8,128)(2,1)}, bf16[512,128]{1,0:T(8,128)(2,1)S(1)}, u32[]{:S(2)}, u32[]{:S(2)}) collective-permute-start(bf16[512,128]{1,0:T(8,128)(2,1)} %get-tuple-element.27), channel_id=1, source_target_pairs={{0,2},{1,3},{2,0},{3,1},{4,6},{5,7},{6,4},{7,5},{8,10},{9,11},{10,... | collective-permute-start | bytes 393224 | tf_op jit(solution)/shard_map/ppermute | solution.py:439
  26.9 11.5 %collective-permute-start.3 = (bf16[512,128]{1,0:T(8,128)(2,1)}, bf16[512,128]{1,0:T(8,128)(2,1)S(1)}, u32[]{:S(2)}, u32[]{:S(2)}) collective-permute-start(bf16[512,128]{1,0:T(8,128)(2,1)} %get-tuple-element.28), channel_id=1, source_target_pairs={{0,3},{1,2},{2,1},{3,0},{4,7},{5,6},{6,5},{7,4},{8,11},{9,10},{10,... | collective-permute-start | bytes 393224 | tf_op jit(solution)/shard_map/ppermute | solution.py:439
  26.9 14.2 %collective-permute-start.4 = (bf16[512,128]{1,0:T(8,128)(2,1)}, bf16[512,128]{1,0:T(8,128)(2,1)S(1)}, u32[]{:S(2)}, u32[]{:S(2)}) collective-permute-start(bf16[512,128]{1,0:T(8,128)(2,1)} %get-tuple-element.29), channel_id=1, source_target_pairs={{0,4},{1,5},{2,6},{3,7},{4,0},{5,1},{6,2},{7,3},{8,12},{9,13},{10,... | collective-permute-start | bytes 393224 | tf_op jit(solution)/shard_map/ppermute | solution.py:439
  33.5 11.4 %collective-permute-start.5 = (bf16[512,128]{1,0:T(8,128)(2,1)S(1)}, bf16[512,128]{1,0:T(8,128)(2,1)S(1)}, u32[]{:S(2)}, u32[]{:S(2)}) collective-permute-start(bf16[512,128]{1,0:T(8,128)(2,1)S(1)} %copy-done.19), channel_id=1, source_target_pairs={{0,5},{1,4},{2,7},{3,6},{4,1},{5,0},{6,3},{7,2},{8,13},{9,12},{10,... | collective-permute-start | bytes 393224 | tf_op jit(solution)/shard_map/ppermute | solution.py:439
  33.7 21.9 %copy-start.3 = (bf16[512,128]{1,0:T(8,128)(2,1)}, bf16[512,128]{1,0:T(8,128)(2,1)S(1)}, u32[]{:S(2)}) copy-start(bf16[512,128]{1,0:T(8,128)(2,1)S(1)} %collective-permute-done.1.refs_9_) | copy-start | bytes 393220
  33.7 16.0 %collective-permute-start.6 = (bf16[512,128]{1,0:T(8,128)(2,1)S(1)}, bf16[512,128]{1,0:T(8,128)(2,1)S(1)}, u32[]{:S(2)}, u32[]{:S(2)}) collective-permute-start(bf16[512,128]{1,0:T(8,128)(2,1)S(1)} %copy-done.18), channel_id=1, source_target_pairs={{0,6},{1,7},{2,4},{3,5},{4,2},{5,3},{6,0},{7,1},{8,14},{9,15},{10,... | collective-permute-start | bytes 393224 | tf_op jit(solution)/shard_map/ppermute | solution.py:439
  36.3 19.3 %copy-start.4 = (bf16[512,128]{1,0:T(8,128)(2,1)}, bf16[512,128]{1,0:T(8,128)(2,1)S(1)}, u32[]{:S(2)}) copy-start(bf16[512,128]{1,0:T(8,128)(2,1)S(1)} %collective-permute-done.2.refs_10_) | copy-start | bytes 393220
  36.4 15.2 %collective-permute-start.7 = (bf16[512,128]{1,0:T(8,128)(2,1)S(1)}, bf16[512,128]{1,0:T(8,128)(2,1)S(1)}, u32[]{:S(2)}, u32[]{:S(2)}) collective-permute-start(bf16[512,128]{1,0:T(8,128)(2,1)S(1)} %copy-done.17), channel_id=1, source_target_pairs={{0,7},{1,6},{2,5},{3,4},{4,3},{5,2},{6,1},{7,0},{8,15},{9,14},{10,... | collective-permute-start | bytes 393224 | tf_op jit(solution)/shard_map/ppermute | solution.py:439
  38.4 17.2 %copy-start.5 = (bf16[512,128]{1,0:T(8,128)(2,1)}, bf16[512,128]{1,0:T(8,128)(2,1)S(1)}, u32[]{:S(2)}) copy-start(bf16[512,128]{1,0:T(8,128)(2,1)S(1)} %collective-permute-done.3.refs_11_) | copy-start | bytes 393220
  38.4 13.6 %collective-permute-start.8 = (bf16[512,128]{1,0:T(8,128)(2,1)}, bf16[512,128]{1,0:T(8,128)(2,1)S(1)}, u32[]{:S(2)}, u32[]{:S(2)}) collective-permute-start(bf16[512,128]{1,0:T(8,128)(2,1)} %get-tuple-element.34), channel_id=1, source_target_pairs={{0,1},{1,0},{2,3},{3,2},{4,5},{5,4},{6,7},{7,6},{8,9},{9,8},{10,11... | collective-permute-start | bytes 393224 | tf_op jit(solution)/shard_map/ppermute | solution.py:439
  41.1 14.6 %copy-start.6 = (bf16[512,128]{1,0:T(8,128)(2,1)}, bf16[512,128]{1,0:T(8,128)(2,1)S(1)}, u32[]{:S(2)}) copy-start(bf16[512,128]{1,0:T(8,128)(2,1)S(1)} %collective-permute-done.4.refs_12_) | copy-start | bytes 393220
  41.1 12.4 %collective-permute-start.9 = (bf16[512,128]{1,0:T(8,128)(2,1)}, bf16[512,128]{1,0:T(8,128)(2,1)S(1)}, u32[]{:S(2)}, u32[]{:S(2)}) collective-permute-start(bf16[512,128]{1,0:T(8,128)(2,1)} %get-tuple-element.35), channel_id=1, source_target_pairs={{0,2},{1,3},{2,0},{3,1},{4,6},{5,7},{6,4},{7,5},{8,10},{9,11},{10,... | collective-permute-start | bytes 393224 | tf_op jit(solution)/shard_map/ppermute | solution.py:439
  44.9 19.3 %collective-permute-start.10 = (bf16[512,128]{1,0:T(8,128)(2,1)}, bf16[512,128]{1,0:T(8,128)(2,1)S(1)}, u32[]{:S(2)}, u32[]{:S(2)}) collective-permute-start(bf16[512,128]{1,0:T(8,128)(2,1)} %get-tuple-element.36), channel_id=1, source_target_pairs={{0,3},{1,2},{2,1},{3,0},{4,7},{5,6},{6,5},{7,4},{8,11},{9,10},{10,... | collective-permute-start | bytes 393224 | tf_op jit(solution)/shard_map/ppermute | solution.py:439
  49.7 14.6 %collective-permute-start.11 = (bf16[512,128]{1,0:T(8,128)(2,1)}, bf16[512,128]{1,0:T(8,128)(2,1)S(1)}, u32[]{:S(2)}, u32[]{:S(2)}) collective-permute-start(bf16[512,128]{1,0:T(8,128)(2,1)} %get-tuple-element.37), channel_id=1, source_target_pairs={{0,4},{1,5},{2,6},{3,7},{4,0},{5,1},{6,2},{7,3},{8,12},{9,13},{10,... | collective-permute-start | bytes 393224 | tf_op jit(solution)/shard_map/ppermute | solution.py:439
  51.5 12.8 %collective-permute-start.12 = (bf16[512,128]{1,0:T(8,128)(2,1)}, bf16[512,128]{1,0:T(8,128)(2,1)S(1)}, u32[]{:S(2)}, u32[]{:S(2)}) collective-permute-start(bf16[512,128]{1,0:T(8,128)(2,1)} %get-tuple-element.38), channel_id=1, source_target_pairs={{0,5},{1,4},{2,7},{3,6},{4,1},{5,0},{6,3},{7,2},{8,13},{9,12},{10,... | collective-permute-start | bytes 393224 | tf_op jit(solution)/shard_map/ppermute | solution.py:439
  52.0 12.4 %copy-start.7 = (bf16[512,128]{1,0:T(8,128)(2,1)}, bf16[512,128]{1,0:T(8,128)(2,1)S(1)}, u32[]{:S(2)}) copy-start(bf16[512,128]{1,0:T(8,128)(2,1)S(1)} %collective-permute-done.8.refs_9_) | copy-start | bytes 393220
  52.0 12.3 %collective-permute-start.13 = (bf16[512,128]{1,0:T(8,128)(2,1)}, bf16[512,128]{1,0:T(8,128)(2,1)S(1)}, u32[]{:S(2)}, u32[]{:S(2)}) collective-permute-start(bf16[512,128]{1,0:T(8,128)(2,1)} %get-tuple-element.39), channel_id=1, source_target_pairs={{0,6},{1,7},{2,4},{3,5},{4,2},{5,3},{6,0},{7,1},{8,14},{9,15},{10,... | collective-permute-start | bytes 393224 | tf_op jit(solution)/shard_map/ppermute | solution.py:439
  53.5 10.9 %copy-start.8 = (bf16[512,128]{1,0:T(8,128)(2,1)}, bf16[512,128]{1,0:T(8,128)(2,1)S(1)}, u32[]{:S(2)}) copy-start(bf16[512,128]{1,0:T(8,128)(2,1)S(1)} %collective-permute-done.9.refs_10_) | copy-start | bytes 393220
  53.5 10.9 %collective-permute-start.14 = (bf16[512,128]{1,0:T(8,128)(2,1)}, bf16[512,128]{1,0:T(8,128)(2,1)S(1)}, u32[]{:S(2)}, u32[]{:S(2)}) collective-permute-start(bf16[512,128]{1,0:T(8,128)(2,1)} %get-tuple-element.40), channel_id=1, source_target_pairs={{0,7},{1,6},{2,5},{3,4},{4,3},{5,2},{6,1},{7,0},{8,15},{9,14},{10,... | collective-permute-start | bytes 393224 | tf_op jit(solution)/shard_map/ppermute | solution.py:439
  65.1 27.3 %copy-start = (bf16[1024,256]{1,0:T(8,128)(2,1)S(1)}, bf16[1024,256]{1,0:T(8,128)(2,1)}, u32[]{:S(2)}) copy-start(bf16[1024,256]{1,0:T(8,128)(2,1)} %gate.3) | copy-start | bytes 1572868
  (12 other events, 47.4 us)

commit v4 on v3

--- a/solution.py
+++ b/solution.py
@@ -116,8 +116,22 @@
     return me, me // peers, lax.rem(me, peers), me == 0, me == peers
 
 
-def special_kernel(spec_one, spec_two, special, raw, strided, landed):
+def sent_blocks(peers, parity):
+    chips = [[s, s + 1] for s in range(2, peers // 2, 2)]
+    return [[0], [1]] + chips + [[s + parity] for s in range(peers // 2, peers, 2)]
+
+
+def held_blocks(peers, parity):
+    received = [offsets[0] for offsets in sent_blocks(peers, parity)]
+    beside = list(range(3, peers // 2, 2))
+    return received + beside + [s + 1 - parity for s in range(peers // 2, peers, 2)]
+
+
+def special_kernel(spec_one, spec_two, *refs):
+    *outs, raw, strided, turned, landed = refs
+    parity = lax.rem(lax.axis_index("group"), 2)
     step = spec_one.shape[2] // LANES
+    lines = step // 2
     width = raw.shape[3]
     _, half, _, is_first, _ = place()
     columns = pl.ds(pl.multiple_of((1 - half) * width, width), width)
@@ -132,13 +146,18 @@
         for ri in range(2):
             copies[2 * index + ri].wait()
             strided[ri] = raw[index, ri].astype(F32)
-        for j in range(step // 2):
+        for j in range(lines):
             pair = [strided[ri, pl.ds(j, LANES, stride=step), :] for ri in range(2)]
             if j == 0:
                 packed = pack_row(strided, pair[0], pair[1], step)
                 pair = [jnp.where(is_first, p, v) for p, v in zip(packed, pair)]
             for ri in range(2):
-                special[index, ri, j] = pair[ri].astype(BF16)
+                turned[index, pl.ds(ri * lines + j, width, stride=step), :] = pair[ri].T
+        size = outs[0].shape[2]
+        for i, out in enumerate(outs):
+            for core in range(2):
+                begin = pl.multiple_of((4 * i + 2 * parity + core) * size, size)
+                out[core, index] = turned[index, pl.ds(begin, size), :].astype(BF16)
 
 
 def pack_row(strided, real_part, imag_part, step):
@@ -151,48 +170,47 @@
     return packed_real, jnp.where(top, middle, packed_imag)
 
 
-def pack_kernel(index, spec, special, *refs):
+def pack_kernel(spec_one, spec_two, *refs):
     *outs, raw, strided, turned, landed = refs
-    peers = len(outs)
-    step = spec.shape[2] // LANES
-    channels = raw.shape[3]
+    peers = lax.axis_size("ctx") // 2
+    step = spec_one.shape[2] // LANES
+    channels = raw.shape[4]
     _, half, low_index, is_first, is_middle = place()
+    parity = lax.rem(lax.axis_index("group"), 2)
     row_count = 2 * step
     columns = pl.ds(pl.multiple_of(half * channels, channels), channels)
     copies = {
-        (a, ri): pltpu.make_async_copy(
-            spec.at[ri, a, :, columns], raw.at[a, ri], landed.at[a, ri]
-        )
-        for a in (1, 0)
+        (index, a, ri): pltpu.make_async_copy(
+            spec.at[ri, a, :, columns], raw.at[index, a, ri], landed.at[index, a, ri]
+        )
+        for index, spec in enumerate((spec_one, spec_two))
+        for a in range(2)
         for ri in range(2)
     }
     for copy in copies.values():
         copy.start()
-    for a in (1, 0):
-        for ri in range(2):
-            copies[a, ri].wait()
-            strided[ri] = raw[a, ri].astype(F32)
-        for low in range(step):
-            pair = [strided[ri, pl.ds(low, LANES, stride=step), :] for ri in range(2)]
-            if a == 0 and low == 0:
-                packed = pack_row(strided, pair[0], pair[1], step)
-                pair = [jnp.where(is_first, p, v) for p, v in zip(packed, pair)]
+    for index in range(2):
+        for a in range(2):
             for ri in range(2):
-                value = pair[ri]
-                if a == 0 and low < step // 2:
-                    other = special[index, ri, low].astype(F32)
-                    value = jnp.where(is_middle, other, value)
-                elif a == 0:
-                    j = low - step // 2
-                    own = strided[ri, pl.ds(j, LANES, stride=step), :]
-                    other = special[index, ri, j].astype(F32)
-                    value = jnp.where(is_first, other, jnp.where(is_middle, own, value))
-                row = ri * row_count + a * step + low
-                turned[pl.ds(row, channels, stride=2 * row_count), :] = value.T
-    block = channels // peers * 2 * row_count
-    for s, out in enumerate(outs):
-        start = pl.multiple_of((low_index ^ s) * block, block)
-        out[...] = turned[pl.ds(start, block), :].astype(BF16)
+                copies[index, a, ri].wait()
+                strided[ri] = raw[index, a, ri].astype(F32)
+            for low in range(step):
+                pair = [strided[ri, pl.ds(low, LANES, stride=step), :] for ri in range(2)]
+                if a == 0 and low == 0:
+                    packed = pack_row(strided, pair[0], pair[1], step)
+                    pair = [jnp.where(is_first, p, v) for p, v in zip(packed, pair)]
+                for ri in range(2):
+                    value = pair[ri]
+                    if a == 0 and low >= step // 2:
+                        own = strided[ri, pl.ds(low - step // 2, LANES, stride=step), :]
+                        value = jnp.where(is_middle, own, value)
+                    row = ri * row_count + a * step + low
+                    turned[pl.ds(row, channels, stride=2 * row_count), :] = value.T
+        block = channels // peers * 2 * row_count
+        for offsets, out in zip(sent_blocks(peers, parity), outs):
+            for i, s in enumerate(offsets):
+                start = pl.multiple_of((low_index ^ s) * block, block)
+                out[i, index] = turned[pl.ds(start, block), :].astype(BF16)
 
 
 def split_value(value):
@@ -214,28 +232,63 @@
     return jnp.dot(left, right, preferred_element_type=F32)
 
 
+def insert_rows(filters, lacking, half, step):
+    lines = step // 2
+    shape = (filters.shape[2] // (4 * step), 4 * step, LANES)
+    for index in range(2):
+        own = lacking[index].astype(F32)
+        size = own.shape[0]
+        before, after = pltpu.roll(own, lines, 0), pltpu.roll(own, size - lines, 0)
+        row = lax.rem(lax.broadcasted_iota(jnp.int32, own.shape, 0), step)
+        low = row < lines
+        chosen = (low == (half == 1)).reshape(-1, step, LANES)
+        real_part = jnp.where(low, own, before).reshape(-1, step, LANES)
+        imag_part = jnp.where(low, after, own).reshape(-1, step, LANES)
+        old = filters[0, index].astype(F32).reshape(shape)
+        new = jnp.concatenate(
+            [
+                jnp.where(chosen, real_part, old[:, :step]),
+                old[:, step : 2 * step],
+                jnp.where(chosen, imag_part, old[:, 2 * step : 3 * step]),
+                old[:, 3 * step :],
+            ],
+            axis=1,
+        )
+        filters[0, index] = new.reshape(filters.shape[2:]).astype(BF16)
+
+
 HALVED = ("forward_one", "turns", "inverse_one")
 PARTS = ("data", "forward_one", "turns", "forward_two", "forward_row")
 LATER = ("inverse_two", "inverse_row", "inverse_one")
 
 
-def conv_kernel(peers, gated, skip, *refs):
+def conv_kernel(peers, skip_one, skip_two, *refs):
     names = PARTS + LATER
     sources = dict(zip(names, refs))
     blocks, refs = refs[len(names) : len(names) + peers], refs[len(names) + peers :]
-    out, refs = refs[0], refs[1:]
+    specials, result, refs = refs[:2], refs[2], refs[3:]
     buffers = dict(zip(names, refs))
-    filters, landed = refs[len(names) :]
+    filters, lacking, out, landed, left = refs[len(names) :]
     me, half, low_index, _, _ = place()
     copies = {}
     for i, name in enumerate(names):
         source = sources[name].at[half] if name in HALVED else sources[name]
         copies[name] = pltpu.make_async_copy(source, buffers[name], landed.at[i])
-    for s in range(peers):
-        copies[s] = pltpu.make_async_copy(
-            blocks[s], filters.at[low_index ^ s], landed.at[len(names) + s]
-        )
-    for name in PARTS + tuple(range(peers)) + LATER:
+    parity = lax.rem(lax.axis_index("group"), 2)
+    for i, s in enumerate(held_blocks(peers, parity)):
+        copies[i] = pltpu.make_async_copy(
+            blocks[i].at[0], filters.at[low_index ^ s], landed.at[len(names) + i]
+        )
+    for name in PARTS:
+        copies[name].start()
+    for core, special in enumerate(specials):
+        copies["special"] = pltpu.make_async_copy(special, lacking, landed.at[len(names) + peers])
+
+        @pl.when(lax.rem(me, 2) == core)
+        def _():
+            copies["special"].start()
+
+    for name in tuple(range(peers)) + LATER:
         copies[name].start()
     awaited = set()
 
@@ -269,7 +322,7 @@
         tops = dot(split_columns(jnp.concatenate([v[:step] for v in values], axis=0)), buffers[row_table][...])
         return with_top([main[c * rows : (c + 1) * rows] for c in range(GROUP)], tops)
 
-    def convolve(fields, first):
+    def convolve(fields, layer, first):
         joined = jnp.concatenate(fields, axis=1)
         need("forward_one", "turns")
         cosine, sine = turns[0], turns[1]
@@ -288,10 +341,13 @@
                 )
             )
         spectral = second_stage(turned, "forward_two", "forward_row")
-        need(*range(peers))
+        if "special" not in awaited:
+            need("special", *range(peers))
+            insert_rows(filters, lacking, half, step)
         products = []
         for c in range(GROUP):
-            stored = filters[:, pl.ds(pl.multiple_of((first + c) * 2 * row_count, 2 * row_count), 2 * row_count), :]
+            start = (first + c) * 2 * row_count
+            stored = filters[:, layer, start : start + 2 * row_count, :]
             h_real = stored[:, :row_count].reshape(rows, LANES).astype(F32)
             h_imag = stored[:, row_count:].reshape(rows, LANES).astype(F32)
             x_real, x_imag = spectral[c][:, :LANES], spectral[c][:, LANES:]
@@ -324,6 +380,7 @@
 
     need("data")
     size = GROUP * step
+    writes = []
     for first in range(0, count, GROUP):
 
         def channels(start):
@@ -333,13 +390,24 @@
             ]
 
         base = first * step
+        place_of = me * count + first
         fields = channels(base)
-        results = convolve([f.astype(BF16) for f in fields], first)
-        results = [skip[me * count + first + c] * fields[c] + results[c] for c in range(GROUP)]
-        if gated:
-            results = [g * r for g, r in zip(channels(per_device + base), results)]
-        results = [r.reshape(devices, step, LANES) for r in results]
+        results = convolve([f.astype(BF16) for f in fields], 0, first)
+        middles = [
+            (g * (r + skip_one[place_of + c] * f)).astype(BF16)
+            for c, (g, r, f) in enumerate(zip(channels(per_device + base), results, fields))
+        ]
+        results = convolve(middles, 1, first)
+        results = [
+            (r + skip_two[place_of + c] * m.astype(F32)).reshape(devices, step, LANES)
+            for c, (r, m) in enumerate(zip(results, middles))
+        ]
         out[:, base : base + size, :] = jnp.concatenate(results, axis=1).astype(BF16)
+        part = (slice(None), pl.ds(base, size))
+        writes.append(pltpu.make_async_copy(out.at[part], result.at[part], left.at[len(writes)]))
+        writes[-1].start()
+    for write in writes:
+        write.wait()
 
 
 def final_kernel(back, gate, out, turned):
@@ -356,57 +424,45 @@
 VMEM = pl.BlockSpec(memory_space=pltpu.VMEM)
 
 
-def run_convolve(skip, values, blocks, gated, tables, n, step, count):
+def run_convolve(skips, data, blocks, specials, tables, n, step, count):
     peers = n // 2
     per_device = count * step
-    operands = dict(tables, data=values)
+    operands = dict(tables, data=data)
     operands = [operands[name] for name in PARTS + LATER]
     buffers = [
         pltpu.VMEM(o.shape[1:] if name in HALVED else o.shape, o.dtype)
         for name, o in zip(PARTS + LATER, operands)
     ]
     return pl.pallas_call(
-        functools.partial(conv_kernel, peers, gated),
-        in_specs=[pl.BlockSpec(memory_space=pltpu.SMEM)] + [ANY] * (len(operands) + peers),
-        out_specs=VMEM,
+        functools.partial(conv_kernel, peers),
+        in_specs=[pl.BlockSpec(memory_space=pltpu.SMEM)] * 2 + [ANY] * (len(operands) + peers + 2),
+        out_specs=ANY,
         out_shape=jax.ShapeDtypeStruct((n, per_device, LANES), BF16),
         scratch_shapes=buffers
         + [
-            pltpu.VMEM((peers,) + blocks[0].shape, BF16),
-            pltpu.SemaphoreType.DMA((len(operands) + peers,)),
+            pltpu.VMEM((peers,) + blocks[0].shape[1:], BF16),
+            pltpu.VMEM(specials[0].shape, BF16),
+            pltpu.VMEM((n, per_device, LANES), BF16),
+            pltpu.SemaphoreType.DMA((len(operands) + peers + 1,)),
+            pltpu.SemaphoreType.DMA((count // GROUP,)),
         ],
         compiler_params=PARAMS,
         cost_estimate=pl.CostEstimate(
-            flops=1200 * 1000 * 1000, bytes_accessed=6 * 1024 * 1024, transcendentals=0
+            flops=2400 * 1000 * 1000, bytes_accessed=8 * 1024 * 1024, transcendentals=0
         ),
         name="convolve",
-    )(skip, *operands, *blocks)
+    )(*skips, *operands, *blocks, *specials)
 
 
 def on_device(signal, gate_one, mix_two, gate_two, skip_one, skip_two, spectrum_one, spectrum_two):
     n = lax.axis_size("ctx")
+    groups = lax.axis_size("group")
     peers = n // 2
     length, channels = signal.shape
     step = length // LANES
     count = channels // n
     per_device = count * step
     half_channels = channels // 2
-
-    special_shape = (2, 2, step // 2, LANES, half_channels)
-    special = pl.pallas_call(
-        special_kernel,
-        in_specs=[ANY] * 2,
-        out_specs=VMEM,
-        out_shape=jax.ShapeDtypeStruct(special_shape, BF16),
-        scratch_shapes=[
-            pltpu.VMEM((2, 2, length, half_channels), BF16),
-            pltpu.VMEM((2, length, half_channels), F32),
-            pltpu.SemaphoreType.DMA((2, 2)),
-        ],
-        compiler_params=PARAMS,
-        name="special",
-    )(spectrum_one, spectrum_two)
-    special = lax.ppermute(special, "ctx", [(0, peers), (peers, 0)])
 
     data = pl.pallas_call(
         prep_kernel,
@@ -415,37 +471,75 @@
         compiler_params=PARAMS,
         name="prep",
     )(signal, gate_one, mix_two)
-    data, special = lax.optimization_barrier((data, special))
+
+    both = ("group", "ctx")
+    block_shape = (2, count * 4 * step, LANES)
+    shapes = [(len(offsets),) + block_shape for offsets in sent_blocks(peers, 0)]
+    blocks = pl.pallas_call(
+        pack_kernel,
+        in_specs=[ANY, ANY],
+        out_specs=[VMEM] * len(shapes),
+        out_shape=[jax.ShapeDtypeStruct(shape, BF16) for shape in shapes],
+        scratch_shapes=[
+            pltpu.VMEM((2, 2, 2, length, half_channels), BF16),
+            pltpu.VMEM((2, length, half_channels), F32),
+            pltpu.VMEM((half_channels * 4 * step, LANES), F32),
+            pltpu.SemaphoreType.DMA((2, 2, 2)),
+        ],
+        compiler_params=PARAMS,
+        name="pack",
+    )(spectrum_one, spectrum_two)
+    routes = [[offsets[0] for offsets in sent_blocks(peers, g % 2)] for g in range(groups)]
+    received = [
+        lax.ppermute(
+            block, both, [(g * n + d, g * n + (d ^ routes[g][i])) for g in range(groups) for d in range(n)]
+        )
+        if i
+        else block
+        for i, block in enumerate(blocks)
+    ]
+    mates = [(d, d ^ 1) for d in range(n)]
+    swap = [(g, g ^ 1) for g in range(groups)]
+    far = 1 + peers // 4
+    passed = [lax.ppermute(block, "group", swap) for block in received[far:]]
+    beside = [lax.ppermute(block[1:], "ctx", mates) for block in received[2:far]]
+
+    lacked = pl.pallas_call(
+        special_kernel,
+        in_specs=[ANY] * 2,
+        out_specs=[VMEM] * (peers // 4),
+        out_shape=[jax.ShapeDtypeStruct((2, 2, per_device, LANES), BF16)] * (peers // 4),
+        scratch_shapes=[
+            pltpu.VMEM((2, 2, length, half_channels), BF16),
+            pltpu.VMEM((2, length, half_channels), F32),
+            pltpu.VMEM((2, half_channels * step, LANES), F32),
+            pltpu.SemaphoreType.DMA((2, 2)),
+        ],
+        compiler_params=PARAMS,
+        name="special",
+    )(spectrum_one, spectrum_two)
+    lacked = [
+        lax.ppermute(
+            rows,
+            both,
+            [
+                (g * n + peers - end, g * n + end + 4 * i + 2 * (g % 2))
+                for g in range(groups)
+                for end in (0, peers)
+            ],
+        )
+        for i, rows in enumerate(lacked)
+    ]
+    lacked = sum(lacked[1:], lacked[0])
+    others = lax.ppermute(lacked, "group", swap)
+    others, passed[0] = lax.optimization_barrier((others, passed[0]))
+    lacked = lacked + others
+    mine = (lacked[0], lax.ppermute(lacked[1], "ctx", [(d, d + 1) for d in range(0, n, 2)]))
     data = lax.all_to_all(data, "ctx", split_axis=0, concat_axis=0, tiled=True)
-
-    block_shape = (count * 4 * step, LANES)
-
-    def spread(index, spectrum):
-        blocks = pl.pallas_call(
-            functools.partial(pack_kernel, index),
-            in_specs=[ANY, VMEM],
-            out_specs=[VMEM] * peers,
-            out_shape=[jax.ShapeDtypeStruct(block_shape, BF16)] * peers,
-            scratch_shapes=[
-                pltpu.VMEM((2, 2, length, half_channels), BF16),
-                pltpu.VMEM((2, length, half_channels), F32),
-                pltpu.VMEM((half_channels * 4 * step, LANES), F32),
-                pltpu.SemaphoreType.DMA((2, 2)),
-            ],
-            compiler_params=PARAMS,
-            name="pack",
-        )(spectrum, special)
-        return [
-            block if s == 0 else lax.ppermute(block, "ctx", [(i, i ^ s) for i in range(n)])
-            for s, block in enumerate(blocks)
-        ]
-
-    blocks_one = spread(0, spectrum_one)
-    blocks_two = spread(1, spectrum_two)
+    held = received + beside + passed
     tables = {name: jnp.asarray(table) for name, table in make_tables(n, step).items()}
-    sizes = (tables, n, step, count)
-    middle = run_convolve(skip_one, data, blocks_one, True, *sizes)
-    out = run_convolve(skip_two, middle, blocks_two, False, *sizes)
+    skips = (skip_one, skip_two)
+    out = run_convolve(skips, data, held, mine, tables, n, step, count)
     back = lax.all_to_all(out, "ctx", split_axis=0, concat_axis=0, tiled=True)
     return pl.pallas_call(
         final_kernel,

time: 94.2 us -> 86.9 us (0.923)
  Pallas kernels: 31.5 us -> 24.2 us
  waiting for transfers between devices: 15.1 us -> 18.2 us
  starting transfers between devices: 25.4 us -> 22.6 us
    pallas_call x5 -> x3, Pallas kernels: 27.3 us -> 20 us  [the longest x1 11.8 us: run_convolve(): pl.pallas_call(functools.partial(conv_kernel, peers), in_specs=[pl.BlockS...]
    ppermute x15 -> x11, starting transfers between devices: 21.2 us -> 15.2 us  [the longest x2 5.57 us: on_device(): lax.ppermute(rows, both, [(g * n + peers - end, g * n + end + 4 * i + 2 *...]
    ppermute x15 -> x11, waiting for transfers between devices: 15.1 us -> 18.2 us  [the longest x4 9.86 us: on_device(): lax.ppermute(block, both, [(g * n + d, g * n + (d ^ routes[g][i])) for g...]
    all_to_all x1, starting transfers between devices: 4.29 us -> 7.39 us  [on_device(): data = lax.all_to_all(data, 'ctx', split_axis=0, concat_axis=0, tiled=True)]
  transfers between devices with their start and end apart: 16 -> 12, of which waited for: 6 -> 6; matrix products, arithmetic and copies ran while one was open for 0% -> 1% of each run, Pallas kernels for 22% -> 10%
where the time goes in v4:
time: 86.9 us; the launch traced here: 86.4 us
  Pallas kernels  24.2 us (28%)
  starting transfers between devices  22.6 us (26%)
  blocking collectives  19.3 us (22%)
  waiting for transfers between devices  18.2 us (21%)
  local copies, waits for them, and re-layouts  1.88 us (2%)
    all_to_all x1, blocking collectives, on_device(): back = lax.all_to_all(out, 'ctx', split_axis=0, concat_axis=0, tiled=True)  19.3 us
    pallas_call x1, Pallas kernels, run_convolve(): pl.pallas_call(functools.partial(conv_kernel, peers), in_specs=[pl.BlockS...  11.8 us
    ppermute x4, waiting for transfers between devices, on_device(): lax.ppermute(block, both, [(g * n + d, g * n + (d ^ routes[g][i])) for g...  9.86 us
    all_to_all x1, starting transfers between devices, on_device(): data = lax.all_to_all(data, 'ctx', split_axis=0, concat_axis=0, tiled=True)  7.39 us
    pallas_call x1, Pallas kernels, on_device(): pl.pallas_call(pack_kernel, in_specs=[ANY, ANY], out_specs=[VMEM] * len(s...  5.95 us
    ppermute x2, starting transfers between devices, on_device(): lax.ppermute(rows, both, [(g * n + peers - end, g * n + end + 4 * i + 2 *...  5.57 us
    ppermute x1, waiting for transfers between devices, on_device(): others = lax.ppermute(lacked, 'group', swap)  4.4 us
    ppermute x4, starting transfers between devices, on_device(): lax.ppermute(block, both, [(g * n + d, g * n + (d ^ routes[g][i])) for g...  3.52 us
  transfers between devices with their start and end apart: 12, of which 6 were waited for; matrix products, arithmetic and copies ran while one was open for 1% of the time, Pallas kernels for 10%

profile of v4, /device:TPU:0, one launch (start us, length us, event | category | flops | bytes accessed | tf_op | source)
XLA Modules:
  0.0 86.4 jit_solution(4679346742491465149)
XLA Ops:
  0.0 3.0 %prep.1 = bf16[16,256,128]{2,1,0:T(8,128)(2,1)} custom-call(bf16[1024,256]{1,0:T(8,128)(2,1)} %signal.1, bf16[1024,256]{1,0:T(8,128)(2,1)} %gate.2, bf16[1024,256]{1,0:T(8,128)(2,1)} %mix.1), custom_call_target="tpu_custom_call" | custom-call | tf_op jit(solution)/shard_map/prep/pallas_call | solution.py:467
  3.0 7.4 %all-to-all-start = ((bf16[16,256,128]{2,1,0:T(8,128)(2,1)}), bf16[16,256,128]{2,1,0:T(8,128)(2,1)S(1)}, u32[]{:S(2)}, u32[]{:S(2)}) async-start(bf16[16,256,128]{2,1,0:T(8,128)(2,1)} %prep.1), calls=%async_computation | async-start | bytes 2097152 | tf_op jit(solution)/shard_map/all_to_all | solution.py:538
  10.4 6.0 %pack.1 = (bf16[1,2,512,128]{3,2,1,0:T(8,128)(2,1)}, bf16[1,2,512,128]{3,2,1,0:T(8,128)(2,1)}, bf16[2,2,512,128]{3,2,1,0:T(8,128)(2,1)}, bf16[1,2,512,128]{3,2,1,0:T(8,128)(2,1)}, bf16[1,2,512,128]{3,2,1,0:T(8,128)(2,1)}) custom-call(bf16[2,2,1024,256]{3,2,1,0:T(8,128)(2,1)} %spec_one.3, bf16[2,2,1024,256]{3,2,1,0:T(8,128)(2,1)} %spec_two.3), custom_call_target="tpu_custom_call" | custom-call | tf_op jit(solution)/shard_map/pack/pallas_call | solution.py:478
  16.4 2.0 %collective-permute-start.2 = (bf16[1,2,512,128]{3,2,1,0:T(8,128)(2,1)}, bf16[1,2,512,128]{3,2,1,0:T(8,128)(2,1)S(1)}, u32[]{:S(2)}, u32[]{:S(2)}) collective-permute-start(bf16[1,2,512,128]{3,2,1,0:T(8,128)(2,1)} %get-tuple-element.17), channel_id=1, source_target_pairs={{0,4},{1,5},{2,6},{3,7},{4,0},{5,1},{6,2},{7,3},{8,12},{9,13},{10,... | collective-permute-start | bytes 786440 | tf_op jit(solution)/shard_map/ppermute | solution.py:494
  18.3 1.5 %collective-permute-start.1 = (bf16[2,2,512,128]{3,2,1,0:T(8,128)(2,1)}, bf16[2,2,512,128]{3,2,1,0:T(8,128)(2,1)S(1)}, u32[]{:S(2)}, u32[]{:S(2)}) collective-permute-start(bf16[2,2,512,128]{3,2,1,0:T(8,128)(2,1)} %get-tuple-element.16), channel_id=1, source_target_pairs={{0,2},{1,3},{2,0},{3,1},{4,6},{5,7},{6,4},{7,5},{8,10},{9,11},{10,... | collective-permute-start | bytes 1572872 | tf_op jit(solution)/shard_map/ppermute | solution.py:494
  19.8 2.3 %special.1 = (bf16[2,2,128,128]{3,2,1,0:T(8,128)(2,1)}, bf16[2,2,128,128]{3,2,1,0:T(8,128)(2,1)}) custom-call(bf16[2,2,1024,256]{3,2,1,0:T(8,128)(2,1)} %spec_one.3, bf16[2,2,1024,256]{3,2,1,0:T(8,128)(2,1)} %spec_two.3), custom_call_target="tpu_custom_call" | custom-call | tf_op jit(solution)/shard_map/special/pallas_call | solution.py:507
  22.1 4.3 %collective-permute-start.5 = (bf16[2,2,128,128]{3,2,1,0:T(8,128)(2,1)}, bf16[2,2,128,128]{3,2,1,0:T(8,128)(2,1)S(1)}, u32[]{:S(2)}, u32[]{:S(2)}) collective-permute-start(bf16[2,2,128,128]{3,2,1,0:T(8,128)(2,1)} %get-tuple-element.19), channel_id=1, source_target_pairs={{8,0},{0,8},{24,18},{16,26}} | collective-permute-start | bytes 393224 | tf_op jit(solution)/shard_map/ppermute | solution.py:522
  26.4 1.3 %collective-permute-start.6 = (bf16[2,2,128,128]{3,2,1,0:T(8,128)(2,1)}, bf16[2,2,128,128]{3,2,1,0:T(8,128)(2,1)S(1)}, u32[]{:S(2)}, u32[]{:S(2)}) collective-permute-start(bf16[2,2,128,128]{3,2,1,0:T(8,128)(2,1)} %get-tuple-element.20), channel_id=1, source_target_pairs={{8,4},{0,12},{24,22},{16,30}} | collective-permute-start | bytes 393224 | tf_op jit(solution)/shard_map/ppermute | solution.py:522
  27.8 8.7 %collective-permute-done.2.refs_11_ = bf16[1,2,512,128]{3,2,1,0:T(8,128)(2,1)S(1)} collective-permute-done((bf16[1,2,512,128]{3,2,1,0:T(8,128)(2,1)}, bf16[1,2,512,128]{3,2,1,0:T(8,128)(2,1)S(1)}, u32[]{:S(2)}, u32[]{:S(2)}) %collective-permute-start.2) | collective-permute-done | bytes 262176 | tf_op jit(solution)/shard_map/ppermute | solution.py:494
  36.5 0.5 collective-permute-start.8
  37.0 1.5 %collective-permute-done.5 = bf16[2,2,128,128]{3,2,1,0:T(8,128)(2,1)S(1)} collective-permute-done((bf16[2,2,128,128]{3,2,1,0:T(8,128)(2,1)}, bf16[2,2,128,128]{3,2,1,0:T(8,128)(2,1)S(1)}, u32[]{:S(2)}, u32[]{:S(2)}) %collective-permute-start.5) | collective-permute-done | bytes 131104 | tf_op jit(solution)/shard_map/ppermute | solution.py:522
  38.5 1.4 %collective-permute-done.6 = bf16[2,2,128,128]{3,2,1,0:T(8,128)(2,1)S(1)} collective-permute-done((bf16[2,2,128,128]{3,2,1,0:T(8,128)(2,1)}, bf16[2,2,128,128]{3,2,1,0:T(8,128)(2,1)S(1)}, u32[]{:S(2)}, u32[]{:S(2)}) %collective-permute-start.6) | collective-permute-done | bytes 131104 | tf_op jit(solution)/shard_map/ppermute | solution.py:522
  40.0 1.6 %collective-permute-start.7 = (bf16[2,2,128,128]{3,2,1,0:T(8,128)(2,1)S(1)}, bf16[2,2,128,128]{3,2,1,0:T(8,128)(2,1)S(1)}, u32[]{:S(2)}, u32[]{:S(2)}) collective-permute-start(bf16[2,2,128,128]{3,2,1,0:T(8,128)(2,1)S(1)} %add.6), channel_id=1, source_target_pairs={{0,16},{16,0},{1,17},{17,1},{2,18},{18,2},{3,19},{19,3},{4,20},{20... | collective-permute-start | bytes 393224 | tf_op jit(solution)/shard_map/ppermute | solution.py:534
  41.5 1.1 %collective-permute-done.3.refs_12_ = bf16[1,2,512,128]{3,2,1,0:T(8,128)(2,1)S(1)} collective-permute-done((bf16[1,2,512,128]{3,2,1,0:T(8,128)(2,1)S(1)}, bf16[1,2,512,128]{3,2,1,0:T(8,128)(2,1)S(1)}, u32[]{:S(2)}, u32[]{:S(2)}) %collective-permute-start.3) | collective-permute-done | bytes 262176 | tf_op jit(solution)/shard_map/ppermute | solution.py:494
  42.6 1.5 %collective-permute-start.9 = (bf16[1,2,512,128]{3,2,1,0:T(8,128)(2,1)S(1)}, bf16[1,2,512,128]{3,2,1,0:T(8,128)(2,1)S(1)}, u32[]{:S(2)}, u32[]{:S(2)}) collective-permute-start(bf16[1,2,512,128]{3,2,1,0:T(8,128)(2,1)S(1)} %collective-permute-done.3.refs_12_), channel_id=1, source_target_pairs={{0,16},{16,0},{1,17},{17,1},{2,18},{18,2},{3,19},{19,3},{4,20},{20... | collective-permute-start | bytes 786440 | tf_op jit(solution)/shard_map/ppermute | solution.py:504
  44.1 4.4 %collective-permute-done.7 = bf16[2,2,128,128]{3,2,1,0:T(8,128)(2,1)S(1)} collective-permute-done((bf16[2,2,128,128]{3,2,1,0:T(8,128)(2,1)S(1)}, bf16[2,2,128,128]{3,2,1,0:T(8,128)(2,1)S(1)}, u32[]{:S(2)}, u32[]{:S(2)}) %collective-permute-start.7) | collective-permute-done | bytes 131104 | tf_op jit(solution)/shard_map/ppermute | solution.py:534
  48.7 0.7 slice_bitcast_fusion
  49.4 2.5 %collective-permute-start.10 = (bf16[2,128,128]{2,1,0:T(8,128)(2,1)S(1)}, bf16[2,128,128]{2,1,0:T(8,128)(2,1)S(1)}, u32[]{:S(2)}, u32[]{:S(2)}) collective-permute-start(bf16[2,128,128]{2,1,0:T(8,128)(2,1)S(1)} %get-tuple-element.23), channel_id=1, source_target_pairs={{0,1},{2,3},{4,5},{6,7},{8,9},{10,11},{12,13},{14,15},{16,17},{18,... | collective-permute-start | bytes 196616 | tf_op jit(solution)/shard_map/ppermute | solution.py:537
  51.9 1.1 %collective-permute-done.9.refs_15_ = bf16[1,2,512,128]{3,2,1,0:T(8,128)(2,1)S(1)} collective-permute-done((bf16[1,2,512,128]{3,2,1,0:T(8,128)(2,1)S(1)}, bf16[1,2,512,128]{3,2,1,0:T(8,128)(2,1)S(1)}, u32[]{:S(2)}, u32[]{:S(2)}) %collective-permute-start.9) | collective-permute-done | bytes 262176 | tf_op jit(solution)/shard_map/ppermute | solution.py:504
  53.1 0.6 copy-done.8
  53.8 0.4 copy-done.1
  54.2 11.8 %convolve.1 = bf16[16,128,128]{2,1,0:T(8,128)(2,1)} custom-call(f32[256]{0:T(256)} %skip_one.1, f32[256]{0:T(256)} %skip_two.1, bf16[16,256,128]{2,1,0:T(8,128)(2,1)} %copy-done.1, bf16[2,256,256]{2,1,0:T(8,128)(2,1)} %constant.14.clone.refs_1_, f32[2,2,128,128]{3,2,1,0:T(8,128)} %constant.16.clone.refs_2_, bf16[768,256]{1,0:T(8,128)(2,1)} %constant.17.clone.refs_3_, ...), custom_call_target="tpu_custom_call" | custom-call | flops 2400000000 | bytes 8388608 | tf_op jit(solution)/shard_map/convolve/pallas_call | solution.py:436
  66.0 19.3 %all_to_all.10.back = bf16[16,128,128]{2,1,0:T(8,128)(2,1)S(1)} all-to-all(bf16[16,128,128]{2,1,0:T(8,128)(2,1)} %convolve.1), channel_id=1, replica_groups=mesh['group'=2,'ctx'=16] {'ctx'}, dimensions={0} | all-to-all | bytes 1048576 | tf_op jit(solution)/shard_map/all_to_all | solution.py:543
  85.2 1.2 %final.1 = bf16[1024,256]{1,0:T(8,128)(2,1)} custom-call(bf16[16,128,128]{2,1,0:T(8,128)(2,1)S(1)} %all_to_all.10.back, bf16[1024,256]{1,0:T(8,128)(2,1)S(1)} %copy-done), custom_call_target="tpu_custom_call" | custom-call | tf_op jit(solution)/shard_map/final/pallas_call | solution.py:544
  (34 shorter events, 0.4 us)
Async XLA Ops:
  3.0 50.0 %all-to-all-start = ((bf16[16,256,128]{2,1,0:T(8,128)(2,1)}), bf16[16,256,128]{2,1,0:T(8,128)(2,1)S(1)}, u32[]{:S(2)}, u32[]{:S(2)}) async-start(bf16[16,256,128]{2,1,0:T(8,128)(2,1)} %prep.1), calls=%async_computation | async-start | bytes 2097152 | tf_op jit(solution)/shard_map/all_to_all | solution.py:538
  16.4 20.2 %collective-permute-start.2 = (bf16[1,2,512,128]{3,2,1,0:T(8,128)(2,1)}, bf16[1,2,512,128]{3,2,1,0:T(8,128)(2,1)S(1)}, u32[]{:S(2)}, u32[]{:S(2)}) collective-permute-start(bf16[1,2,512,128]{3,2,1,0:T(8,128)(2,1)} %get-tuple-element.17), channel_id=1, source_target_pairs={{0,4},{1,5},{2,6},{3,7},{4,0},{5,1},{6,2},{7,3},{8,12},{9,13},{10,... | collective-permute-start | bytes 786440 | tf_op jit(solution)/shard_map/ppermute | solution.py:494
  18.3 9.3 %copy-start.9 = (bf16[1,2,512,128]{3,2,1,0:T(8,128)(2,1)S(1)}, bf16[1,2,512,128]{3,2,1,0:T(8,128)(2,1)}, u32[]{:S(2)}) copy-start(bf16[1,2,512,128]{3,2,1,0:T(8,128)(2,1)} %get-tuple-element.18) | copy-start | bytes 786436
  18.3 23.2 %copy-start.6 = (bf16[1,2,512,128]{3,2,1,0:T(8,128)(2,1)S(1)}, bf16[1,2,512,128]{3,2,1,0:T(8,128)(2,1)}, u32[]{:S(2)}) copy-start(bf16[1,2,512,128]{3,2,1,0:T(8,128)(2,1)} %get-tuple-element.15) | copy-start | bytes 786436
  18.3 30.2 %collective-permute-start.1 = (bf16[2,2,512,128]{3,2,1,0:T(8,128)(2,1)}, bf16[2,2,512,128]{3,2,1,0:T(8,128)(2,1)S(1)}, u32[]{:S(2)}, u32[]{:S(2)}) collective-permute-start(bf16[2,2,512,128]{3,2,1,0:T(8,128)(2,1)} %get-tuple-element.16), channel_id=1, source_target_pairs={{0,2},{1,3},{2,0},{3,1},{4,6},{5,7},{6,4},{7,5},{8,10},{9,11},{10,... | collective-permute-start | bytes 1572872 | tf_op jit(solution)/shard_map/ppermute | solution.py:494
  22.1 16.4 %collective-permute-start.5 = (bf16[2,2,128,128]{3,2,1,0:T(8,128)(2,1)}, bf16[2,2,128,128]{3,2,1,0:T(8,128)(2,1)S(1)}, u32[]{:S(2)}, u32[]{:S(2)}) collective-permute-start(bf16[2,2,128,128]{3,2,1,0:T(8,128)(2,1)} %get-tuple-element.19), channel_id=1, source_target_pairs={{8,0},{0,8},{24,18},{16,26}} | collective-permute-start | bytes 393224 | tf_op jit(solution)/shard_map/ppermute | solution.py:522
  26.4 13.5 %collective-permute-start.6 = (bf16[2,2,128,128]{3,2,1,0:T(8,128)(2,1)}, bf16[2,2,128,128]{3,2,1,0:T(8,128)(2,1)S(1)}, u32[]{:S(2)}, u32[]{:S(2)}) collective-permute-start(bf16[2,2,128,128]{3,2,1,0:T(8,128)(2,1)} %get-tuple-element.20), channel_id=1, source_target_pairs={{8,4},{0,12},{24,22},{16,30}} | collective-permute-start | bytes 393224 | tf_op jit(solution)/shard_map/ppermute | solution.py:522
  27.7 14.9 %collective-permute-start.3 = (bf16[1,2,512,128]{3,2,1,0:T(8,128)(2,1)S(1)}, bf16[1,2,512,128]{3,2,1,0:T(8,128)(2,1)S(1)}, u32[]{:S(2)}, u32[]{:S(2)}) collective-permute-start(bf16[1,2,512,128]{3,2,1,0:T(8,128)(2,1)S(1)} %copy-done.9), channel_id=1, source_target_pairs={{0,6},{1,7},{2,4},{3,5},{4,2},{5,3},{6,0},{7,1},{8,14},{9,15},{10,... | collective-permute-start | bytes 786440 | tf_op jit(solution)/shard_map/ppermute | solution.py:494
  36.5 16.5 %copy-start.3 = (bf16[1,2,512,128]{3,2,1,0:T(8,128)(2,1)}, bf16[1,2,512,128]{3,2,1,0:T(8,128)(2,1)S(1)}, u32[]{:S(2)}) copy-start(bf16[1,2,512,128]{3,2,1,0:T(8,128)(2,1)S(1)} %collective-permute-done.2.refs_11_) | copy-start | bytes 786436
  36.5 12.0 %collective-permute-start.8 = (bf16[1,2,512,128]{3,2,1,0:T(8,128)(2,1)S(1)}, bf16[1,2,512,128]{3,2,1,0:T(8,128)(2,1)S(1)}, u32[]{:S(2)}, u32[]{:S(2)}) collective-permute-start(bf16[1,2,512,128]{3,2,1,0:T(8,128)(2,1)S(1)} %collective-permute-done.2.refs_11_), channel_id=1, source_target_pairs={{0,16},{16,0},{1,17},{17,1},{2,18},{18,2},{3,19},{19,3},{4,20},{20... | collective-permute-start | bytes 786440 | tf_op jit(solution)/shard_map/ppermute | solution.py:504
  40.0 8.6 %collective-permute-start.7 = (bf16[2,2,128,128]{3,2,1,0:T(8,128)(2,1)S(1)}, bf16[2,2,128,128]{3,2,1,0:T(8,128)(2,1)S(1)}, u32[]{:S(2)}, u32[]{:S(2)}) collective-permute-start(bf16[2,2,128,128]{3,2,1,0:T(8,128)(2,1)S(1)} %add.6), channel_id=1, source_target_pairs={{0,16},{16,0},{1,17},{17,1},{2,18},{18,2},{3,19},{19,3},{4,20},{20... | collective-permute-start | bytes 393224 | tf_op jit(solution)/shard_map/ppermute | solution.py:534
  41.5 10.4 %collective-permute-start = (bf16[1,2,512,128]{3,2,1,0:T(8,128)(2,1)S(1)}, bf16[1,2,512,128]{3,2,1,0:T(8,128)(2,1)S(1)}, u32[]{:S(2)}, u32[]{:S(2)}) collective-permute-start(bf16[1,2,512,128]{3,2,1,0:T(8,128)(2,1)S(1)} %copy-done.6), channel_id=1, source_target_pairs={{0,1},{1,0},{2,3},{3,2},{4,5},{5,4},{6,7},{7,6},{8,9},{9,8},{10,11... | collective-permute-start | bytes 786440 | tf_op jit(solution)/shard_map/ppermute | solution.py:494
  42.6 10.4 %copy-start.4 = (bf16[1,2,512,128]{3,2,1,0:T(8,128)(2,1)}, bf16[1,2,512,128]{3,2,1,0:T(8,128)(2,1)S(1)}, u32[]{:S(2)}) copy-start(bf16[1,2,512,128]{3,2,1,0:T(8,128)(2,1)S(1)} %collective-permute-done.3.refs_12_) | copy-start | bytes 786436
  42.6 10.3 %collective-permute-start.9 = (bf16[1,2,512,128]{3,2,1,0:T(8,128)(2,1)S(1)}, bf16[1,2,512,128]{3,2,1,0:T(8,128)(2,1)S(1)}, u32[]{:S(2)}, u32[]{:S(2)}) collective-permute-start(bf16[1,2,512,128]{3,2,1,0:T(8,128)(2,1)S(1)} %collective-permute-done.3.refs_12_), channel_id=1, source_target_pairs={{0,16},{16,0},{1,17},{17,1},{2,18},{18,2},{3,19},{19,3},{4,20},{20... | collective-permute-start | bytes 786440 | tf_op jit(solution)/shard_map/ppermute | solution.py:504
  48.5 4.5 %copy-start.5 = (bf16[1,2,512,128]{3,2,1,0:T(8,128)(2,1)}, bf16[1,2,512,128]{3,2,1,0:T(8,128)(2,1)S(1)}, u32[]{:S(2)}) copy-start(bf16[1,2,512,128]{3,2,1,0:T(8,128)(2,1)S(1)} %collective-permute-done.8.refs_14_) | copy-start | bytes 786436
  48.6 4.5 %copy-start.2 = (bf16[2,2,512,128]{3,2,1,0:T(8,128)(2,1)}, bf16[2,2,512,128]{3,2,1,0:T(8,128)(2,1)S(1)}, u32[]{:S(2)}) copy-start(bf16[2,2,512,128]{3,2,1,0:T(8,128)(2,1)S(1)} %collective-permute-done.1.refs_10_) | copy-start | bytes 1572868
  48.6 4.4 %collective-permute-start.4 = (bf16[1,2,512,128]{3,2,1,0:T(8,128)(2,1)S(1)}, bf16[1,2,512,128]{3,2,1,0:T(8,128)(2,1)S(1)}, u32[]{:S(2)}, u32[]{:S(2)}) collective-permute-start(bf16[1,2,512,128]{3,2,1,0:T(8,128)(2,1)S(1)} %slice.12), channel_id=1, source_target_pairs={{0,1},{1,0},{2,3},{3,2},{4,5},{5,4},{6,7},{7,6},{8,9},{9,8},{10,11... | collective-permute-start | bytes 786440 | tf_op jit(solution)/shard_map/ppermute | solution.py:505
  49.4 3.6 %collective-permute-start.10 = (bf16[2,128,128]{2,1,0:T(8,128)(2,1)S(1)}, bf16[2,128,128]{2,1,0:T(8,128)(2,1)S(1)}, u32[]{:S(2)}, u32[]{:S(2)}) collective-permute-start(bf16[2,128,128]{2,1,0:T(8,128)(2,1)S(1)} %get-tuple-element.23), channel_id=1, source_target_pairs={{0,1},{2,3},{4,5},{6,7},{8,9},{10,11},{12,13},{14,15},{16,17},{18,... | collective-permute-start | bytes 196616 | tf_op jit(solution)/shard_map/ppermute | solution.py:537
  51.9 1.1 %copy-start.7 = (bf16[1,2,512,128]{3,2,1,0:T(8,128)(2,1)}, bf16[1,2,512,128]{3,2,1,0:T(8,128)(2,1)S(1)}, u32[]{:S(2)}) copy-start(bf16[1,2,512,128]{3,2,1,0:T(8,128)(2,1)S(1)} %collective-permute-done.refs_9_) | copy-start | bytes 786436
  53.0 0.7 copy-start.8
  53.0 0.7 copy-start.11
  53.0 0.8 copy-start.10
  53.0 1.2 %copy-start.1 = (bf16[16,256,128]{2,1,0:T(8,128)(2,1)}, bf16[16,256,128]{2,1,0:T(8,128)(2,1)S(1)}, u32[]{:S(2)}) copy-start(bf16[16,256,128]{2,1,0:T(8,128)(2,1)S(1)} %all-to-all-done.refs_0_) | copy-start | bytes 3145732
  54.2 31.1 %copy-start = (bf16[1024,256]{1,0:T(8,128)(2,1)S(1)}, bf16[1024,256]{1,0:T(8,128)(2,1)}, u32[]{:S(2)}) copy-start(bf16[1024,256]{1,0:T(8,128)(2,1)} %gate.3) | copy-start | bytes 1572868

commit v5 on v4

--- a/solution.py
+++ b/solution.py
@@ -91,22 +91,33 @@
     }
 
 
-def prep_kernel(signal, gate, mix, data, turned):
-    step = signal.shape[0] // LANES
-    channels = signal.shape[1]
-    devices = data.shape[0]
+def prep_kernel(signal, gate, mix, result, raw, turned, data, landed, left):
+    step = raw.shape[1] // LANES
+    channels = raw.shape[2]
     rows = data.shape[1] // 2
+    copies = [
+        pltpu.make_async_copy(source, raw.at[i], landed.at[i])
+        for i, source in enumerate((signal, gate, mix))
+    ]
+    for copy in copies:
+        copy.start()
+    writes = []
     for part in range(2):
+        for copy in copies[1:] if part else copies[:1]:
+            copy.wait()
         for t in range(step):
             piece = pl.ds(t * LANES, LANES)
             if part == 0:
-                value = signal[piece, :].astype(F32)
+                value = raw[0, piece, :].astype(F32)
             else:
-                value = gate[piece, :].astype(F32) * mix[piece, :].astype(F32)
+                value = raw[1, piece, :].astype(F32) * raw[2, piece, :].astype(F32)
             turned[pl.ds(t, channels, stride=step), :] = value.T
-        data[:, part * rows : (part + 1) * rows, :] = (
-            turned[...].reshape(devices, rows, LANES).astype(BF16)
-        )
+        half = (slice(None), pl.ds(part * rows, rows))
+        data[half] = turned[: channels * step].reshape(data.shape[0], rows, LANES).astype(BF16)
+        writes.append(pltpu.make_async_copy(data.at[half], result.at[half], left.at[part]))
+        writes[part].start()
+    for write in writes:
+        write.wait()
 
 
 def place():
@@ -145,7 +156,7 @@
     for index in range(2):
         for ri in range(2):
             copies[2 * index + ri].wait()
-            strided[ri] = raw[index, ri].astype(F32)
+            strided[ri, : raw.shape[2]] = raw[index, ri].astype(F32)
         for j in range(lines):
             pair = [strided[ri, pl.ds(j, LANES, stride=step), :] for ri in range(2)]
             if j == 0:
@@ -193,7 +204,7 @@
         for a in range(2):
             for ri in range(2):
                 copies[index, a, ri].wait()
-                strided[ri] = raw[index, a, ri].astype(F32)
+                strided[ri, : raw.shape[3]] = raw[index, a, ri].astype(F32)
             for low in range(step):
                 pair = [strided[ri, pl.ds(low, LANES, stride=step), :] for ri in range(2)]
                 if a == 0 and low == 0:
@@ -413,7 +424,7 @@
 def final_kernel(back, gate, out, turned):
     step = gate.shape[0] // LANES
     channels = gate.shape[1]
-    turned[...] = back[...].astype(F32).reshape(channels * step, LANES)
+    turned[: channels * step] = back[...].astype(F32).reshape(channels * step, LANES)
     for t in range(step):
         piece = pl.ds(t * LANES, LANES)
         value = turned[pl.ds(t, channels, stride=step), :].T
@@ -464,10 +475,19 @@
     per_device = count * step
     half_channels = channels // 2
 
+    data_shape = (n, 2 * per_device, LANES)
     data = pl.pallas_call(
         prep_kernel,
-        out_shape=jax.ShapeDtypeStruct((n, 2 * per_device, LANES), BF16),
-        scratch_shapes=[pltpu.VMEM((channels * step, LANES), F32)],
+        in_specs=[ANY] * 3,
+        out_specs=ANY,
+        out_shape=jax.ShapeDtypeStruct(data_shape, BF16),
+        scratch_shapes=[
+            pltpu.VMEM((3, length, channels), BF16),
+            pltpu.VMEM(((channels + 1) * step, LANES), F32),
+            pltpu.VMEM(data_shape, BF16),
+            pltpu.SemaphoreType.DMA((3,)),
+            pltpu.SemaphoreType.DMA((2,)),
+        ],
         compiler_params=PARAMS,
         name="prep",
     )(signal, gate_one, mix_two)
@@ -482,8 +502,8 @@
         out_shape=[jax.ShapeDtypeStruct(shape, BF16) for shape in shapes],
         scratch_shapes=[
             pltpu.VMEM((2, 2, 2, length, half_channels), BF16),
-            pltpu.VMEM((2, length, half_channels), F32),
-            pltpu.VMEM((half_channels * 4 * step, LANES), F32),
+            pltpu.VMEM((2, length + step, half_channels), F32),
+            pltpu.VMEM(((half_channels + 1) * 4 * step, LANES), F32),
             pltpu.SemaphoreType.DMA((2, 2, 2)),
         ],
         compiler_params=PARAMS,
@@ -511,8 +531,8 @@
         out_shape=[jax.ShapeDtypeStruct((2, 2, per_device, LANES), BF16)] * (peers // 4),
         scratch_shapes=[
             pltpu.VMEM((2, 2, length, half_channels), BF16),
-            pltpu.VMEM((2, length, half_channels), F32),
-            pltpu.VMEM((2, half_channels * step, LANES), F32),
+            pltpu.VMEM((2, length + step, half_channels), F32),
+            pltpu.VMEM((2, (half_channels + 1) * step, LANES), F32),
             pltpu.SemaphoreType.DMA((2, 2)),
         ],
         compiler_params=PARAMS,
@@ -531,7 +551,8 @@
         for i, rows in enumerate(lacked)
     ]
     lacked = sum(lacked[1:], lacked[0])
-    others = lax.ppermute(lacked, "group", swap)
+    holders = [(g, d) for g in range(groups) for d in range(0, n, 2) if d // 2 % 2 == g % 2]
+    others = lax.ppermute(lacked, both, [(g * n + d, (g ^ 1) * n + d) for g, d in holders])
     others, passed[0] = lax.optimization_barrier((others, passed[0]))
     lacked = lacked + others
     mine = (lacked[0], lax.ppermute(lacked[1], "ctx", [(d, d + 1) for d in range(0, n, 2)]))
@@ -544,7 +565,7 @@
     return pl.pallas_call(
         final_kernel,
         out_shape=jax.ShapeDtypeStruct((length, channels), BF16),
-        scratch_shapes=[pltpu.VMEM((channels * step, LANES), F32)],
+        scratch_shapes=[pltpu.VMEM(((channels + 1) * step, LANES), F32)],
         compiler_params=SMALL,
         name="final",
     )(back, gate_two)

time: 86.9 us -> 86.6 us (level)
  waiting for transfers between devices: 18.2 us -> 16.3 us
  starting transfers between devices: 22.6 us -> 23.7 us
    ppermute x1, starting transfers between devices: 1.56 us -> 3.41 us  [on_device(): lax.ppermute(lacked, both, [(g * n + d, (g ^ 1) * n + d) for g, d in hold...]
    ppermute x1, waiting for transfers between devices: 4.4 us -> 3.12 us  [on_device(): lax.ppermute(lacked, both, [(g * n + d, (g ^ 1) * n + d) for g, d in hold...]
    ppermute x4, waiting for transfers between devices: 9.86 us -> 8.74 us  [on_device(): lax.ppermute(block, both, [(g * n + d, g * n + (d ^ routes[g][i])) for g...]
  transfers between devices with their start and end apart: 12 -> 12, of which waited for: 6 -> 5; matrix products, arithmetic and copies ran while one was open for 1% -> 1% of each run, Pallas kernels for 10% -> 10%
where the time goes in v5:
time: 86.6 us; the launch traced here: 86.2 us
  Pallas kernels  23.8 us (27%)
  starting transfers between devices  23.7 us (27%)
  blocking collectives  20.1 us (23%)
  waiting for transfers between devices  16.3 us (19%)
  local copies, waits for them, and re-layouts  1.88 us (2%)
    all_to_all x1, blocking collectives, on_device(): back = lax.all_to_all(out, 'ctx', split_axis=0, concat_axis=0, tiled=True)  20.1 us
    pallas_call x1, Pallas kernels, run_convolve(): pl.pallas_call(functools.partial(conv_kernel, peers), in_specs=[pl.BlockS...  11.8 us
    ppermute x4, waiting for transfers between devices, on_device(): lax.ppermute(block, both, [(g * n + d, g * n + (d ^ routes[g][i])) for g...  8.74 us
    all_to_all x1, starting transfers between devices, on_device(): data = lax.all_to_all(data, 'ctx', split_axis=0, concat_axis=0, tiled=True)  7.4 us
    pallas_call x1, Pallas kernels, on_device(): pl.pallas_call(pack_kernel, in_specs=[ANY, ANY], out_specs=[VMEM] * len(s...  5.95 us
    ppermute x2, starting transfers between devices, on_device(): lax.ppermute(rows, both, [(g * n + peers - end, g * n + end + 4 * i + 2 *...  5.57 us
    ppermute x4, starting transfers between devices, on_device(): lax.ppermute(block, both, [(g * n + d, g * n + (d ^ routes[g][i])) for g...  3.59 us
    ppermute x1, starting transfers between devices, on_device(): lax.ppermute(lacked, both, [(g * n + d, (g ^ 1) * n + d) for g, d in hold...  3.41 us
  transfers between devices with their start and end apart: 12, of which 5 were waited for; matrix products, arithmetic and copies ran while one was open for 1% of the time, Pallas kernels for 10%

profile of v5, /device:TPU:0, one launch (start us, length us, event | category | flops | bytes accessed | tf_op | source)
XLA Modules:
  0.0 86.2 jit_solution(6820421365707726543)
XLA Ops:
  0.0 2.6 %prep.1 = bf16[16,256,128]{2,1,0:T(8,128)(2,1)} custom-call(bf16[1024,256]{1,0:T(8,128)(2,1)} %signal.1, bf16[1024,256]{1,0:T(8,128)(2,1)} %gate.2, bf16[1024,256]{1,0:T(8,128)(2,1)} %mix.1), custom_call_target="tpu_custom_call" | custom-call | tf_op jit(solution)/shard_map/prep/pallas_call | solution.py:479
  2.6 7.4 %all-to-all-start = ((bf16[16,256,128]{2,1,0:T(8,128)(2,1)}), bf16[16,256,128]{2,1,0:T(8,128)(2,1)S(1)}, u32[]{:S(2)}, u32[]{:S(2)}) async-start(bf16[16,256,128]{2,1,0:T(8,128)(2,1)} %prep.1), calls=%async_computation | async-start | bytes 2097152 | tf_op jit(solution)/shard_map/all_to_all | solution.py:559
  10.0 6.0 %pack.1 = (bf16[1,2,512,128]{3,2,1,0:T(8,128)(2,1)}, bf16[1,2,512,128]{3,2,1,0:T(8,128)(2,1)}, bf16[2,2,512,128]{3,2,1,0:T(8,128)(2,1)}, bf16[1,2,512,128]{3,2,1,0:T(8,128)(2,1)}, bf16[1,2,512,128]{3,2,1,0:T(8,128)(2,1)}) custom-call(bf16[2,2,1024,256]{3,2,1,0:T(8,128)(2,1)} %spec_one.3, bf16[2,2,1024,256]{3,2,1,0:T(8,128)(2,1)} %spec_two.3), custom_call_target="tpu_custom_call" | custom-call | tf_op jit(solution)/shard_map/pack/pallas_call | solution.py:498
  16.0 2.0 %collective-permute-start.2 = (bf16[1,2,512,128]{3,2,1,0:T(8,128)(2,1)}, bf16[1,2,512,128]{3,2,1,0:T(8,128)(2,1)S(1)}, u32[]{:S(2)}, u32[]{:S(2)}) collective-permute-start(bf16[1,2,512,128]{3,2,1,0:T(8,128)(2,1)} %get-tuple-element.17), channel_id=1, source_target_pairs={{0,4},{1,5},{2,6},{3,7},{4,0},{5,1},{6,2},{7,3},{8,12},{9,13},{10,... | collective-permute-start | bytes 786440 | tf_op jit(solution)/shard_map/ppermute | solution.py:514
  18.0 1.5 %collective-permute-start.1 = (bf16[2,2,512,128]{3,2,1,0:T(8,128)(2,1)}, bf16[2,2,512,128]{3,2,1,0:T(8,128)(2,1)S(1)}, u32[]{:S(2)}, u32[]{:S(2)}) collective-permute-start(bf16[2,2,512,128]{3,2,1,0:T(8,128)(2,1)} %get-tuple-element.16), channel_id=1, source_target_pairs={{0,2},{1,3},{2,0},{3,1},{4,6},{5,7},{6,4},{7,5},{8,10},{9,11},{10,... | collective-permute-start | bytes 1572872 | tf_op jit(solution)/shard_map/ppermute | solution.py:514
  19.5 2.3 %special.1 = (bf16[2,2,128,128]{3,2,1,0:T(8,128)(2,1)}, bf16[2,2,128,128]{3,2,1,0:T(8,128)(2,1)}) custom-call(bf16[2,2,1024,256]{3,2,1,0:T(8,128)(2,1)} %spec_one.3, bf16[2,2,1024,256]{3,2,1,0:T(8,128)(2,1)} %spec_two.3), custom_call_target="tpu_custom_call" | custom-call | tf_op jit(solution)/shard_map/special/pallas_call | solution.py:527
  21.8 4.3 %collective-permute-start.5 = (bf16[2,2,128,128]{3,2,1,0:T(8,128)(2,1)}, bf16[2,2,128,128]{3,2,1,0:T(8,128)(2,1)S(1)}, u32[]{:S(2)}, u32[]{:S(2)}) collective-permute-start(bf16[2,2,128,128]{3,2,1,0:T(8,128)(2,1)} %get-tuple-element.19), channel_id=1, source_target_pairs={{8,0},{0,8},{24,18},{16,26}} | collective-permute-start | bytes 393224 | tf_op jit(solution)/shard_map/ppermute | solution.py:542
  26.0 1.3 %collective-permute-start.6 = (bf16[2,2,128,128]{3,2,1,0:T(8,128)(2,1)}, bf16[2,2,128,128]{3,2,1,0:T(8,128)(2,1)S(1)}, u32[]{:S(2)}, u32[]{:S(2)}) collective-permute-start(bf16[2,2,128,128]{3,2,1,0:T(8,128)(2,1)} %get-tuple-element.20), channel_id=1, source_target_pairs={{8,4},{0,12},{24,22},{16,30}} | collective-permute-start | bytes 393224 | tf_op jit(solution)/shard_map/ppermute | solution.py:542
  27.4 8.7 %collective-permute-done.2.refs_11_ = bf16[1,2,512,128]{3,2,1,0:T(8,128)(2,1)S(1)} collective-permute-done((bf16[1,2,512,128]{3,2,1,0:T(8,128)(2,1)}, bf16[1,2,512,128]{3,2,1,0:T(8,128)(2,1)S(1)}, u32[]{:S(2)}, u32[]{:S(2)}) %collective-permute-start.2) | collective-permute-done | bytes 262176 | tf_op jit(solution)/shard_map/ppermute | solution.py:514
  36.2 0.5 collective-permute-start.8
  36.7 1.5 %collective-permute-done.5 = bf16[2,2,128,128]{3,2,1,0:T(8,128)(2,1)S(1)} collective-permute-done((bf16[2,2,128,128]{3,2,1,0:T(8,128)(2,1)}, bf16[2,2,128,128]{3,2,1,0:T(8,128)(2,1)S(1)}, u32[]{:S(2)}, u32[]{:S(2)}) %collective-permute-start.5) | collective-permute-done | bytes 131104 | tf_op jit(solution)/shard_map/ppermute | solution.py:542
  38.2 1.4 %collective-permute-done.6 = bf16[2,2,128,128]{3,2,1,0:T(8,128)(2,1)S(1)} collective-permute-done((bf16[2,2,128,128]{3,2,1,0:T(8,128)(2,1)}, bf16[2,2,128,128]{3,2,1,0:T(8,128)(2,1)S(1)}, u32[]{:S(2)}, u32[]{:S(2)}) %collective-permute-start.6) | collective-permute-done | bytes 131104 | tf_op jit(solution)/shard_map/ppermute | solution.py:542
  39.6 3.4 %collective-permute-start.7 = (bf16[2,2,128,128]{3,2,1,0:T(8,128)(2,1)S(1)}, bf16[2,2,128,128]{3,2,1,0:T(8,128)(2,1)S(1)}, u32[]{:S(2)}, u32[]{:S(2)}) collective-permute-start(bf16[2,2,128,128]{3,2,1,0:T(8,128)(2,1)S(1)} %add.6), channel_id=1, source_target_pairs={{0,16},{4,20},{8,24},{12,28},{18,2},{22,6},{26,10},{30,14}} | collective-permute-start | bytes 393224 | tf_op jit(solution)/shard_map/ppermute | solution.py:555
  43.1 0.6 collective-permute-start.9
  43.8 3.1 %collective-permute-done.7 = bf16[2,2,128,128]{3,2,1,0:T(8,128)(2,1)S(1)} collective-permute-done((bf16[2,2,128,128]{3,2,1,0:T(8,128)(2,1)S(1)}, bf16[2,2,128,128]{3,2,1,0:T(8,128)(2,1)S(1)}, u32[]{:S(2)}, u32[]{:S(2)}) %collective-permute-start.7) | collective-permute-done | bytes 131104 | tf_op jit(solution)/shard_map/ppermute | solution.py:555
  47.1 0.7 slice_bitcast_fusion
  47.8 2.5 %collective-permute-start.10 = (bf16[2,128,128]{2,1,0:T(8,128)(2,1)S(1)}, bf16[2,128,128]{2,1,0:T(8,128)(2,1)S(1)}, u32[]{:S(2)}, u32[]{:S(2)}) collective-permute-start(bf16[2,128,128]{2,1,0:T(8,128)(2,1)S(1)} %get-tuple-element.23), channel_id=1, source_target_pairs={{0,1},{2,3},{4,5},{6,7},{8,9},{10,11},{12,13},{14,15},{16,17},{18,... | collective-permute-start | bytes 196616 | tf_op jit(solution)/shard_map/ppermute | solution.py:558
  50.3 1.6 %collective-permute-done.9.refs_15_ = bf16[1,2,512,128]{3,2,1,0:T(8,128)(2,1)S(1)} collective-permute-done((bf16[1,2,512,128]{3,2,1,0:T(8,128)(2,1)S(1)}, bf16[1,2,512,128]{3,2,1,0:T(8,128)(2,1)S(1)}, u32[]{:S(2)}, u32[]{:S(2)}) %collective-permute-start.9) | collective-permute-done | bytes 262176 | tf_op jit(solution)/shard_map/ppermute | solution.py:524
  51.9 0.6 copy-done.8
  52.6 0.1 copy-done.10
  52.7 0.4 copy-done.1
  53.0 11.8 %convolve.1 = bf16[16,128,128]{2,1,0:T(8,128)(2,1)} custom-call(f32[256]{0:T(256)} %skip_one.1, f32[256]{0:T(256)} %skip_two.1, bf16[16,256,128]{2,1,0:T(8,128)(2,1)} %copy-done.1, bf16[2,256,256]{2,1,0:T(8,128)(2,1)} %constant.14.clone.refs_1_, f32[2,2,128,128]{3,2,1,0:T(8,128)} %constant.16.clone.refs_2_, bf16[768,256]{1,0:T(8,128)(2,1)} %constant.17.clone.refs_3_, ...), custom_call_target="tpu_custom_call" | custom-call | flops 2400000000 | bytes 8388608 | tf_op jit(solution)/shard_map/convolve/pallas_call | solution.py:447
  64.8 20.1 %all_to_all.10.back = bf16[16,128,128]{2,1,0:T(8,128)(2,1)S(1)} all-to-all(bf16[16,128,128]{2,1,0:T(8,128)(2,1)} %convolve.1), channel_id=1, replica_groups=mesh['group'=2,'ctx'=16] {'ctx'}, dimensions={0} | all-to-all | bytes 1048576 | tf_op jit(solution)/shard_map/all_to_all | solution.py:564
  84.9 1.2 %final.1 = bf16[1024,256]{1,0:T(8,128)(2,1)} custom-call(bf16[16,128,128]{2,1,0:T(8,128)(2,1)S(1)} %all_to_all.10.back, bf16[1024,256]{1,0:T(8,128)(2,1)S(1)} %copy-done), custom_call_target="tpu_custom_call" | custom-call | tf_op jit(solution)/shard_map/final/pallas_call | solution.py:565
  (34 shorter events, 0.4 us)
Async XLA Ops:
  2.6 49.2 %all-to-all-start = ((bf16[16,256,128]{2,1,0:T(8,128)(2,1)}), bf16[16,256,128]{2,1,0:T(8,128)(2,1)S(1)}, u32[]{:S(2)}, u32[]{:S(2)}) async-start(bf16[16,256,128]{2,1,0:T(8,128)(2,1)} %prep.1), calls=%async_computation | async-start | bytes 2097152 | tf_op jit(solution)/shard_map/all_to_all | solution.py:559
  16.0 20.2 %collective-permute-start.2 = (bf16[1,2,512,128]{3,2,1,0:T(8,128)(2,1)}, bf16[1,2,512,128]{3,2,1,0:T(8,128)(2,1)S(1)}, u32[]{:S(2)}, u32[]{:S(2)}) collective-permute-start(bf16[1,2,512,128]{3,2,1,0:T(8,128)(2,1)} %get-tuple-element.17), channel_id=1, source_target_pairs={{0,4},{1,5},{2,6},{3,7},{4,0},{5,1},{6,2},{7,3},{8,12},{9,13},{10,... | collective-permute-start | bytes 786440 | tf_op jit(solution)/shard_map/ppermute | solution.py:514
  18.0 9.3 %copy-start.9 = (bf16[1,2,512,128]{3,2,1,0:T(8,128)(2,1)S(1)}, bf16[1,2,512,128]{3,2,1,0:T(8,128)(2,1)}, u32[]{:S(2)}) copy-start(bf16[1,2,512,128]{3,2,1,0:T(8,128)(2,1)} %get-tuple-element.18) | copy-start | bytes 786436
  18.0 25.0 %copy-start.6 = (bf16[1,2,512,128]{3,2,1,0:T(8,128)(2,1)S(1)}, bf16[1,2,512,128]{3,2,1,0:T(8,128)(2,1)}, u32[]{:S(2)}) copy-start(bf16[1,2,512,128]{3,2,1,0:T(8,128)(2,1)} %get-tuple-element.15) | copy-start | bytes 786436
  18.0 28.9 %collective-permute-start.1 = (bf16[2,2,512,128]{3,2,1,0:T(8,128)(2,1)}, bf16[2,2,512,128]{3,2,1,0:T(8,128)(2,1)S(1)}, u32[]{:S(2)}, u32[]{:S(2)}) collective-permute-start(bf16[2,2,512,128]{3,2,1,0:T(8,128)(2,1)} %get-tuple-element.16), channel_id=1, source_target_pairs={{0,2},{1,3},{2,0},{3,1},{4,6},{5,7},{6,4},{7,5},{8,10},{9,11},{10,... | collective-permute-start | bytes 1572872 | tf_op jit(solution)/shard_map/ppermute | solution.py:514
  21.8 16.4 %collective-permute-start.5 = (bf16[2,2,128,128]{3,2,1,0:T(8,128)(2,1)}, bf16[2,2,128,128]{3,2,1,0:T(8,128)(2,1)S(1)}, u32[]{:S(2)}, u32[]{:S(2)}) collective-permute-start(bf16[2,2,128,128]{3,2,1,0:T(8,128)(2,1)} %get-tuple-element.19), channel_id=1, source_target_pairs={{8,0},{0,8},{24,18},{16,26}} | collective-permute-start | bytes 393224 | tf_op jit(solution)/shard_map/ppermute | solution.py:542
  26.0 13.5 %collective-permute-start.6 = (bf16[2,2,128,128]{3,2,1,0:T(8,128)(2,1)}, bf16[2,2,128,128]{3,2,1,0:T(8,128)(2,1)S(1)}, u32[]{:S(2)}, u32[]{:S(2)}) collective-permute-start(bf16[2,2,128,128]{3,2,1,0:T(8,128)(2,1)} %get-tuple-element.20), channel_id=1, source_target_pairs={{8,4},{0,12},{24,22},{16,30}} | collective-permute-start | bytes 393224 | tf_op jit(solution)/shard_map/ppermute | solution.py:542
  27.4 15.8 %collective-permute-start.3 = (bf16[1,2,512,128]{3,2,1,0:T(8,128)(2,1)S(1)}, bf16[1,2,512,128]{3,2,1,0:T(8,128)(2,1)S(1)}, u32[]{:S(2)}, u32[]{:S(2)}) collective-permute-start(bf16[1,2,512,128]{3,2,1,0:T(8,128)(2,1)S(1)} %copy-done.9), channel_id=1, source_target_pairs={{0,6},{1,7},{2,4},{3,5},{4,2},{5,3},{6,0},{7,1},{8,14},{9,15},{10,... | collective-permute-start | bytes 786440 | tf_op jit(solution)/shard_map/ppermute | solution.py:514
  36.2 15.7 %copy-start.3 = (bf16[1,2,512,128]{3,2,1,0:T(8,128)(2,1)}, bf16[1,2,512,128]{3,2,1,0:T(8,128)(2,1)S(1)}, u32[]{:S(2)}) copy-start(bf16[1,2,512,128]{3,2,1,0:T(8,128)(2,1)S(1)} %collective-permute-done.2.refs_11_) | copy-start | bytes 786436
  36.2 10.7 %collective-permute-start.8 = (bf16[1,2,512,128]{3,2,1,0:T(8,128)(2,1)S(1)}, bf16[1,2,512,128]{3,2,1,0:T(8,128)(2,1)S(1)}, u32[]{:S(2)}, u32[]{:S(2)}) collective-permute-start(bf16[1,2,512,128]{3,2,1,0:T(8,128)(2,1)S(1)} %collective-permute-done.2.refs_11_), channel_id=1, source_target_pairs={{0,16},{16,0},{1,17},{17,1},{2,18},{18,2},{3,19},{19,3},{4,20},{20... | collective-permute-start | bytes 786440 | tf_op jit(solution)/shard_map/ppermute | solution.py:524
  39.6 7.3 %collective-permute-start.7 = (bf16[2,2,128,128]{3,2,1,0:T(8,128)(2,1)S(1)}, bf16[2,2,128,128]{3,2,1,0:T(8,128)(2,1)S(1)}, u32[]{:S(2)}, u32[]{:S(2)}) collective-permute-start(bf16[2,2,128,128]{3,2,1,0:T(8,128)(2,1)S(1)} %add.6), channel_id=1, source_target_pairs={{0,16},{4,20},{8,24},{12,28},{18,2},{22,6},{26,10},{30,14}} | collective-permute-start | bytes 393224 | tf_op jit(solution)/shard_map/ppermute | solution.py:555
  43.0 7.2 %collective-permute-start = (bf16[1,2,512,128]{3,2,1,0:T(8,128)(2,1)S(1)}, bf16[1,2,512,128]{3,2,1,0:T(8,128)(2,1)S(1)}, u32[]{:S(2)}, u32[]{:S(2)}) collective-permute-start(bf16[1,2,512,128]{3,2,1,0:T(8,128)(2,1)S(1)} %copy-done.6), channel_id=1, source_target_pairs={{0,1},{1,0},{2,3},{3,2},{4,5},{5,4},{6,7},{7,6},{8,9},{9,8},{10,11... | collective-permute-start | bytes 786440 | tf_op jit(solution)/shard_map/ppermute | solution.py:514
  43.1 8.8 %copy-start.4 = (bf16[1,2,512,128]{3,2,1,0:T(8,128)(2,1)}, bf16[1,2,512,128]{3,2,1,0:T(8,128)(2,1)S(1)}, u32[]{:S(2)}) copy-start(bf16[1,2,512,128]{3,2,1,0:T(8,128)(2,1)S(1)} %collective-permute-done.3.refs_12_) | copy-start | bytes 786436
  43.1 8.7 %collective-permute-start.9 = (bf16[1,2,512,128]{3,2,1,0:T(8,128)(2,1)S(1)}, bf16[1,2,512,128]{3,2,1,0:T(8,128)(2,1)S(1)}, u32[]{:S(2)}, u32[]{:S(2)}) collective-permute-start(bf16[1,2,512,128]{3,2,1,0:T(8,128)(2,1)S(1)} %collective-permute-done.3.refs_12_), channel_id=1, source_target_pairs={{0,16},{16,0},{1,17},{17,1},{2,18},{18,2},{3,19},{19,3},{4,20},{20... | collective-permute-start | bytes 786440 | tf_op jit(solution)/shard_map/ppermute | solution.py:524
  46.9 5.0 %copy-start.5 = (bf16[1,2,512,128]{3,2,1,0:T(8,128)(2,1)}, bf16[1,2,512,128]{3,2,1,0:T(8,128)(2,1)S(1)}, u32[]{:S(2)}) copy-start(bf16[1,2,512,128]{3,2,1,0:T(8,128)(2,1)S(1)} %collective-permute-done.8.refs_14_) | copy-start | bytes 786436
  46.9 5.0 %copy-start.2 = (bf16[2,2,512,128]{3,2,1,0:T(8,128)(2,1)}, bf16[2,2,512,128]{3,2,1,0:T(8,128)(2,1)S(1)}, u32[]{:S(2)}) copy-start(bf16[2,2,512,128]{3,2,1,0:T(8,128)(2,1)S(1)} %collective-permute-done.1.refs_10_) | copy-start | bytes 1572868
  47.0 4.9 %collective-permute-start.4 = (bf16[1,2,512,128]{3,2,1,0:T(8,128)(2,1)S(1)}, bf16[1,2,512,128]{3,2,1,0:T(8,128)(2,1)S(1)}, u32[]{:S(2)}, u32[]{:S(2)}) collective-permute-start(bf16[1,2,512,128]{3,2,1,0:T(8,128)(2,1)S(1)} %slice.12), channel_id=1, source_target_pairs={{0,1},{1,0},{2,3},{3,2},{4,5},{5,4},{6,7},{7,6},{8,9},{9,8},{10,11... | collective-permute-start | bytes 786440 | tf_op jit(solution)/shard_map/ppermute | solution.py:525
  47.8 4.1 %collective-permute-start.10 = (bf16[2,128,128]{2,1,0:T(8,128)(2,1)S(1)}, bf16[2,128,128]{2,1,0:T(8,128)(2,1)S(1)}, u32[]{:S(2)}, u32[]{:S(2)}) collective-permute-start(bf16[2,128,128]{2,1,0:T(8,128)(2,1)S(1)} %get-tuple-element.23), channel_id=1, source_target_pairs={{0,1},{2,3},{4,5},{6,7},{8,9},{10,11},{12,13},{14,15},{16,17},{18,... | collective-permute-start | bytes 196616 | tf_op jit(solution)/shard_map/ppermute | solution.py:558
  50.3 1.6 %copy-start.7 = (bf16[1,2,512,128]{3,2,1,0:T(8,128)(2,1)}, bf16[1,2,512,128]{3,2,1,0:T(8,128)(2,1)S(1)}, u32[]{:S(2)}) copy-start(bf16[1,2,512,128]{3,2,1,0:T(8,128)(2,1)S(1)} %collective-permute-done.refs_9_) | copy-start | bytes 786436
  51.8 0.7 copy-start.8
  51.8 0.7 copy-start.11
  51.8 0.8 copy-start.10
  51.9 1.2 %copy-start.1 = (bf16[16,256,128]{2,1,0:T(8,128)(2,1)}, bf16[16,256,128]{2,1,0:T(8,128)(2,1)S(1)}, u32[]{:S(2)}) copy-start(bf16[16,256,128]{2,1,0:T(8,128)(2,1)S(1)} %all-to-all-done.refs_0_) | copy-start | bytes 3145732
  53.0 31.9 %copy-start = (bf16[1024,256]{1,0:T(8,128)(2,1)S(1)}, bf16[1024,256]{1,0:T(8,128)(2,1)}, u32[]{:S(2)}) copy-start(bf16[1024,256]{1,0:T(8,128)(2,1)} %gate.3) | copy-start | bytes 1572868

commit v6 on v5

--- a/solution.py
+++ b/solution.py
@@ -182,8 +182,9 @@
 
 
 def pack_kernel(spec_one, spec_two, *refs):
-    *outs, raw, strided, turned, landed = refs
+    *outs, raw, strided, turned, landed, other_raw, other_turned, other_landed = refs
     peers = lax.axis_size("ctx") // 2
+    lacked, outs = outs[-(peers // 4) :], outs[: -(peers // 4)]
     step = spec_one.shape[2] // LANES
     channels = raw.shape[4]
     _, half, low_index, is_first, is_middle = place()
@@ -200,6 +201,9 @@
     }
     for copy in copies.values():
         copy.start()
+    special_kernel(
+        spec_one, spec_two, *lacked, other_raw, strided, other_turned, other_landed
+    )
     for index in range(2):
         for a in range(2):
             for ri in range(2):
@@ -495,20 +499,26 @@
     both = ("group", "ctx")
     block_shape = (2, count * 4 * step, LANES)
     shapes = [(len(offsets),) + block_shape for offsets in sent_blocks(peers, 0)]
-    blocks = pl.pallas_call(
+    lacked_shape = jax.ShapeDtypeStruct((2, 2, per_device, LANES), BF16)
+    turned = pl.pallas_call(
         pack_kernel,
         in_specs=[ANY, ANY],
-        out_specs=[VMEM] * len(shapes),
-        out_shape=[jax.ShapeDtypeStruct(shape, BF16) for shape in shapes],
+        out_specs=[VMEM] * (len(shapes) + peers // 4),
+        out_shape=[jax.ShapeDtypeStruct(shape, BF16) for shape in shapes]
+        + [lacked_shape] * (peers // 4),
         scratch_shapes=[
             pltpu.VMEM((2, 2, 2, length, half_channels), BF16),
             pltpu.VMEM((2, length + step, half_channels), F32),
             pltpu.VMEM(((half_channels + 1) * 4 * step, LANES), F32),
             pltpu.SemaphoreType.DMA((2, 2, 2)),
+            pltpu.VMEM((2, 2, length, half_channels), BF16),
+            pltpu.VMEM((2, (half_channels + 1) * step, LANES), F32),
+            pltpu.SemaphoreType.DMA((2, 2)),
         ],
         compiler_params=PARAMS,
         name="pack",
     )(spectrum_one, spectrum_two)
+    blocks, lacked = turned[: len(shapes)], turned[len(shapes) :]
     routes = [[offsets[0] for offsets in sent_blocks(peers, g % 2)] for g in range(groups)]
     received = [
         lax.ppermute(
@@ -524,20 +534,6 @@
     passed = [lax.ppermute(block, "group", swap) for block in received[far:]]
     beside = [lax.ppermute(block[1:], "ctx", mates) for block in received[2:far]]
 
-    lacked = pl.pallas_call(
-        special_kernel,
-        in_specs=[ANY] * 2,
-        out_specs=[VMEM] * (peers // 4),
-        out_shape=[jax.ShapeDtypeStruct((2, 2, per_device, LANES), BF16)] * (peers // 4),
-        scratch_shapes=[
-            pltpu.VMEM((2, 2, length, half_channels), BF16),
-            pltpu.VMEM((2, length + step, half_channels), F32),
-            pltpu.VMEM((2, (half_channels + 1) * step, LANES), F32),
-            pltpu.SemaphoreType.DMA((2, 2)),
-        ],
-        compiler_params=PARAMS,
-        name="special",
-    )(spectrum_one, spectrum_two)
     lacked = [
         lax.ppermute(
             rows,

time: 86.6 us -> 86.5 us (level)
  Pallas kernels: 23.8 us -> 22.7 us
  waiting for transfers between devices: 16.3 us -> 17.3 us
    ppermute x4, waiting for transfers between devices: 8.74 us -> 9.91 us  [on_device(): lax.ppermute(block, both, [(g * n + d, g * n + (d ^ routes[g][i])) for g...]
    pallas_call x2 -> x1, Pallas kernels: 8.24 us -> 7.11 us  [on_device(): pl.pallas_call(pack_kernel, in_specs=[ANY, ANY], out_specs=[VMEM] * (len(...]
  transfers between devices with their start and end apart: 12 -> 12, of which waited for: 5 -> 5; matrix products, arithmetic and copies ran while one was open for 1% -> 1% of each run, Pallas kernels for 10% -> 8%
where the time goes in v6:
time: 86.5 us; the launch traced here: 86.1 us
  starting transfers between devices  23.8 us (28%)
  Pallas kernels  22.7 us (26%)
  blocking collectives  20.1 us (23%)
  waiting for transfers between devices  17.3 us (20%)
  local copies, waits for them, and re-layouts  1.85 us (2%)
    all_to_all x1, blocking collectives, on_device(): back = lax.all_to_all(out, 'ctx', split_axis=0, concat_axis=0, tiled=True)  20.1 us
    pallas_call x1, Pallas kernels, run_convolve(): pl.pallas_call(functools.partial(conv_kernel, peers), in_specs=[pl.BlockS...  11.8 us
    ppermute x4, waiting for transfers between devices, on_device(): lax.ppermute(block, both, [(g * n + d, g * n + (d ^ routes[g][i])) for g...  9.91 us
    all_to_all x1, starting transfers between devices, on_device(): data = lax.all_to_all(data, 'ctx', split_axis=0, concat_axis=0, tiled=True)  7.4 us
    pallas_call x1, Pallas kernels, on_device(): pl.pallas_call(pack_kernel, in_specs=[ANY, ANY], out_specs=[VMEM] * (len(...  7.11 us
    ppermute x2, starting transfers between devices, on_device(): lax.ppermute(rows, both, [(g * n + peers - end, g * n + end + 4 * i + 2 *...  5.56 us
    ppermute x4, starting transfers between devices, on_device(): lax.ppermute(block, both, [(g * n + d, g * n + (d ^ routes[g][i])) for g...  3.59 us
    ppermute x1, starting transfers between devices, on_device(): lax.ppermute(lacked, both, [(g * n + d, (g ^ 1) * n + d) for g, d in hold...  3.4 us
  transfers between devices with their start and end apart: 12, of which 5 were waited for; matrix products, arithmetic and copies ran while one was open for 1% of the time, Pallas kernels for 8%

profile of v6, /device:TPU:0, one launch (start us, length us, event | category | flops | bytes accessed | tf_op | source)
XLA Modules:
  0.0 86.1 jit_solution(15893560934967657855)
XLA Ops:
  0.0 2.6 %prep.1 = bf16[16,256,128]{2,1,0:T(8,128)(2,1)} custom-call(bf16[1024,256]{1,0:T(8,128)(2,1)} %signal.1, bf16[1024,256]{1,0:T(8,128)(2,1)} %gate.2, bf16[1024,256]{1,0:T(8,128)(2,1)} %mix.1), custom_call_target="tpu_custom_call" | custom-call | tf_op jit(solution)/shard_map/prep/pallas_call | solution.py:483
  2.6 7.4 %all-to-all-start = ((bf16[16,256,128]{2,1,0:T(8,128)(2,1)}), bf16[16,256,128]{2,1,0:T(8,128)(2,1)S(1)}, u32[]{:S(2)}, u32[]{:S(2)}) async-start(bf16[16,256,128]{2,1,0:T(8,128)(2,1)} %prep.1), calls=%async_computation | async-start | bytes 2097152 | tf_op jit(solution)/shard_map/all_to_all | solution.py:555
  10.0 7.1 %pack.1 = (bf16[1,2,512,128]{3,2,1,0:T(8,128)(2,1)}, bf16[1,2,512,128]{3,2,1,0:T(8,128)(2,1)}, bf16[2,2,512,128]{3,2,1,0:T(8,128)(2,1)}, bf16[1,2,512,128]{3,2,1...) custom-call(bf16[2,2,1024,256]{3,2,1,0:T(8,128)(2,1)} %spec_one.1, ...), custom_call_target="tpu_custom_call" | custom-call | tf_op jit(solution)/shard_map/pack/pallas_call | solution.py:503
  17.2 2.0 %collective-permute-start.2 = (bf16[1,2,512,128]{3,2,1,0:T(8,128)(2,1)}, bf16[1,2,512,128]{3,2,1,0:T(8,128)(2,1)S(1)}, u32[]{:S(2)}, u32[]{:S(2)}) collective-permute-start(bf16[1,2,512,128]{3,2,1,0:T(8,128)(2,1)} %get-tuple-element.17), channel_id=1, source_target_pairs={{0,4},{1,5},{2,6},{3,7},{4,0},{5,1},{6,2},{7,3},{8,12},{9,13},{10,... | collective-permute-start | bytes 786440 | tf_op jit(solution)/shard_map/ppermute | solution.py:524
  19.1 1.5 %collective-permute-start.1 = (bf16[2,2,512,128]{3,2,1,0:T(8,128)(2,1)}, bf16[2,2,512,128]{3,2,1,0:T(8,128)(2,1)S(1)}, u32[]{:S(2)}, u32[]{:S(2)}) collective-permute-start(bf16[2,2,512,128]{3,2,1,0:T(8,128)(2,1)} %get-tuple-element.16), channel_id=1, source_target_pairs={{0,2},{1,3},{2,0},{3,1},{4,6},{5,7},{6,4},{7,5},{8,10},{9,11},{10,... | collective-permute-start | bytes 1572872 | tf_op jit(solution)/shard_map/ppermute | solution.py:524
  20.6 4.3 %collective-permute-start.5 = (bf16[2,2,128,128]{3,2,1,0:T(8,128)(2,1)}, bf16[2,2,128,128]{3,2,1,0:T(8,128)(2,1)S(1)}, u32[]{:S(2)}, u32[]{:S(2)}) collective-permute-start(bf16[2,2,128,128]{3,2,1,0:T(8,128)(2,1)} %get-tuple-element.19), channel_id=1, source_target_pairs={{8,0},{0,8},{24,18},{16,26}} | collective-permute-start | bytes 393224 | tf_op jit(solution)/shard_map/ppermute | solution.py:538
  24.9 1.3 %collective-permute-start.6 = (bf16[2,2,128,128]{3,2,1,0:T(8,128)(2,1)}, bf16[2,2,128,128]{3,2,1,0:T(8,128)(2,1)S(1)}, u32[]{:S(2)}, u32[]{:S(2)}) collective-permute-start(bf16[2,2,128,128]{3,2,1,0:T(8,128)(2,1)} %get-tuple-element.20), channel_id=1, source_target_pairs={{8,4},{0,12},{24,22},{16,30}} | collective-permute-start | bytes 393224 | tf_op jit(solution)/shard_map/ppermute | solution.py:538
  26.3 9.9 %collective-permute-done.2.refs_11_ = bf16[1,2,512,128]{3,2,1,0:T(8,128)(2,1)S(1)} collective-permute-done((bf16[1,2,512,128]{3,2,1,0:T(8,128)(2,1)}, bf16[1,2,512,128]{3,2,1,0:T(8,128)(2,1)S(1)}, u32[]{:S(2)}, u32[]{:S(2)}) %collective-permute-start.2) | collective-permute-done | bytes 262176 | tf_op jit(solution)/shard_map/ppermute | solution.py:524
  36.2 0.5 collective-permute-start.8
  36.7 1.5 %collective-permute-done.5 = bf16[2,2,128,128]{3,2,1,0:T(8,128)(2,1)S(1)} collective-permute-done((bf16[2,2,128,128]{3,2,1,0:T(8,128)(2,1)}, bf16[2,2,128,128]{3,2,1,0:T(8,128)(2,1)S(1)}, u32[]{:S(2)}, u32[]{:S(2)}) %collective-permute-start.5) | collective-permute-done | bytes 131104 | tf_op jit(solution)/shard_map/ppermute | solution.py:538
  38.2 1.4 %collective-permute-done.6 = bf16[2,2,128,128]{3,2,1,0:T(8,128)(2,1)S(1)} collective-permute-done((bf16[2,2,128,128]{3,2,1,0:T(8,128)(2,1)}, bf16[2,2,128,128]{3,2,1,0:T(8,128)(2,1)S(1)}, u32[]{:S(2)}, u32[]{:S(2)}) %collective-permute-start.6) | collective-permute-done | bytes 131104 | tf_op jit(solution)/shard_map/ppermute | solution.py:538
  39.6 3.4 %collective-permute-start.7 = (bf16[2,2,128,128]{3,2,1,0:T(8,128)(2,1)S(1)}, bf16[2,2,128,128]{3,2,1,0:T(8,128)(2,1)S(1)}, u32[]{:S(2)}, u32[]{:S(2)}) collective-permute-start(bf16[2,2,128,128]{3,2,1,0:T(8,128)(2,1)S(1)} %add.6), channel_id=1, source_target_pairs={{0,16},{4,20},{8,24},{12,28},{18,2},{22,6},{26,10},{30,14}} | collective-permute-start | bytes 393224 | tf_op jit(solution)/shard_map/ppermute | solution.py:551
  43.1 0.8 collective-permute-start.9
  43.9 3.0 %collective-permute-done.7 = bf16[2,2,128,128]{3,2,1,0:T(8,128)(2,1)S(1)} collective-permute-done((bf16[2,2,128,128]{3,2,1,0:T(8,128)(2,1)S(1)}, bf16[2,2,128,128]{3,2,1,0:T(8,128)(2,1)S(1)}, u32[]{:S(2)}, u32[]{:S(2)}) %collective-permute-start.7) | collective-permute-done | bytes 131104 | tf_op jit(solution)/shard_map/ppermute | solution.py:551
  47.0 0.1 collective-permute-start.4
  47.1 0.7 slice_bitcast_fusion
  47.8 2.5 %collective-permute-start.10 = (bf16[2,128,128]{2,1,0:T(8,128)(2,1)S(1)}, bf16[2,128,128]{2,1,0:T(8,128)(2,1)S(1)}, u32[]{:S(2)}, u32[]{:S(2)}) collective-permute-start(bf16[2,128,128]{2,1,0:T(8,128)(2,1)S(1)} %get-tuple-element.23), channel_id=1, source_target_pairs={{0,1},{2,3},{4,5},{6,7},{8,9},{10,11},{12,13},{14,15},{16,17},{18,... | collective-permute-start | bytes 196616 | tf_op jit(solution)/shard_map/ppermute | solution.py:554
  50.3 1.5 %collective-permute-done.9.refs_15_ = bf16[1,2,512,128]{3,2,1,0:T(8,128)(2,1)S(1)} collective-permute-done((bf16[1,2,512,128]{3,2,1,0:T(8,128)(2,1)S(1)}, bf16[1,2,512,128]{3,2,1,0:T(8,128)(2,1)S(1)}, u32[]{:S(2)}, u32[]{:S(2)}) %collective-permute-start.9) | collective-permute-done | bytes 262176 | tf_op jit(solution)/shard_map/ppermute | solution.py:534
  51.9 0.6 copy-done.7
  52.6 0.1 copy-done.8
  52.6 0.4 copy-done.1
  53.0 11.8 %convolve.1 = bf16[16,128,128]{2,1,0:T(8,128)(2,1)} custom-call(f32[256]{0:T(256)} %skip_one.1, f32[256]{0:T(256)} %skip_two.1, bf16[16,256,128]{2,1,0:T(8,128)(2,1)} %copy-done.1, bf16[2,256,256]{2,1,0:T(8,128)(2,1)} %constant.14.clone.refs_1_, f32[2,2,128,128]{3,2,1,0:T(8,128)} %constant.16.clone.refs_2_, bf16[768,256]{1,0:T(8,128)(2,1)} %constant.17.clone.refs_3_, ...), custom_call_target="tpu_custom_call" | custom-call | flops 2400000000 | bytes 8388608 | tf_op jit(solution)/shard_map/convolve/pallas_call | solution.py:451
  64.8 20.1 %all_to_all.10.back = bf16[16,128,128]{2,1,0:T(8,128)(2,1)S(1)} all-to-all(bf16[16,128,128]{2,1,0:T(8,128)(2,1)} %convolve.1), channel_id=1, replica_groups=mesh['group'=2,'ctx'=16] {'ctx'}, dimensions={0} | all-to-all | bytes 1048576 | tf_op jit(solution)/shard_map/all_to_all | solution.py:560
  84.9 1.2 %final.1 = bf16[1024,256]{1,0:T(8,128)(2,1)} custom-call(bf16[16,128,128]{2,1,0:T(8,128)(2,1)S(1)} %all_to_all.10.back, bf16[1024,256]{1,0:T(8,128)(2,1)S(1)} %copy-done), custom_call_target="tpu_custom_call" | custom-call | tf_op jit(solution)/shard_map/final/pallas_call | solution.py:561
  (29 shorter events, 0.3 us)
Async XLA Ops:
  2.6 49.2 %all-to-all-start = ((bf16[16,256,128]{2,1,0:T(8,128)(2,1)}), bf16[16,256,128]{2,1,0:T(8,128)(2,1)S(1)}, u32[]{:S(2)}, u32[]{:S(2)}) async-start(bf16[16,256,128]{2,1,0:T(8,128)(2,1)} %prep.1), calls=%async_computation | async-start | bytes 2097152 | tf_op jit(solution)/shard_map/all_to_all | solution.py:555
  17.2 19.0 %collective-permute-start.2 = (bf16[1,2,512,128]{3,2,1,0:T(8,128)(2,1)}, bf16[1,2,512,128]{3,2,1,0:T(8,128)(2,1)S(1)}, u32[]{:S(2)}, u32[]{:S(2)}) collective-permute-start(bf16[1,2,512,128]{3,2,1,0:T(8,128)(2,1)} %get-tuple-element.17), channel_id=1, source_target_pairs={{0,4},{1,5},{2,6},{3,7},{4,0},{5,1},{6,2},{7,3},{8,12},{9,13},{10,... | collective-permute-start | bytes 786440 | tf_op jit(solution)/shard_map/ppermute | solution.py:524
  19.1 27.8 %collective-permute-start.1 = (bf16[2,2,512,128]{3,2,1,0:T(8,128)(2,1)}, bf16[2,2,512,128]{3,2,1,0:T(8,128)(2,1)S(1)}, u32[]{:S(2)}, u32[]{:S(2)}) collective-permute-start(bf16[2,2,512,128]{3,2,1,0:T(8,128)(2,1)} %get-tuple-element.16), channel_id=1, source_target_pairs={{0,2},{1,3},{2,0},{3,1},{4,6},{5,7},{6,4},{7,5},{8,10},{9,11},{10,... | collective-permute-start | bytes 1572872 | tf_op jit(solution)/shard_map/ppermute | solution.py:524
  20.6 17.6 %collective-permute-start.5 = (bf16[2,2,128,128]{3,2,1,0:T(8,128)(2,1)}, bf16[2,2,128,128]{3,2,1,0:T(8,128)(2,1)S(1)}, u32[]{:S(2)}, u32[]{:S(2)}) collective-permute-start(bf16[2,2,128,128]{3,2,1,0:T(8,128)(2,1)} %get-tuple-element.19), channel_id=1, source_target_pairs={{8,0},{0,8},{24,18},{16,26}} | collective-permute-start | bytes 393224 | tf_op jit(solution)/shard_map/ppermute | solution.py:538
  24.9 14.7 %collective-permute-start.6 = (bf16[2,2,128,128]{3,2,1,0:T(8,128)(2,1)}, bf16[2,2,128,128]{3,2,1,0:T(8,128)(2,1)S(1)}, u32[]{:S(2)}, u32[]{:S(2)}) collective-permute-start(bf16[2,2,128,128]{3,2,1,0:T(8,128)(2,1)} %get-tuple-element.20), channel_id=1, source_target_pairs={{8,4},{0,12},{24,22},{16,30}} | collective-permute-start | bytes 393224 | tf_op jit(solution)/shard_map/ppermute | solution.py:538
  26.2 16.9 %collective-permute-start.3 = (bf16[1,2,512,128]{3,2,1,0:T(8,128)(2,1)}, bf16[1,2,512,128]{3,2,1,0:T(8,128)(2,1)S(1)}, u32[]{:S(2)}, u32[]{:S(2)}) collective-permute-start(bf16[1,2,512,128]{3,2,1,0:T(8,128)(2,1)} %get-tuple-element.18), channel_id=1, source_target_pairs={{0,6},{1,7},{2,4},{3,5},{4,2},{5,3},{6,0},{7,1},{8,14},{9,15},{10,... | collective-permute-start | bytes 786440 | tf_op jit(solution)/shard_map/ppermute | solution.py:524
  36.2 15.7 %copy-start.3 = (bf16[1,2,512,128]{3,2,1,0:T(8,128)(2,1)}, bf16[1,2,512,128]{3,2,1,0:T(8,128)(2,1)S(1)}, u32[]{:S(2)}) copy-start(bf16[1,2,512,128]{3,2,1,0:T(8,128)(2,1)S(1)} %collective-permute-done.2.refs_11_) | copy-start | bytes 786436
  36.2 10.7 %collective-permute-start.8 = (bf16[1,2,512,128]{3,2,1,0:T(8,128)(2,1)S(1)}, bf16[1,2,512,128]{3,2,1,0:T(8,128)(2,1)S(1)}, u32[]{:S(2)}, u32[]{:S(2)}) collective-permute-start(bf16[1,2,512,128]{3,2,1,0:T(8,128)(2,1)S(1)} %collective-permute-done.2.refs_11_), channel_id=1, source_target_pairs={{0,16},{16,0},{1,17},{17,1},{2,18},{18,2},{3,19},{19,3},{4,20},{20... | collective-permute-start | bytes 786440 | tf_op jit(solution)/shard_map/ppermute | solution.py:534
  39.6 7.3 %collective-permute-start.7 = (bf16[2,2,128,128]{3,2,1,0:T(8,128)(2,1)S(1)}, bf16[2,2,128,128]{3,2,1,0:T(8,128)(2,1)S(1)}, u32[]{:S(2)}, u32[]{:S(2)}) collective-permute-start(bf16[2,2,128,128]{3,2,1,0:T(8,128)(2,1)S(1)} %add.6), channel_id=1, source_target_pairs={{0,16},{4,20},{8,24},{12,28},{18,2},{22,6},{26,10},{30,14}} | collective-permute-start | bytes 393224 | tf_op jit(solution)/shard_map/ppermute | solution.py:551
  43.0 7.2 %collective-permute-start = (bf16[1,2,512,128]{3,2,1,0:T(8,128)(2,1)}, bf16[1,2,512,128]{3,2,1,0:T(8,128)(2,1)S(1)}, u32[]{:S(2)}, u32[]{:S(2)}) collective-permute-start(bf16[1,2,512,128]{3,2,1,0:T(8,128)(2,1)} %get-tuple-element.15), channel_id=1, source_target_pairs={{0,1},{1,0},{2,3},{3,2},{4,5},{5,4},{6,7},{7,6},{8,9},{9,8},{10,11... | collective-permute-start | bytes 786440 | tf_op jit(solution)/shard_map/ppermute | solution.py:524
  43.1 8.8 %copy-start.4 = (bf16[1,2,512,128]{3,2,1,0:T(8,128)(2,1)}, bf16[1,2,512,128]{3,2,1,0:T(8,128)(2,1)S(1)}, u32[]{:S(2)}) copy-start(bf16[1,2,512,128]{3,2,1,0:T(8,128)(2,1)S(1)} %collective-permute-done.3.refs_12_) | copy-start | bytes 786436
  43.1 8.7 %collective-permute-start.9 = (bf16[1,2,512,128]{3,2,1,0:T(8,128)(2,1)S(1)}, bf16[1,2,512,128]{3,2,1,0:T(8,128)(2,1)S(1)}, u32[]{:S(2)}, u32[]{:S(2)}) collective-permute-start(bf16[1,2,512,128]{3,2,1,0:T(8,128)(2,1)S(1)} %collective-permute-done.3.refs_12_), channel_id=1, source_target_pairs={{0,16},{16,0},{1,17},{17,1},{2,18},{18,2},{3,19},{19,3},{4,20},{20... | collective-permute-start | bytes 786440 | tf_op jit(solution)/shard_map/ppermute | solution.py:534
  46.9 5.0 %copy-start.5 = (bf16[1,2,512,128]{3,2,1,0:T(8,128)(2,1)}, bf16[1,2,512,128]{3,2,1,0:T(8,128)(2,1)S(1)}, u32[]{:S(2)}) copy-start(bf16[1,2,512,128]{3,2,1,0:T(8,128)(2,1)S(1)} %collective-permute-done.8.refs_14_) | copy-start | bytes 786436
  46.9 5.0 %copy-start.2 = (bf16[2,2,512,128]{3,2,1,0:T(8,128)(2,1)}, bf16[2,2,512,128]{3,2,1,0:T(8,128)(2,1)S(1)}, u32[]{:S(2)}) copy-start(bf16[2,2,512,128]{3,2,1,0:T(8,128)(2,1)S(1)} %collective-permute-done.1.refs_10_) | copy-start | bytes 1572868
  47.0 4.9 %collective-permute-start.4 = (bf16[1,2,512,128]{3,2,1,0:T(8,128)(2,1)S(1)}, bf16[1,2,512,128]{3,2,1,0:T(8,128)(2,1)S(1)}, u32[]{:S(2)}, u32[]{:S(2)}) collective-permute-start(bf16[1,2,512,128]{3,2,1,0:T(8,128)(2,1)S(1)} %slice.12), channel_id=1, source_target_pairs={{0,1},{1,0},{2,3},{3,2},{4,5},{5,4},{6,7},{7,6},{8,9},{9,8},{10,11... | collective-permute-start | bytes 786440 | tf_op jit(solution)/shard_map/ppermute | solution.py:535
  47.8 4.1 %collective-permute-start.10 = (bf16[2,128,128]{2,1,0:T(8,128)(2,1)S(1)}, bf16[2,128,128]{2,1,0:T(8,128)(2,1)S(1)}, u32[]{:S(2)}, u32[]{:S(2)}) collective-permute-start(bf16[2,128,128]{2,1,0:T(8,128)(2,1)S(1)} %get-tuple-element.23), channel_id=1, source_target_pairs={{0,1},{2,3},{4,5},{6,7},{8,9},{10,11},{12,13},{14,15},{16,17},{18,... | collective-permute-start | bytes 196616 | tf_op jit(solution)/shard_map/ppermute | solution.py:554
  50.3 1.6 %copy-start.6 = (bf16[1,2,512,128]{3,2,1,0:T(8,128)(2,1)}, bf16[1,2,512,128]{3,2,1,0:T(8,128)(2,1)S(1)}, u32[]{:S(2)}) copy-start(bf16[1,2,512,128]{3,2,1,0:T(8,128)(2,1)S(1)} %collective-permute-done.refs_9_) | copy-start | bytes 786436
  51.8 0.7 copy-start.7
  51.8 0.7 copy-start.9
  51.8 0.8 copy-start.8
  51.9 1.2 %copy-start.1 = (bf16[16,256,128]{2,1,0:T(8,128)(2,1)}, bf16[16,256,128]{2,1,0:T(8,128)(2,1)S(1)}, u32[]{:S(2)}) copy-start(bf16[16,256,128]{2,1,0:T(8,128)(2,1)S(1)} %all-to-all-done.refs_0_) | copy-start | bytes 3145732
  53.0 31.9 %copy-start = (bf16[1024,256]{1,0:T(8,128)(2,1)S(1)}, bf16[1024,256]{1,0:T(8,128)(2,1)}, u32[]{:S(2)}) copy-start(bf16[1024,256]{1,0:T(8,128)(2,1)} %gate.3) | copy-start | bytes 1572868

commit v7 on v6

--- a/solution.py
+++ b/solution.py
@@ -549,7 +549,7 @@
     lacked = sum(lacked[1:], lacked[0])
     holders = [(g, d) for g in range(groups) for d in range(0, n, 2) if d // 2 % 2 == g % 2]
     others = lax.ppermute(lacked, both, [(g * n + d, (g ^ 1) * n + d) for g, d in holders])
-    others, passed[0] = lax.optimization_barrier((others, passed[0]))
+    others, passed[0], received[2] = lax.optimization_barrier((others, passed[0], received[2]))
     lacked = lacked + others
     mine = (lacked[0], lax.ppermute(lacked[1], "ctx", [(d, d + 1) for d in range(0, n, 2)]))
     data = lax.all_to_all(data, "ctx", split_axis=0, concat_axis=0, tiled=True)

time: 86.5 us -> 86.5 us (level)
  no operation moved by 1% of the time
where the time goes in v7:
time: 86.5 us; the launch traced here: 86.1 us
  starting transfers between devices  23.8 us (28%)
  Pallas kernels  22.7 us (26%)
  blocking collectives  20.1 us (23%)
  waiting for transfers between devices  17.3 us (20%)
  local copies, waits for them, and re-layouts  1.86 us (2%)
    all_to_all x1, blocking collectives, on_device(): back = lax.all_to_all(out, 'ctx', split_axis=0, concat_axis=0, tiled=True)  20.1 us
    pallas_call x1, Pallas kernels, run_convolve(): pl.pallas_call(functools.partial(conv_kernel, peers), in_specs=[pl.BlockS...  11.8 us
    ppermute x4, waiting for transfers between devices, on_device(): lax.ppermute(block, both, [(g * n + d, g * n + (d ^ routes[g][i])) for g...  9.91 us
    all_to_all x1, starting transfers between devices, on_device(): data = lax.all_to_all(data, 'ctx', split_axis=0, concat_axis=0, tiled=True)  7.4 us
    pallas_call x1, Pallas kernels, on_device(): pl.pallas_call(pack_kernel, in_specs=[ANY, ANY], out_specs=[VMEM] * (len(...  7.11 us
    ppermute x2, starting transfers between devices, on_device(): lax.ppermute(rows, both, [(g * n + peers - end, g * n + end + 4 * i + 2 *...  5.56 us
    ppermute x4, starting transfers between devices, on_device(): lax.ppermute(block, both, [(g * n + d, g * n + (d ^ routes[g][i])) for g...  3.59 us
    ppermute x1, starting transfers between devices, on_device(): lax.ppermute(lacked, both, [(g * n + d, (g ^ 1) * n + d) for g, d in hold...  3.4 us
  transfers between devices with their start and end apart: 12, of which 5 were waited for; matrix products, arithmetic and copies ran while one was open for 1% of the time, Pallas kernels for 8%

profile of v7, /device:TPU:0, one launch (start us, length us, event | category | flops | bytes accessed | tf_op | source)
XLA Modules:
  0.0 86.1 jit_solution(5894080443337284241)
XLA Ops:
  0.0 2.6 %prep.1 = bf16[16,256,128]{2,1,0:T(8,128)(2,1)} custom-call(bf16[1024,256]{1,0:T(8,128)(2,1)} %signal.1, bf16[1024,256]{1,0:T(8,128)(2,1)} %gate.2, bf16[1024,256]{1,0:T(8,128)(2,1)} %mix.1), custom_call_target="tpu_custom_call" | custom-call | tf_op jit(solution)/shard_map/prep/pallas_call | solution.py:483
  2.6 7.4 %all-to-all-start = ((bf16[16,256,128]{2,1,0:T(8,128)(2,1)}), bf16[16,256,128]{2,1,0:T(8,128)(2,1)S(1)}, u32[]{:S(2)}, u32[]{:S(2)}) async-start(bf16[16,256,128]{2,1,0:T(8,128)(2,1)} %prep.1), calls=%async_computation | async-start | bytes 2097152 | tf_op jit(solution)/shard_map/all_to_all | solution.py:555
  10.0 7.1 %pack.1 = (bf16[1,2,512,128]{3,2,1,0:T(8,128)(2,1)}, bf16[1,2,512,128]{3,2,1,0:T(8,128)(2,1)}, bf16[2,2,512,128]{3,2,1,0:T(8,128)(2,1)}, bf16[1,2,512,128]{3,2,1...) custom-call(bf16[2,2,1024,256]{3,2,1,0:T(8,128)(2,1)} %spec_one.1, ...), custom_call_target="tpu_custom_call" | custom-call | tf_op jit(solution)/shard_map/pack/pallas_call | solution.py:503
  17.2 2.0 %collective-permute-start.4 = (bf16[1,2,512,128]{3,2,1,0:T(8,128)(2,1)}, bf16[1,2,512,128]{3,2,1,0:T(8,128)(2,1)S(1)}, u32[]{:S(2)}, u32[]{:S(2)}) collective-permute-start(bf16[1,2,512,128]{3,2,1,0:T(8,128)(2,1)} %get-tuple-element.19), channel_id=1, source_target_pairs={{0,4},{1,5},{2,6},{3,7},{4,0},{5,1},{6,2},{7,3},{8,12},{9,13},{10,... | collective-permute-start | bytes 786440 | tf_op jit(solution)/shard_map/ppermute | solution.py:524
  19.1 1.5 %collective-permute-start.6 = (bf16[2,2,512,128]{3,2,1,0:T(8,128)(2,1)}, bf16[2,2,512,128]{3,2,1,0:T(8,128)(2,1)S(1)}, u32[]{:S(2)}, u32[]{:S(2)}) collective-permute-start(bf16[2,2,512,128]{3,2,1,0:T(8,128)(2,1)} %get-tuple-element.20), channel_id=1, source_target_pairs={{0,2},{1,3},{2,0},{3,1},{4,6},{5,7},{6,4},{7,5},{8,10},{9,11},{10,... | collective-permute-start | bytes 1572872 | tf_op jit(solution)/shard_map/ppermute | solution.py:524
  20.6 4.3 %collective-permute-start.1 = (bf16[2,2,128,128]{3,2,1,0:T(8,128)(2,1)}, bf16[2,2,128,128]{3,2,1,0:T(8,128)(2,1)S(1)}, u32[]{:S(2)}, u32[]{:S(2)}) collective-permute-start(bf16[2,2,128,128]{3,2,1,0:T(8,128)(2,1)} %get-tuple-element.17), channel_id=1, source_target_pairs={{8,0},{0,8},{24,18},{16,26}} | collective-permute-start | bytes 393224 | tf_op jit(solution)/shard_map/ppermute | solution.py:538
  24.9 1.3 %collective-permute-start.2 = (bf16[2,2,128,128]{3,2,1,0:T(8,128)(2,1)}, bf16[2,2,128,128]{3,2,1,0:T(8,128)(2,1)S(1)}, u32[]{:S(2)}, u32[]{:S(2)}) collective-permute-start(bf16[2,2,128,128]{3,2,1,0:T(8,128)(2,1)} %get-tuple-element.18), channel_id=1, source_target_pairs={{8,4},{0,12},{24,22},{16,30}} | collective-permute-start | bytes 393224 | tf_op jit(solution)/shard_map/ppermute | solution.py:538
  26.3 9.9 %collective-permute-done.4.refs_11_ = bf16[1,2,512,128]{3,2,1,0:T(8,128)(2,1)S(1)} collective-permute-done((bf16[1,2,512,128]{3,2,1,0:T(8,128)(2,1)}, bf16[1,2,512,128]{3,2,1,0:T(8,128)(2,1)S(1)}, u32[]{:S(2)}, u32[]{:S(2)}) %collective-permute-start.4) | collective-permute-done | bytes 262176 | tf_op jit(solution)/shard_map/ppermute | solution.py:524
  36.2 0.5 collective-permute-start.5
  36.7 1.5 %collective-permute-done.1 = bf16[2,2,128,128]{3,2,1,0:T(8,128)(2,1)S(1)} collective-permute-done((bf16[2,2,128,128]{3,2,1,0:T(8,128)(2,1)}, bf16[2,2,128,128]{3,2,1,0:T(8,128)(2,1)S(1)}, u32[]{:S(2)}, u32[]{:S(2)}) %collective-permute-start.1) | collective-permute-done | bytes 131104 | tf_op jit(solution)/shard_map/ppermute | solution.py:538
  38.2 1.4 %collective-permute-done.2 = bf16[2,2,128,128]{3,2,1,0:T(8,128)(2,1)S(1)} collective-permute-done((bf16[2,2,128,128]{3,2,1,0:T(8,128)(2,1)}, bf16[2,2,128,128]{3,2,1,0:T(8,128)(2,1)S(1)}, u32[]{:S(2)}, u32[]{:S(2)}) %collective-permute-start.2) | collective-permute-done | bytes 131104 | tf_op jit(solution)/shard_map/ppermute | solution.py:538
  39.6 3.4 %collective-permute-start.3 = (bf16[2,2,128,128]{3,2,1,0:T(8,128)(2,1)S(1)}, bf16[2,2,128,128]{3,2,1,0:T(8,128)(2,1)S(1)}, u32[]{:S(2)}, u32[]{:S(2)}) collective-permute-start(bf16[2,2,128,128]{3,2,1,0:T(8,128)(2,1)S(1)} %add.6), channel_id=1, source_target_pairs={{0,16},{4,20},{8,24},{12,28},{18,2},{22,6},{26,10},{30,14}} | collective-permute-start | bytes 393224 | tf_op jit(solution)/shard_map/ppermute | solution.py:551
  43.1 0.8 collective-permute-start.9
  43.9 3.0 %collective-permute-done.3 = bf16[2,2,128,128]{3,2,1,0:T(8,128)(2,1)S(1)} collective-permute-done((bf16[2,2,128,128]{3,2,1,0:T(8,128)(2,1)S(1)}, bf16[2,2,128,128]{3,2,1,0:T(8,128)(2,1)S(1)}, u32[]{:S(2)}, u32[]{:S(2)}) %collective-permute-start.3) | collective-permute-done | bytes 131104 | tf_op jit(solution)/shard_map/ppermute | solution.py:551
  47.0 0.1 collective-permute-start.8
  47.0 0.7 slice_bitcast_fusion
  47.8 2.5 %collective-permute-start.10 = (bf16[2,128,128]{2,1,0:T(8,128)(2,1)S(1)}, bf16[2,128,128]{2,1,0:T(8,128)(2,1)S(1)}, u32[]{:S(2)}, u32[]{:S(2)}) collective-permute-start(bf16[2,128,128]{2,1,0:T(8,128)(2,1)S(1)} %get-tuple-element.25), channel_id=1, source_target_pairs={{0,1},{2,3},{4,5},{6,7},{8,9},{10,11},{12,13},{14,15},{16,17},{18,... | collective-permute-start | bytes 196616 | tf_op jit(solution)/shard_map/ppermute | solution.py:554
  50.3 1.5 %collective-permute-done.9.refs_15_ = bf16[1,2,512,128]{3,2,1,0:T(8,128)(2,1)S(1)} collective-permute-done((bf16[1,2,512,128]{3,2,1,0:T(8,128)(2,1)S(1)}, bf16[1,2,512,128]{3,2,1,0:T(8,128)(2,1)S(1)}, u32[]{:S(2)}, u32[]{:S(2)}) %collective-permute-start.9) | collective-permute-done | bytes 262176 | tf_op jit(solution)/shard_map/ppermute | solution.py:534
  51.9 0.6 copy-done.7
  52.6 0.1 copy-done.8
  52.6 0.4 copy-done.1
  53.0 11.8 %convolve.1 = bf16[16,128,128]{2,1,0:T(8,128)(2,1)} custom-call(f32[256]{0:T(256)} %skip_one.1, f32[256]{0:T(256)} %skip_two.1, bf16[16,256,128]{2,1,0:T(8,128)(2,1)} %copy-done.1, bf16[2,256,256]{2,1,0:T(8,128)(2,1)} %constant.14.clone.refs_1_, f32[2,2,128,128]{3,2,1,0:T(8,128)} %constant.16.clone.refs_2_, bf16[768,256]{1,0:T(8,128)(2,1)} %constant.17.clone.refs_3_, ...), custom_call_target="tpu_custom_call" | custom-call | flops 2400000000 | bytes 8388608 | tf_op jit(solution)/shard_map/convolve/pallas_call | solution.py:451
  64.8 20.1 %all_to_all.10.back = bf16[16,128,128]{2,1,0:T(8,128)(2,1)S(1)} all-to-all(bf16[16,128,128]{2,1,0:T(8,128)(2,1)} %convolve.1), channel_id=1, replica_groups=mesh['group'=2,'ctx'=16] {'ctx'}, dimensions={0} | all-to-all | bytes 1048576 | tf_op jit(solution)/shard_map/all_to_all | solution.py:560
  84.9 1.2 %final.1 = bf16[1024,256]{1,0:T(8,128)(2,1)} custom-call(bf16[16,128,128]{2,1,0:T(8,128)(2,1)S(1)} %all_to_all.10.back, bf16[1024,256]{1,0:T(8,128)(2,1)S(1)} %copy-done), custom_call_target="tpu_custom_call" | custom-call | tf_op jit(solution)/shard_map/final/pallas_call | solution.py:561
  (29 shorter events, 0.3 us)
Async XLA Ops:
  2.6 49.2 %all-to-all-start = ((bf16[16,256,128]{2,1,0:T(8,128)(2,1)}), bf16[16,256,128]{2,1,0:T(8,128)(2,1)S(1)}, u32[]{:S(2)}, u32[]{:S(2)}) async-start(bf16[16,256,128]{2,1,0:T(8,128)(2,1)} %prep.1), calls=%async_computation | async-start | bytes 2097152 | tf_op jit(solution)/shard_map/all_to_all | solution.py:555
  17.2 19.0 %collective-permute-start.4 = (bf16[1,2,512,128]{3,2,1,0:T(8,128)(2,1)}, bf16[1,2,512,128]{3,2,1,0:T(8,128)(2,1)S(1)}, u32[]{:S(2)}, u32[]{:S(2)}) collective-permute-start(bf16[1,2,512,128]{3,2,1,0:T(8,128)(2,1)} %get-tuple-element.19), channel_id=1, source_target_pairs={{0,4},{1,5},{2,6},{3,7},{4,0},{5,1},{6,2},{7,3},{8,12},{9,13},{10,... | collective-permute-start | bytes 786440 | tf_op jit(solution)/shard_map/ppermute | solution.py:524
  19.1 27.7 %collective-permute-start.6 = (bf16[2,2,512,128]{3,2,1,0:T(8,128)(2,1)}, bf16[2,2,512,128]{3,2,1,0:T(8,128)(2,1)S(1)}, u32[]{:S(2)}, u32[]{:S(2)}) collective-permute-start(bf16[2,2,512,128]{3,2,1,0:T(8,128)(2,1)} %get-tuple-element.20), channel_id=1, source_target_pairs={{0,2},{1,3},{2,0},{3,1},{4,6},{5,7},{6,4},{7,5},{8,10},{9,11},{10,... | collective-permute-start | bytes 1572872 | tf_op jit(solution)/shard_map/ppermute | solution.py:524
  20.6 17.6 %collective-permute-start.1 = (bf16[2,2,128,128]{3,2,1,0:T(8,128)(2,1)}, bf16[2,2,128,128]{3,2,1,0:T(8,128)(2,1)S(1)}, u32[]{:S(2)}, u32[]{:S(2)}) collective-permute-start(bf16[2,2,128,128]{3,2,1,0:T(8,128)(2,1)} %get-tuple-element.17), channel_id=1, source_target_pairs={{8,0},{0,8},{24,18},{16,26}} | collective-permute-start | bytes 393224 | tf_op jit(solution)/shard_map/ppermute | solution.py:538
  24.9 14.7 %collective-permute-start.2 = (bf16[2,2,128,128]{3,2,1,0:T(8,128)(2,1)}, bf16[2,2,128,128]{3,2,1,0:T(8,128)(2,1)S(1)}, u32[]{:S(2)}, u32[]{:S(2)}) collective-permute-start(bf16[2,2,128,128]{3,2,1,0:T(8,128)(2,1)} %get-tuple-element.18), channel_id=1, source_target_pairs={{8,4},{0,12},{24,22},{16,30}} | collective-permute-start | bytes 393224 | tf_op jit(solution)/shard_map/ppermute | solution.py:538
  26.2 16.9 %collective-permute-start.7 = (bf16[1,2,512,128]{3,2,1,0:T(8,128)(2,1)}, bf16[1,2,512,128]{3,2,1,0:T(8,128)(2,1)S(1)}, u32[]{:S(2)}, u32[]{:S(2)}) collective-permute-start(bf16[1,2,512,128]{3,2,1,0:T(8,128)(2,1)} %get-tuple-element.22), channel_id=1, source_target_pairs={{0,6},{1,7},{2,4},{3,5},{4,2},{5,3},{6,0},{7,1},{8,14},{9,15},{10,... | collective-permute-start | bytes 786440 | tf_op jit(solution)/shard_map/ppermute | solution.py:524
  36.2 15.7 %copy-start.3 = (bf16[1,2,512,128]{3,2,1,0:T(8,128)(2,1)}, bf16[1,2,512,128]{3,2,1,0:T(8,128)(2,1)S(1)}, u32[]{:S(2)}) copy-start(bf16[1,2,512,128]{3,2,1,0:T(8,128)(2,1)S(1)} %collective-permute-done.4.refs_11_) | copy-start | bytes 786436
  36.2 10.7 %collective-permute-start.5 = (bf16[1,2,512,128]{3,2,1,0:T(8,128)(2,1)S(1)}, bf16[1,2,512,128]{3,2,1,0:T(8,128)(2,1)S(1)}, u32[]{:S(2)}, u32[]{:S(2)}) collective-permute-start(bf16[1,2,512,128]{3,2,1,0:T(8,128)(2,1)S(1)} %collective-permute-done.4.refs_11_), channel_id=1, source_target_pairs={{0,16},{16,0},{1,17},{17,1},{2,18},{18,2},{3,19},{19,3},{4,20},{20... | collective-permute-start | bytes 786440 | tf_op jit(solution)/shard_map/ppermute | solution.py:534
  39.6 7.3 %collective-permute-start.3 = (bf16[2,2,128,128]{3,2,1,0:T(8,128)(2,1)S(1)}, bf16[2,2,128,128]{3,2,1,0:T(8,128)(2,1)S(1)}, u32[]{:S(2)}, u32[]{:S(2)}) collective-permute-start(bf16[2,2,128,128]{3,2,1,0:T(8,128)(2,1)S(1)} %add.6), channel_id=1, source_target_pairs={{0,16},{4,20},{8,24},{12,28},{18,2},{22,6},{26,10},{30,14}} | collective-permute-start | bytes 393224 | tf_op jit(solution)/shard_map/ppermute | solution.py:551
  43.0 7.2 %collective-permute-start = (bf16[1,2,512,128]{3,2,1,0:T(8,128)(2,1)}, bf16[1,2,512,128]{3,2,1,0:T(8,128)(2,1)S(1)}, u32[]{:S(2)}, u32[]{:S(2)}) collective-permute-start(bf16[1,2,512,128]{3,2,1,0:T(8,128)(2,1)} %get-tuple-element.16), channel_id=1, source_target_pairs={{0,1},{1,0},{2,3},{3,2},{4,5},{5,4},{6,7},{7,6},{8,9},{9,8},{10,11... | collective-permute-start | bytes 786440 | tf_op jit(solution)/shard_map/ppermute | solution.py:524
  43.1 8.8 %copy-start.4 = (bf16[1,2,512,128]{3,2,1,0:T(8,128)(2,1)}, bf16[1,2,512,128]{3,2,1,0:T(8,128)(2,1)S(1)}, u32[]{:S(2)}) copy-start(bf16[1,2,512,128]{3,2,1,0:T(8,128)(2,1)S(1)} %collective-permute-done.7.refs_12_) | copy-start | bytes 786436
  43.1 8.7 %collective-permute-start.9 = (bf16[1,2,512,128]{3,2,1,0:T(8,128)(2,1)S(1)}, bf16[1,2,512,128]{3,2,1,0:T(8,128)(2,1)S(1)}, u32[]{:S(2)}, u32[]{:S(2)}) collective-permute-start(bf16[1,2,512,128]{3,2,1,0:T(8,128)(2,1)S(1)} %collective-permute-done.7.refs_12_), channel_id=1, source_target_pairs={{0,16},{16,0},{1,17},{17,1},{2,18},{18,2},{3,19},{19,3},{4,20},{20... | collective-permute-start | bytes 786440 | tf_op jit(solution)/shard_map/ppermute | solution.py:534
  46.9 5.0 %copy-start.5 = (bf16[1,2,512,128]{3,2,1,0:T(8,128)(2,1)}, bf16[1,2,512,128]{3,2,1,0:T(8,128)(2,1)S(1)}, u32[]{:S(2)}) copy-start(bf16[1,2,512,128]{3,2,1,0:T(8,128)(2,1)S(1)} %collective-permute-done.5.refs_14_) | copy-start | bytes 786436
  46.9 5.0 %copy-start.2 = (bf16[2,2,512,128]{3,2,1,0:T(8,128)(2,1)}, bf16[2,2,512,128]{3,2,1,0:T(8,128)(2,1)S(1)}, u32[]{:S(2)}) copy-start(bf16[2,2,512,128]{3,2,1,0:T(8,128)(2,1)S(1)} %collective-permute-done.6.refs_10_) | copy-start | bytes 1572868
  47.0 4.9 %collective-permute-start.8 = (bf16[1,2,512,128]{3,2,1,0:T(8,128)(2,1)S(1)}, bf16[1,2,512,128]{3,2,1,0:T(8,128)(2,1)S(1)}, u32[]{:S(2)}, u32[]{:S(2)}) collective-permute-start(bf16[1,2,512,128]{3,2,1,0:T(8,128)(2,1)S(1)} %slice.12), channel_id=1, source_target_pairs={{0,1},{1,0},{2,3},{3,2},{4,5},{5,4},{6,7},{7,6},{8,9},{9,8},{10,11... | collective-permute-start | bytes 786440 | tf_op jit(solution)/shard_map/ppermute | solution.py:535
  47.8 4.1 %collective-permute-start.10 = (bf16[2,128,128]{2,1,0:T(8,128)(2,1)S(1)}, bf16[2,128,128]{2,1,0:T(8,128)(2,1)S(1)}, u32[]{:S(2)}, u32[]{:S(2)}) collective-permute-start(bf16[2,128,128]{2,1,0:T(8,128)(2,1)S(1)} %get-tuple-element.25), channel_id=1, source_target_pairs={{0,1},{2,3},{4,5},{6,7},{8,9},{10,11},{12,13},{14,15},{16,17},{18,... | collective-permute-start | bytes 196616 | tf_op jit(solution)/shard_map/ppermute | solution.py:554
  50.3 1.6 %copy-start.6 = (bf16[1,2,512,128]{3,2,1,0:T(8,128)(2,1)}, bf16[1,2,512,128]{3,2,1,0:T(8,128)(2,1)S(1)}, u32[]{:S(2)}) copy-start(bf16[1,2,512,128]{3,2,1,0:T(8,128)(2,1)S(1)} %collective-permute-done.refs_9_) | copy-start | bytes 786436
  51.8 0.7 copy-start.7
  51.8 0.7 copy-start.9
  51.8 0.8 copy-start.8
  51.9 1.2 %copy-start.1 = (bf16[16,256,128]{2,1,0:T(8,128)(2,1)}, bf16[16,256,128]{2,1,0:T(8,128)(2,1)S(1)}, u32[]{:S(2)}) copy-start(bf16[16,256,128]{2,1,0:T(8,128)(2,1)S(1)} %all-to-all-done.refs_0_) | copy-start | bytes 3145732
  53.0 31.9 %copy-start = (bf16[1024,256]{1,0:T(8,128)(2,1)S(1)}, bf16[1024,256]{1,0:T(8,128)(2,1)}, u32[]{:S(2)}) copy-start(bf16[1024,256]{1,0:T(8,128)(2,1)} %gate.3) | copy-start | bytes 1572868
